TPU v7x, 32 devices: a whole 2x2x4 slice. The times are simulated.
32 devices in a mesh: dp: 8 (over z, y), rep: 4 (over x, core).
Axes of the slice: x: 2, y: 2, z: 4, core: 2. Of those that a mesh axis runs over, the one named last changes fastest.
Arguments:
- features: bfloat16 [32, 64, 64, 512], P(('dp', 'rep')), may hold values from -8 to 8
- cotangent: bfloat16 [32, 64, 64, 512], P(('dp', 'rep')), may hold values from -6 to 6
- holes: int32 [32, 64, 64], P(('dp', 'rep')), may hold values from 0 to 1
- w_ll: bfloat16 [1, 1152, 128], P(None, 'dp'), may hold values from -0.09375 to 0.09375
- w_gl: bfloat16 [1, 3456, 128], P(None, 'dp'), may hold values from -0.09375 to 0.09375
- w_lg: bfloat16 [1, 1152, 384], P(None, 'dp'), may hold values from -0.1875 to 0.1875
- w_in: bfloat16 [1, 384, 192], P(None, 'dp'), may hold values from -0.3125 to 0.3125
- w_fu: bfloat16 [1, 384, 384], P(None, 'dp'), may hold values from -0.3125 to 0.3125
- w_out: bfloat16 [1, 192, 384], P(None, 'dp'), may hold values from -0.4375 to 0.4375
- gains: bfloat16 [1, 1088], P(None, 'dp'), may hold values from 0.5 to 1.5
- biases: bfloat16 [1, 1088], P(None, 'dp'), may hold values from -2 to 2
Outputs:
- block_out: bfloat16 [32, 64, 64, 512], P(('dp', 'rep'))
- input_grad: bfloat16 [32, 64, 64, 512], P(('dp', 'rep'))
- grad_ll: float32 [1, 1152, 128], P(None, 'dp')
- grad_gl: float32 [1, 3456, 128], P(None, 'dp')
- grad_lg: float32 [1, 1152, 384], P(None, 'dp')
- grad_in: float32 [1, 384, 192], P(None, 'dp')
- grad_fu: float32 [1, 384, 384], P(None, 'dp')
- grad_out: float32 [1, 192, 384], P(None, 'dp')
- gain_grad: float32 [1, 1088], P(None, 'dp')
- bias_grad: float32 [1, 1088], P(None, 'dp')
All inputs are finite; a program needn't handle non-finite values.
Results may differ from a plain program's by a relative error of at most 0.013.
Values may be sent and summed in bfloat16 or wider, within the bound.
A program may use at most 192 MiB of HBM per device.

v0:
```python
import math

import jax
import jax.numpy as jnp
from jax import lax
from jax.sharding import PartitionSpec as P

EPS = 1e-05
HIGH = lax.Precision.HIGHEST


def gelu(values):
    return jax.nn.gelu(values, approximate=True)


def gelu_back(values, grad):
    return jax.vjp(gelu, values)[1](grad)[0]


def conv_forward(field, weight):
    kernel = weight.reshape(3, 3, field.shape[-1], weight.shape[-1])
    return lax.conv_general_dilated(
        field,
        kernel,
        (1, 1),
        ((1, 1), (1, 1)),
        dimension_numbers=("NHWC", "HWIO", "NHWC"),
        preferred_element_type=jnp.float32,
    )


def conv_backward(field, weight, grad):
    channels = field.shape[-1]
    outputs = weight.shape[-1]
    kernel = weight.reshape(3, 3, channels, outputs)[::-1, ::-1]
    field_grad = lax.conv_general_dilated(
        grad,
        kernel,
        (1, 1),
        ((1, 1), (1, 1)),
        dimension_numbers=("NHWC", "HWOI", "NHWC"),
        preferred_element_type=jnp.float32,
    )
    taps = lax.conv_general_dilated(
        field,
        grad,
        (1, 1),
        ((1, 1), (1, 1)),
        dimension_numbers=("CHWN", "IHWO", "NHWC"),
        preferred_element_type=jnp.float32,
    )
    weight_grad = jnp.transpose(taps, (1, 2, 0, 3)).reshape(9 * channels, outputs)
    return (field_grad, weight_grad)


def dft_tables(extent):
    freqs = extent // 2 + 1
    rows = jnp.arange(extent, dtype=jnp.int32)
    cols = jnp.arange(freqs, dtype=jnp.int32)
    row_angle = (
        2.0 * math.pi / extent * (rows[:, None] * rows[None, :] % extent).astype(jnp.float32)
    )
    col_angle = (
        2.0 * math.pi / extent * (rows[:, None] * cols[None, :] % extent).astype(jnp.float32)
    )
    doubled = jnp.where((cols == 0) | (2 * cols == extent), 1.0, 2.0).astype(jnp.float32)
    return (jnp.cos(row_angle), jnp.sin(row_angle), jnp.cos(col_angle), jnp.sin(col_angle), doubled)


def over_rows(table, values):
    return jnp.einsum("hk,bhlc->bklc", table, values, precision=HIGH)


def rows_forward(tables, real, imag):
    return (
        over_rows(tables[0], real) + over_rows(tables[1], imag),
        over_rows(tables[0], imag) - over_rows(tables[1], real),
    )


def rows_inverse(tables, real, imag):
    return (
        over_rows(tables[0], real) - over_rows(tables[1], imag),
        over_rows(tables[1], real) + over_rows(tables[0], imag),
    )


def rfft_stack(tables, field):
    extent = field.shape[1]
    real = jnp.einsum("wl,bhwc->bhlc", tables[2], field, precision=HIGH)
    imag = -jnp.einsum("wl,bhwc->bhlc", tables[3], field, precision=HIGH)
    real, imag = rows_forward(tables, real, imag)
    return jnp.concatenate([real, imag], axis=-1) / extent


def irfft_stack(tables, stacked):
    extent = stacked.shape[1]
    half_width = stacked.shape[-1] // 2
    real, imag = rows_inverse(tables, stacked[..., :half_width], stacked[..., half_width:])
    cos_cols = tables[2] * tables[4]
    sin_cols = tables[3] * tables[4]
    field = jnp.einsum("wl,bhlc->bhwc", cos_cols, real, precision=HIGH)
    field = field - jnp.einsum("wl,bhlc->bhwc", sin_cols, imag, precision=HIGH)
    return field / extent


def irfft_adjoint(tables, grad):
    extent = grad.shape[1]
    cos_cols = tables[2] * tables[4]
    sin_cols = tables[3] * tables[4]
    real = jnp.einsum("wl,bhwc->bhlc", cos_cols, grad, precision=HIGH)
    imag = -jnp.einsum("wl,bhwc->bhlc", sin_cols, grad, precision=HIGH)
    real, imag = rows_forward(tables, real, imag)
    return jnp.concatenate([real, imag], axis=-1) / extent


def rfft_adjoint(tables, grad):
    extent = grad.shape[1]
    half_width = grad.shape[-1] // 2
    real, imag = rows_inverse(tables, grad[..., :half_width], grad[..., half_width:])
    field = jnp.einsum("wl,bhlc->bhwc", tables[2], real, precision=HIGH)
    field = field - jnp.einsum("wl,bhlc->bhwc", tables[3], imag, precision=HIGH)
    return field / extent


def split_row(row, widths):
    parts = []
    offset = 0
    for width in widths:
        parts.append(row[offset : offset + width].astype(jnp.float32))
        offset = offset + width
    return parts


def norm_stats(arrays, devices):
    pieces = []
    for values in arrays:
        pieces.append(jnp.sum(values, axis=(0, 1, 2)))
        pieces.append(jnp.sum(values * values, axis=(0, 1, 2)))
    totals = lax.psum(jnp.concatenate(pieces), ("dp", "rep"))
    stats = []
    offset = 0
    for values in arrays:
        width = values.shape[-1]
        count = values.shape[0] * values.shape[1] * values.shape[2] * devices
        mean = totals[offset : offset + width] / count
        square = totals[offset + width : offset + 2 * width] / count
        offset = offset + 2 * width
        stats.append((mean, lax.rsqrt(square - mean * mean + EPS)))
    return stats


def norm_back(items, devices):
    pieces = []
    for grad_y, normed, gain, scale in items:
        pieces.append(jnp.sum(grad_y, axis=(0, 1, 2)))
        pieces.append(jnp.sum(grad_y * normed, axis=(0, 1, 2)))
    totals = lax.psum(jnp.concatenate(pieces), ("dp", "rep"))
    results = []
    offset = 0
    for grad_y, normed, gain, scale in items:
        width = grad_y.shape[-1]
        count = grad_y.shape[0] * grad_y.shape[1] * grad_y.shape[2] * devices
        bias_total = totals[offset : offset + width]
        gain_total = totals[offset + width : offset + 2 * width]
        offset = offset + 2 * width
        grad_pre = scale * (
            gain * grad_y - gain * bias_total / count - normed * gain * gain_total / count
        )
        results.append((grad_pre, gain_total, bias_total))
    return results


def layer_widths(weights):
    return (weights[3].shape[-1], weights[4].shape[-1], weights[0].shape[-1], weights[4].shape[-1])


def spectral_front(pre_spec, stats, gain, bias, w_fu, tables):
    normed = (pre_spec - stats[0]) * stats[1]
    spectral = gelu(gain * normed + bias)
    stacked = rfft_stack(tables, spectral).astype(jnp.bfloat16)
    pre_freq = jnp.einsum("bhwc,cd->bhwd", stacked, w_fu, preferred_element_type=jnp.float32)
    return (normed, spectral, stacked, pre_freq)


def layer_forward(loc_in, glo_in, weights, gain_row, bias_row, tables, devices):
    w_ll, w_gl, w_lg, w_in, w_fu, w_out = weights
    gain_parts = split_row(gain_row, layer_widths(weights))
    bias_parts = split_row(bias_row, layer_widths(weights))
    pre_loc = conv_forward(loc_in, w_ll) + conv_forward(glo_in, w_gl)
    cross = conv_forward(loc_in, w_lg)
    pre_spec = jnp.einsum("bhwc,cd->bhwd", glo_in, w_in, preferred_element_type=jnp.float32)
    spec_stats = norm_stats([pre_spec], devices)[0]
    normed_spec, spectral, stacked, pre_freq = spectral_front(
        pre_spec, spec_stats, gain_parts[0], bias_parts[0], w_fu, tables
    )
    freq_stats = norm_stats([pre_freq], devices)[0]
    mixed = gelu(gain_parts[1] * (pre_freq - freq_stats[0]) * freq_stats[1] + bias_parts[1])
    joined = (spectral + irfft_stack(tables, mixed)).astype(jnp.bfloat16)
    pre_glo = cross + jnp.einsum("bhwc,cd->bhwd", joined, w_out, preferred_element_type=jnp.float32)
    loc_stats, glo_stats = norm_stats([pre_loc, pre_glo], devices)
    out_loc = gelu(gain_parts[2] * (pre_loc - loc_stats[0]) * loc_stats[1] + bias_parts[2])
    out_glo = gelu(gain_parts[3] * (pre_glo - glo_stats[0]) * glo_stats[1] + bias_parts[3])
    saved = (
        loc_in,
        glo_in,
        pre_loc,
        pre_glo,
        pre_spec,
        (spec_stats, freq_stats, loc_stats, glo_stats),
    )
    return (out_loc, out_glo, saved)


def layer_backward(grad_loc, grad_glo, saved, weights, gain_row, bias_row, tables, devices):
    w_ll, w_gl, w_lg, w_in, w_fu, w_out = weights
    loc_in, glo_in, pre_loc, pre_glo, pre_spec, stats = saved
    gain_parts = split_row(gain_row, layer_widths(weights))
    bias_parts = split_row(bias_row, layer_widths(weights))
    normed_loc = (pre_loc - stats[2][0]) * stats[2][1]
    normed_glo = (pre_glo - stats[3][0]) * stats[3][1]
    dy_loc = gelu_back(gain_parts[2] * normed_loc + bias_parts[2], grad_loc)
    dy_glo = gelu_back(gain_parts[3] * normed_glo + bias_parts[3], grad_glo)
    loc_back, glo_back = norm_back(
        [
            (dy_loc, normed_loc, gain_parts[2], stats[2][1]),
            (dy_glo, normed_glo, gain_parts[3], stats[3][1]),
        ],
        devices,
    )
    d_pre_loc = loc_back[0].astype(jnp.bfloat16)
    d_pre_glo = glo_back[0].astype(jnp.bfloat16)
    grad_loc_in, grad_ll = conv_backward(loc_in, w_ll, d_pre_loc)
    grad_glo_in, grad_gl = conv_backward(glo_in, w_gl, d_pre_loc)
    extra_loc, grad_lg = conv_backward(loc_in, w_lg, d_pre_glo)
    grad_loc_in = grad_loc_in + extra_loc
    normed_spec, spectral, stacked, pre_freq = spectral_front(
        pre_spec, stats[0], gain_parts[0], bias_parts[0], w_fu, tables
    )
    normed_freq = (pre_freq - stats[1][0]) * stats[1][1]
    freq_act = gain_parts[1] * normed_freq + bias_parts[1]
    joined = (spectral + irfft_stack(tables, gelu(freq_act))).astype(jnp.bfloat16)
    grad_out = jnp.einsum("bhwc,bhwd->cd", joined, d_pre_glo, preferred_element_type=jnp.float32)
    d_joined = jnp.einsum("bhwd,cd->bhwc", d_pre_glo, w_out, preferred_element_type=jnp.float32)
    dy_freq = gelu_back(freq_act, irfft_adjoint(tables, d_joined))
    freq_back = norm_back([(dy_freq, normed_freq, gain_parts[1], stats[1][1])], devices)[0]
    d_pre_freq = freq_back[0].astype(jnp.bfloat16)
    grad_fu = jnp.einsum("bhwc,bhwd->cd", stacked, d_pre_freq, preferred_element_type=jnp.float32)
    d_stacked = jnp.einsum("bhwd,cd->bhwc", d_pre_freq, w_fu, preferred_element_type=jnp.float32)
    d_spectral = d_joined + rfft_adjoint(tables, d_stacked)
    dy_spec = gelu_back(gain_parts[0] * normed_spec + bias_parts[0], d_spectral)
    spec_back = norm_back([(dy_spec, normed_spec, gain_parts[0], stats[0][1])], devices)[0]
    d_pre_spec = spec_back[0].astype(jnp.bfloat16)
    grad_in = jnp.einsum("bhwc,bhwd->cd", glo_in, d_pre_spec, preferred_element_type=jnp.float32)
    grad_glo_in = grad_glo_in + jnp.einsum(
        "bhwd,cd->bhwc", d_pre_spec, w_in, preferred_element_type=jnp.float32
    )
    gain_grads = jnp.concatenate([spec_back[1], freq_back[1], loc_back[1], glo_back[1]])
    bias_grads = jnp.concatenate([spec_back[2], freq_back[2], loc_back[2], glo_back[2]])
    return (
        grad_loc_in,
        grad_glo_in,
        (grad_ll, grad_gl, grad_lg, grad_in, grad_fu, grad_out),
        gain_grads,
        bias_grads,
    )


def on_device(features, cotangent, holes, w_ll, w_gl, w_lg, w_in, w_fu, w_out, gains, biases):
    devices = lax.axis_size("dp") * lax.axis_size("rep")
    gathered = (
        lax.all_gather(w_ll, "dp", axis=1, tiled=True),
        lax.all_gather(w_gl, "dp", axis=1, tiled=True),
        lax.all_gather(w_lg, "dp", axis=1, tiled=True),
        lax.all_gather(w_in, "dp", axis=1, tiled=True),
        lax.all_gather(w_fu, "dp", axis=1, tiled=True),
        lax.all_gather(w_out, "dp", axis=1, tiled=True),
        lax.all_gather(gains, "dp", axis=1, tiled=True),
        lax.all_gather(biases, "dp", axis=1, tiled=True),
    )
    loc_width = w_ll.shape[-1]
    layers = w_ll.shape[0]
    tables = dft_tables(features.shape[1])
    loc_in = features[..., :loc_width]
    glo_in = features[..., loc_width:]
    out_loc = None
    out_glo = None
    layer = 0
    weights = tuple((stacked_weight[layer] for stacked_weight in gathered[:6]))
    out_loc, out_glo, saved = layer_forward(
        loc_in, glo_in, weights, gathered[6][layer], gathered[7][layer], tables, devices
    )
    saved_all = [saved]
    block_out = (
        features.astype(jnp.float32) + jnp.concatenate([out_loc, out_glo], axis=-1)
    ).astype(jnp.bfloat16)
    back_set = (
        lax.all_gather(w_ll, "dp", axis=1, tiled=True),
        lax.all_gather(w_gl, "dp", axis=1, tiled=True),
        lax.all_gather(w_lg, "dp", axis=1, tiled=True),
        lax.all_gather(w_in, "dp", axis=1, tiled=True),
        lax.all_gather(w_fu, "dp", axis=1, tiled=True),
        lax.all_gather(w_out, "dp", axis=1, tiled=True),
        lax.all_gather(gains, "dp", axis=1, tiled=True),
        lax.all_gather(biases, "dp", axis=1, tiled=True),
    )
    weighting = cotangent.astype(jnp.float32) * (0.25 + holes.astype(jnp.float32))[..., None]
    grad_loc = weighting[..., :loc_width]
    grad_glo = weighting[..., loc_width:]
    weight_grads = [None] * layers
    gain_rows = [None] * layers
    bias_rows = [None] * layers
    for layer in reversed(range(layers)):
        weights = tuple((stacked_weight[layer] for stacked_weight in back_set[:6]))
        grad_loc, grad_glo, weight_grads[layer], gain_rows[layer], bias_rows[layer] = (
            layer_backward(
                grad_loc,
                grad_glo,
                saved_all[layer],
                weights,
                back_set[6][layer],
                back_set[7][layer],
                tables,
                devices,
            )
        )
    input_grad = (weighting + jnp.concatenate([grad_loc, grad_glo], axis=-1)).astype(jnp.bfloat16)
    grad_ll = jnp.stack([weight_grads[0][0]])
    grad_gl = jnp.stack([weight_grads[0][1]])
    grad_lg = jnp.stack([weight_grads[0][2]])
    grad_in = jnp.stack([weight_grads[0][3]])
    grad_fu = jnp.stack([weight_grads[0][4]])
    grad_out = jnp.stack([weight_grads[0][5]])
    grad_ll, grad_gl, grad_lg, grad_in, grad_fu, grad_out = (
        lax.psum(grad_ll.astype(jnp.bfloat16), "rep").astype(jnp.float32),
        lax.psum(grad_gl.astype(jnp.bfloat16), "rep").astype(jnp.float32),
        lax.psum(grad_lg.astype(jnp.bfloat16), "rep").astype(jnp.float32),
        lax.psum(grad_in.astype(jnp.bfloat16), "rep").astype(jnp.float32),
        lax.psum(grad_fu.astype(jnp.bfloat16), "rep").astype(jnp.float32),
        lax.psum(grad_out.astype(jnp.bfloat16), "rep").astype(jnp.float32),
    )
    grad_ll, grad_gl, grad_lg, grad_in, grad_fu, grad_out = (
        lax.psum_scatter(grad_ll, "dp", scatter_dimension=1, tiled=True),
        lax.psum_scatter(grad_gl, "dp", scatter_dimension=1, tiled=True),
        lax.psum_scatter(grad_lg, "dp", scatter_dimension=1, tiled=True),
        lax.psum_scatter(grad_in, "dp", scatter_dimension=1, tiled=True),
        lax.psum_scatter(grad_fu, "dp", scatter_dimension=1, tiled=True),
        lax.psum_scatter(grad_out, "dp", scatter_dimension=1, tiled=True),
    )
    share = gains.shape[1]
    first_row = lax.axis_index("dp") * share
    gain_grad = lax.dynamic_slice_in_dim(jnp.stack(gain_rows), first_row, share, 1)
    bias_grad = lax.dynamic_slice_in_dim(jnp.stack(bias_rows), first_row, share, 1)
    return (
        block_out,
        input_grad,
        grad_ll,
        grad_gl,
        grad_lg,
        grad_in,
        grad_fu,
        grad_out,
        gain_grad,
        bias_grad,
    )


def solution(mesh):
    in_specs = (
        P(("dp", "rep"), None, None, None),
        P(("dp", "rep"), None, None, None),
        P(("dp", "rep"), None, None),
        P(None, "dp", None),
        P(None, "dp", None),
        P(None, "dp", None),
        P(None, "dp", None),
        P(None, "dp", None),
        P(None, "dp", None),
        P(None, "dp"),
        P(None, "dp"),
    )
    out_specs = (
        P(("dp", "rep"), None, None, None),
        P(("dp", "rep"), None, None, None),
        P(None, "dp", None),
        P(None, "dp", None),
        P(None, "dp", None),
        P(None, "dp", None),
        P(None, "dp", None),
        P(None, "dp", None),
        P(None, "dp"),
        P(None, "dp"),
    )
    return jax.shard_map(
        on_device, mesh=mesh, in_specs=in_specs, out_specs=out_specs, check_vma=False
    )
```

profile of v0, /device:TPU:0, one launch (start us, length us, event | category | flops | bytes accessed | tf_op | source)
XLA Modules:
  0.0 1294.6 jit_solution(18410309780964489915)
XLA Ops:
  11.6 23.4 %all-reduce.4 = (bf16[1088]{0:T(1024)(128)(2,1)S(1)}, bf16[1088]{0:T(1024)(128)(2,1)S(1)}) all-reduce(bf16[1088]{0:T(1024)(128)(2,1)S(1)} %dynamic-update-slice.1, bf16[1088]{0:T(1024)(128)(2,1)S(1)} %dynamic-update-slice), channel_id=1, replica_groups=mesh['dp'=8,'rep'=4] {'dp'}, use_global_device_ids=true, to_apply=%add.1 | all-reduce | flops 2176 | bytes 8704
  36.4 30.8 %all_gather.36 = bf16[1,384,192]{2,1,0:T(8,128)(2,1)S(1)} all-gather(bf16[1,48,192]{2,1,0:T(8,128)(2,1)} %param.17), channel_id=1, replica_groups=mesh['dp'=8,'rep'=4] {'dp'}, dimensions={1}, use_global_device_ids=true | all-gather | bytes 165888 | tf_op jit(solution)/shard_map/all_gather | solution.py:275
  75.7 36.8 %psum.84 = f32[384]{0:T(512)S(1)} all-reduce(f32[384]{0:T(512)S(1)} %pad_maximum_fusion.4), channel_id=1, replica_groups=mesh['dp'=8,'rep'=4] {'dp','rep'}, use_global_device_ids=true, to_apply=%region_4.5 | all-reduce | flops 384 | bytes 3072 | tf_op jit(solution)/shard_map/psum | solution.py:140
  129.9 31.3 %all_gather.38 = bf16[1,384,384]{2,1,0:T(8,128)(2,1)S(1)} all-gather(bf16[1,48,384]{2,1,0:T(8,128)(2,1)S(1)} %copy-done.64), channel_id=1, replica_groups=mesh['dp'=8,'rep'=4] {'dp'}, dimensions={1}, use_global_device_ids=true | all-gather | bytes 331776 | tf_op jit(solution)/shard_map/all_gather | solution.py:276
  168.2 39.7 %psum.85 = f32[768]{0:T(1024)} all-reduce(f32[768]{0:T(1024)S(1)} %pad_maximum_fusion), channel_id=1, replica_groups=mesh['dp'=8,'rep'=4] {'dp','rep'}, use_global_device_ids=true, to_apply=%region_7.8 | all-reduce | flops 768 | bytes 6144 | tf_op jit(solution)/shard_map/psum | solution.py:140
  217.5 30.5 %all_gather.39 = bf16[1,192,384]{2,1,0:T(8,128)(2,1)S(1)} all-gather(bf16[1,24,384]{2,1,0:T(8,128)(2,1)S(1)} %copy-done.72), channel_id=1, replica_groups=mesh['dp'=8,'rep'=4] {'dp'}, dimensions={1}, use_global_device_ids=true | all-gather | bytes 165888 | tf_op jit(solution)/shard_map/all_gather | solution.py:277
  248.0 30.9 %all_gather.33 = bf16[1,1152,128]{2,1,0:T(8,128)(2,1)S(1)} all-gather(bf16[1,144,128]{2,1,0:T(8,128)(2,1)S(1)} %copy-done.65), channel_id=1, replica_groups=mesh['dp'=8,'rep'=4] {'dp'}, dimensions={1}, use_global_device_ids=true | all-gather | bytes 331776 | tf_op jit(solution)/shard_map/all_gather | solution.py:272
  279.0 31.8 %all_gather.34 = bf16[1,3456,128]{2,1,0:T(8,128)(2,1)S(1)} all-gather(bf16[1,432,128]{2,1,0:T(8,128)(2,1)S(1)} %copy-done.62), channel_id=1, replica_groups=mesh['dp'=8,'rep'=4] {'dp'}, dimensions={1}, use_global_device_ids=true | all-gather | bytes 995328 | tf_op jit(solution)/shard_map/all_gather | solution.py:273
  310.8 32.4 %all_gather.35 = bf16[1,1152,384]{2,1,0:T(8,128)(2,1)S(1)} all-gather(bf16[1,144,384]{2,1,0:T(8,128)(2,1)S(1)} %copy-done.63), channel_id=1, replica_groups=mesh['dp'=8,'rep'=4] {'dp'}, dimensions={1}, use_global_device_ids=true | all-gather | bytes 995328 | tf_op jit(solution)/shard_map/all_gather | solution.py:274
  398.3 38.6 %psum.86 = f32[1024]{0:T(1024)} all-reduce(f32[1024]{0:T(1024)} %pad_maximum_fusion.1), channel_id=1, replica_groups=mesh['dp'=8,'rep'=4] {'dp','rep'}, use_global_device_ids=true, to_apply=%region_10.11 | all-reduce | flops 1024 | bytes 8192 | tf_op jit(solution)/shard_map/psum | solution.py:140
  473.6 42.7 %psum.87 = f32[1024]{0:T(1024)} all-reduce(f32[1024]{0:T(1024)} %pad_maximum_fusion.2), channel_id=1, replica_groups=mesh['dp'=8,'rep'=4] {'dp','rep'}, use_global_device_ids=true, to_apply=%region_15.16 | all-reduce | flops 1024 | bytes 8192 | tf_op jit(solution)/shard_map/psum | solution.py:158
  550.2 39.1 %psum.88 = f32[768]{0:T(1024)S(1)} all-reduce(f32[768]{0:T(1024)} %pad_maximum_fusion.3), channel_id=1, replica_groups=mesh['dp'=8,'rep'=4] {'dp','rep'}, use_global_device_ids=true, to_apply=%region_18.19 | all-reduce | flops 768 | bytes 6144 | tf_op jit(solution)/shard_map/psum | solution.py:158
  614.9 48.3 %fusion.173 = bf16[3,3,128,384]{3,2,1,0:T(8,128)(2,1)} fusion(bf16[1,64,64,384]{3,2,1,0:T(8,128)(2,1)S(1)} %copy-done.7, bf16[1,64,64,128]{3,2,1,0:T(8,128)(2,1)S(1)} %copy-done.43), kind=kOutput, calls=%fused_computation.237 | convolution fusion | flops 3549216768 | bytes 5079040 | tf_op jit(solution)/shard_map/transpose | solution.py:52
  664.5 13.3 %fusion.179 = bf16[3,3,128,128]{3,2,1,0:T(8,128)(2,1)} fusion(bf16[1,64,64,128]{3,2,1,0:T(8,128)(2,1)S(1)} %fusion.109, bf16[1,64,64,128]{3,2,1,0:T(8,128)(2,1)S(1)} %copy-done.43), kind=kOutput, calls=%fused_computation.240 | convolution fusion | flops 1183072256 | bytes 2392064 | tf_op jit(solution)/shard_map/transpose | solution.py:52
  677.8 51.1 %fusion.168 = bf16[3,3,384,128]{3,2,1,0:T(8,128)(2,1)} fusion(bf16[1,64,64,128]{3,2,1,0:T(8,128)(2,1)S(1)} %fusion.109, bf16[1,64,64,384]{3,2,1,0:T(8,128)(2,1)S(1)} %copy-done.39), kind=kOutput, calls=%fused_computation.236 | convolution fusion | flops 3549216768 | bytes 5079040 | tf_op jit(solution)/shard_map/transpose | solution.py:52
  739.1 11.7 fusion.466
  750.9 42.3 %psum.89 = f32[384]{0:T(512)S(1)} all-reduce(f32[384]{0:T(512)S(1)} %pad_maximum_fusion.5), channel_id=1, replica_groups=mesh['dp'=8,'rep'=4] {'dp','rep'}, use_global_device_ids=true, to_apply=%region_21.22 | all-reduce | flops 384 | bytes 3072 | tf_op jit(solution)/shard_map/psum | solution.py:158
  821.0 60.9 %all-reduce.11.cloned.1.call-done = (bf16[1,384,192]{1,2,0:T(8,128)(2,1)}, bf16[1,1152,128]{2,1,0:T(8,128)(2,1)}, bf16[1,3456,128]{2,1,0:T(8,128)(2,1)}, bf16[1,...) async-done(((bf16[1,384,192]{1,2,0:T(8,128)(2,1)}, bf16[1,1152,128]{2,1,0:T(8,128)(2,1)}, bf16[1,3456,128]{2,1,0:T(8,128)(2,1)}, ...) | async-done | bytes 2654224 | tf_op jit(solution)/shard_map/psum | solution.py:338
  905.8 10.9 fusion.29
  958.2 60.6 %reduce-scatter.17.cloned.1.call-done = f32[1,24,384]{2,1,0:T(8,128)} async-done(((f32[1,192,384]{2,1,0:T(8,128)}), f32[1,24,384]{2,1,0:T(8,128)}) %reduce-scatter.17.cloned.1.call-update) | async-done | bytes 36880
  1018.8 65.2 %reduce-scatter.9.cloned.1.call-done = f32[1,144,128]{2,1,0:T(8,128)} async-done(((f32[1,1152,128]{2,1,0:T(8,128)}), f32[1,144,128]{2,1,0:T(8,128)}) %reduce-scatter.9.cloned.1.call-update) | async-done | bytes 73744 | tf_op jit(solution)/shard_map/reduce_scatter | solution.py:343
  1084.0 64.9 %reduce-scatter.15.cloned.1.call-done = f32[1,48,384]{2,1,0:T(8,128)} async-done(((f32[1,384,384]{2,1,0:T(8,128)}), f32[1,48,384]{2,1,0:T(8,128)}) %reduce-scatter.15.cloned.1.call-update) | async-done | bytes 73744 | tf_op jit(solution)/shard_map/reduce_scatter | solution.py:347
  1148.9 69.4 %reduce-scatter.11.cloned.1.call-done = f32[1,432,128]{2,1,0:T(8,128)} async-done(((f32[1,3456,128]{2,1,0:T(8,128)}), f32[1,432,128]{2,1,0:T(8,128)}) %reduce-scatter.11.cloned.1.call-update) | async-done | bytes 221200 | tf_op jit(solution)/shard_map/reduce_scatter | solution.py:344
  1218.3 69.2 %reduce-scatter.13.cloned.1.call-done = f32[1,144,384]{2,1,0:T(8,128)} async-done(((f32[1,1152,384]{2,1,0:T(8,128)}), f32[1,144,384]{2,1,0:T(8,128)}) %reduce-scatter.13.cloned.1.call-update) | async-done | bytes 221200 | tf_op jit(solution)/shard_map/reduce_scatter | solution.py:345
  (366 shorter events, 301.5 us)
Async XLA Ops:
  7.2 874.7 %all-reduce.11.cloned.1.call-start = ((), (), s32[]{:S(2)}) async-start(), calls=%async_computation.11 | async-start | bytes 5308416 | tf_op jit(solution)/shard_map/psum | solution.py:338
  35.0 90.0 %copy-start.99 = (f32[1,192]{1,0:T(1,128)}, f32[1,192]{1,0:T(1,128)S(1)}, u32[]{:S(2)}) copy-start(f32[1,192]{1,0:T(1,128)S(1)} %slice_convert_fusion.4) | copy-start | bytes 2308
  35.1 40.5 %copy-start.67 = (bf16[1,1088]{1,0:T(2,128)(2,1)}, bf16[1,1088]{1,0:T(2,128)(2,1)S(1)}, u32[]{:S(2)}) copy-start(bf16[1,1088]{1,0:T(2,128)(2,1)S(1)} %reshape.560) | copy-start | bytes 6532
  35.1 89.9 %copy-start.79 = (f32[1,192]{1,0:T(1,128)}, f32[1,192]{1,0:T(1,128)S(1)}, u32[]{:S(2)}) copy-start(f32[1,192]{1,0:T(1,128)S(1)} %slice_convert_fusion.5) | copy-start | bytes 2308
  215.1 32.9 %copy-start.65 = (bf16[1,144,128]{2,1,0:T(8,128)(2,1)S(1)}, bf16[1,144,128]{2,1,0:T(8,128)(2,1)}, u32[]{:S(2)}) copy-start(bf16[1,144,128]{2,1,0:T(8,128)(2,1)} %param.14) | copy-start | bytes 110596
  215.1 63.9 %copy-start.62 = (bf16[1,432,128]{2,1,0:T(8,128)(2,1)S(1)}, bf16[1,432,128]{2,1,0:T(8,128)(2,1)}, u32[]{:S(2)}) copy-start(bf16[1,432,128]{2,1,0:T(8,128)(2,1)} %param.15) | copy-start | bytes 331780
  215.1 95.7 %copy-start.63 = (bf16[1,144,384]{2,1,0:T(8,128)(2,1)S(1)}, bf16[1,144,384]{2,1,0:T(8,128)(2,1)}, u32[]{:S(2)}) copy-start(bf16[1,144,384]{2,1,0:T(8,128)(2,1)} %param.16) | copy-start | bytes 331780
  215.1 128.0 %copy-start.31 = (bf16[64,1,64,128]{3,2,0,1:T(8,128)(2,1)S(1)}, bf16[64,1,64,128]{3,2,0,1:T(8,128)(2,1)}, u32[]{:S(2)}) copy-start(bf16[64,1,64,128]{3,2,0,1:T(8,128)(2,1)} %get-tuple-element.78) | copy-start | bytes 3145732
  248.0 142.5 %copy-start.51 = (bf16[1,192,384]{2,1,0:T(8,128)(2,1)}, bf16[1,192,384]{2,1,0:T(8,128)(2,1)S(1)}, u32[]{:S(2)}) copy-start(bf16[1,192,384]{2,1,0:T(8,128)(2,1)S(1)} %all_gather.39) | copy-start | bytes 442372
  279.0 106.7 %copy-start.56 = (bf16[1,1152,128]{2,1,0:T(8,128)(2,1)}, bf16[1,1152,128]{2,1,0:T(8,128)(2,1)S(1)}, u32[]{:S(2)}) copy-start(bf16[1,1152,128]{2,1,0:T(8,128)(2,1)S(1)} %all_gather.33) | copy-start | bytes 884740
  310.8 65.2 %copy-start.44 = (bf16[1,3456,128]{2,1,0:T(8,128)(2,1)}, bf16[1,3456,128]{2,1,0:T(8,128)(2,1)S(1)}, u32[]{:S(2)}) copy-start(bf16[1,3456,128]{2,1,0:T(8,128)(2,1)S(1)} %all_gather.34) | copy-start | bytes 2654212
  614.9 48.3 %copy-start.26 = (f32[64,1,64,128]{3,0,2,1:T(8,128)S(1)}, f32[64,1,64,128]{3,0,2,1:T(8,128)}, u32[]{:S(2)}) copy-start(f32[64,1,64,128]{3,0,2,1:T(8,128)} %slice.189) | copy-start | bytes 6291460
  614.9 48.3 %copy-start.27 = (f32[1,64,64,128]{3,2,1,0:T(8,128)S(1)}, f32[1,64,64,128]{3,2,1,0:T(8,128)}, u32[]{:S(2)}) copy-start(f32[1,64,64,128]{3,2,1,0:T(8,128)} %get-tuple-element.69) | copy-start | bytes 6291460
  614.9 48.3 %copy-start.86 = (f32[128]{0:T(128)S(1)}, f32[128]{0:T(128)}, u32[]{:S(2)}) copy-start(f32[128]{0:T(128)} %get-tuple-element.113) | copy-start | bytes 1540
  614.9 48.3 %copy-start.91 = (f32[128]{0:T(128)S(1)}, f32[128]{0:T(128)}, u32[]{:S(2)}) copy-start(f32[128]{0:T(128)} %copy-done.90) | copy-start | bytes 1540
  614.9 48.3 %copy-start.97 = (f32[128]{0:T(128)S(1)}, f32[128]{0:T(128)}, u32[]{:S(2)}) copy-start(f32[128]{0:T(128)} %get-tuple-element.87) | copy-start | bytes 1540
  677.8 51.1 %copy-start.3 = (f32[1,64,33,384]{3,1,2,0:T(8,128)S(1)}, f32[1,64,33,384]{3,1,2,0:T(8,128)}, u32[]{:S(2)}) copy-start(f32[1,64,33,384]{3,1,2,0:T(8,128)} %copy-done.2) | copy-start | bytes 9732100
  677.8 51.1 %copy-start.23 = (f32[33,192,64]{1,2,0:T(8,128)S(1)}, f32[33,192,64]{1,2,0:T(8,128)}, u32[]{:S(2)}) copy-start(f32[33,192,64]{1,2,0:T(8,128)} %fusion.127) | copy-start | bytes 4866052
  821.0 135.8 %all-reduce.9.cloned.1.call-start = ((), (), s32[]{:S(2)}) async-start(), calls=%async_computation.9 | async-start | bytes 786432
  883.8 135.0 %reduce-scatter.17.cloned.1.call-start = ((), (), s32[]{:S(2)}) async-start(), calls=%async_computation.10 | async-start | bytes 331776
  885.5 198.5 %reduce-scatter.9.cloned.1.call-start = ((), (), s32[]{:S(2)}) async-start(), calls=%async_computation.5 | async-start | bytes 663552 | tf_op jit(solution)/shard_map/reduce_scatter | solution.py:343
  887.4 261.5 %reduce-scatter.15.cloned.1.call-start = ((), (), s32[]{:S(2)}) async-start(), calls=%async_computation.8 | async-start | bytes 663552 | tf_op jit(solution)/shard_map/reduce_scatter | solution.py:347
  888.4 330.0 %reduce-scatter.11.cloned.1.call-start = ((), (), s32[]{:S(2)}) async-start(), calls=%async_computation.6 | async-start | bytes 1990656 | tf_op jit(solution)/shard_map/reduce_scatter | solution.py:344
  891.0 396.6 %reduce-scatter.13.cloned.1.call-start = ((), (), s32[]{:S(2)}) async-start(), calls=%async_computation.7 | async-start | bytes 1990656 | tf_op jit(solution)/shard_map/reduce_scatter | solution.py:345
  (89 other events, 518.7 us)
Sparse Core Ops, SparseCore 0:
  821.1 60.7 all-reduce.10
  885.2 71.4 all-reduce.8
  961.0 57.7 reduce-scatter.16
  1022.9 61.0 reduce-scatter.8
  1087.7 61.1 reduce-scatter.14
  1153.2 65.0 reduce-scatter.10
  1222.4 65.1 reduce-scatter.12
where the time goes:
time: 1300 us; the launch traced here: 1290 us
  blocking collectives  450 us (35%)
  waiting for transfers between devices  396 us (30%)
  matrix products  294 us (23%)
  other arithmetic  76.3 us (6%)
  local copies, waits for them, and re-layouts  59.9 us (5%)
  between operations  17.1 us (1%)
    psum x3, blocking collectives, norm_back(): totals = lax.psum(jnp.concatenate(pieces), ('dp', 'rep'))  124 us
    psum x3, blocking collectives, norm_stats(): totals = lax.psum(jnp.concatenate(pieces), ('dp', 'rep'))  115 us
    transpose x3, matrix products, conv_backward(): jnp.transpose(taps, (1, 2, 0, 3)).reshape(9 * channels, outputs)  113 us
    reduce_scatter x1, waiting for transfers between devices, on_device(): lax.psum_scatter(grad_gl, 'dp', scatter_dimension=1, tiled=True)  69.4 us
    reduce_scatter x1, waiting for transfers between devices, on_device(): lax.psum_scatter(grad_lg, 'dp', scatter_dimension=1, tiled=True)  69.2 us
    unnamed x9, waiting for transfers between devices  66.4 us
    reduce_scatter x1, waiting for transfers between devices, on_device(): lax.psum_scatter(grad_ll, 'dp', scatter_dimension=1, tiled=True)  65.2 us
    reduce_scatter x1, waiting for transfers between devices, on_device(): lax.psum_scatter(grad_fu, 'dp', scatter_dimension=1, tiled=True)  64.9 us
  transfers between devices with their start and end apart: 7, of which 7 were waited for; matrix products, arithmetic and copies ran while one was open for 5% of the time, Pallas kernels for 0%

commit v1 on v0

v1 whole, which is shorter than its diff:
```python
import functools
import math

import jax
import jax.numpy as jnp
import ml_dtypes
import numpy as np
from jax import lax
from jax.experimental import pallas as pl
from jax.experimental.pallas import tpu as pltpu
from jax.sharding import PartitionSpec as P

EPS = 1e-05
K0 = math.sqrt(2.0 / math.pi)
K1 = 0.044715
MESH = pl.DeviceIdType.MESH
F32 = jnp.float32
BF = jnp.bfloat16
SIDE = 64
LOC = 128
GLO = 384
HALF = 192
ALL = LOC + GLO
WIDTHS = (HALF, GLO, LOC, GLO)
POS = SIDE * SIDE
FREQ = SIDE * (SIDE // 2 + 1)


def dft_table():
    a = np.arange(16)[:, None, None, None, None]
    j = np.arange(4)[None, :, None, None, None]
    w = np.arange(64)[None, None, :, None, None]
    k1 = np.arange(4)[None, None, None, :, None]
    l = np.arange(32)[None, None, None, None, :]
    angle = 2 * np.pi / 64 * (((a + 16 * j) * k1 + w * l) % 64)
    main_re = np.cos(angle).reshape(16, 256, 128) / 64
    main_im = -np.sin(angle).reshape(16, 256, 128) / 64
    k = np.arange(64)[None, None, None, :]
    a, j, w = a[..., 0], j[..., 0], w[..., 0]
    angle = 2 * np.pi / 64 * (((a + 16 * j) * k + 32 * w) % 64)
    ext_re = np.cos(angle).reshape(16, 256, 64) / 64
    ext_im = -np.sin(angle).reshape(16, 256, 64) / 64
    return np.concatenate([main_re, main_im, ext_re, ext_im], axis=-1).astype(ml_dtypes.bfloat16)


def dot(a, b, ca=1, cb=0):
    return lax.dot_general(a, b, (((ca,), (cb,)), ((), ())), preferred_element_type=F32)


def gelu_value(y):
    half = 0.5 * y
    return half + half * jnp.tanh(y * (K0 + K0 * K1 * (y * y)))


def gelu_both(y):
    y2 = y * y
    t = jnp.tanh(y * (K0 + K0 * K1 * y2))
    half = 0.5 * y
    slope = 0.5 + 0.5 * t + half * (1.0 - t * t) * (K0 + 3.0 * K0 * K1 * y2)
    return half + half * t, slope


def gelu_slope(y):
    return gelu_both(y)[1]


def cmul(z, c, s):
    return (z[0] * c - z[1] * s, z[0] * s + z[1] * c)


def dft4(z, sign):
    (ar, ai), (br, bi), (cr, ci), (dr, di) = z
    pr, pi, qr, qi = ar + cr, ai + ci, ar - cr, ai - ci
    rr, ri, sr, si = br + dr, bi + di, br - dr, bi - di
    tr, ti = (si, -sr) if sign < 0 else (-si, sr)
    return [(pr + rr, pi + ri), (qr + tr, qi + ti), (pr - rr, pi - ri), (qr - tr, qi - ti)]


def dft16(z, sign):
    cols = []
    for n2 in range(4):
        part = dft4([z[4 * n1 + n2] for n1 in range(4)], sign)
        for k1 in range(1, 4):
            e = n2 * k1
            if e == 0:
                continue
            if e == 4:
                re, im = part[k1]
                part[k1] = (im, -re) if sign < 0 else (-im, re)
            else:
                ang = sign * 2 * math.pi * e / 16
                part[k1] = cmul(part[k1], math.cos(ang), math.sin(ang))
        cols.append(part)
    out = [None] * 16
    for k1 in range(4):
        part = dft4([cols[n2][k1] for n2 in range(4)], sign)
        for k2 in range(4):
            out[k1 + 4 * k2] = part[k2]
    return out


def dyf_pos(t):
    if t < 12:
        return 2304 + 384 * (t // 3), 128 + 128 * (t % 3)
    u = t - 12
    return 1152 + 384 * (u // 2), 256 + 128 * (u % 2)


def rows8(x):
    acc = x[0:8]
    for r in range(8, x.shape[0], 8):
        acc = acc + x[r : r + 8]
    return acc


def lane_pair(x):
    return x[:, 0:128] + x[:, 128:256]


class Ring:
    def __init__(self, dps, reps):
        self.D, self.R = dps, reps
        self.N = dps * reps
        self.dp = lax.axis_index("dp")
        self.rp = lax.axis_index("rep")
        self.me = self.dp * reps + self.rp
        self.core = lax.rem(self.rp, 2)
        self.x = lax.div(self.rp, 2)

    def dev(self, i):
        return (lax.div(i, self.R), lax.rem(i, self.R))

    def barrier(self):
        sem = pltpu.get_barrier_semaphore()

        def body(d, c):
            peer = lax.rem(self.me + d, self.N)
            pl.semaphore_signal(sem, inc=1, device_id=self.dev(peer), device_id_type=MESH)
            return c

        lax.fori_loop(1, self.N, body, 0)
        pl.semaphore_wait(sem, self.N - 1)

    def send(self, src, dst, ss, rs, device):
        pltpu.make_async_remote_copy(
            src_ref=src, dst_ref=dst, send_sem=ss, recv_sem=rs, device_id=device, device_id_type=MESH
        ).start()

    def sibling(self):
        return (self.dp, self.rp + 1 - 2 * self.core)

    def across(self):
        return (self.dp, lax.rem(self.rp + 2, 4))


def await_bytes(ref, sem):
    pltpu.make_async_copy(ref, ref, sem).wait()


def kernel(dps, reps, fused, *refs):
    it = iter(refs)
    feat_h, cot_h, holes, tab_h = next(it), next(it), next(it), next(it)
    if fused:
        w_ll, w_gl, w_lg, w_in, w_fu, w_out, gain_in, bias_in = (next(it) for _ in range(8))
    else:
        WCAT, WGLN, WINT, WFU, WFUT, WOUT, GBI = (next(it) for _ in range(7))
    block_out, input_grad, norm_out = next(it), next(it), next(it)
    if fused:
        flat_out = next(it)
    else:
        out_ll, out_gl, out_lg, out_in, out_fu, out_out = (next(it) for _ in range(6))
    F, WF, Z3, D3, PX, DY, PS, ST, PF, Y, J, DC, A = (next(it) for _ in range(13))
    EXA, EXB, DYX, ACC, ACF, COLS, COLF, ROWP, GFU, GOUT, GIN = (next(it) for _ in range(11))
    ARB, ar_s, ar_r, COTB, OUTB, cot_sem, out_sem, in_sem, WGL = (next(it) for _ in range(9))
    if fused:
        WCAT, WINT, WFU, WFUT, WOUT = (next(it) for _ in range(5))
        WI, GBB, WFO, WB, OWNI, OWNF, OWNB, g_sem = (next(it) for _ in range(8))
        RB, RF, RI = ([next(it) for _ in range(4)] for _ in range(3))
        GI, rs_sem = next(it), next(it)
    ring = Ring(dps, reps)
    D, R, N = ring.D, ring.R, ring.N
    me, dp, rp = ring.me, ring.dp, ring.rp
    count = float(POS * N)
    fcount = float(FREQ * N)

    copy_f = pltpu.make_async_copy(feat_h.at[:, :, LOC:ALL], F.at[1:65], in_sem.at[0])
    copy_f.start()
    copy_l = pltpu.make_async_copy(feat_h.at[:, :, 0:LOC], Z3.at[1:65, :, 128:256], in_sem.at[1])
    copy_l.start()
    copy_a = pltpu.make_async_copy(tab_h, A, in_sem.at[2])
    copy_a.start()

    def ar_start(k):
        b = k % 2

        def body(d, c):
            peer = lax.rem(me + d, N)
            ring.send(ARB.at[b, me], ARB.at[b, me], ar_s.at[k], ar_r.at[k], ring.dev(peer))
            return c

        lax.fori_loop(1, N, body, 0)

    def ar_wait(k):
        b = k % 2
        await_bytes(ARB.at[b, pl.ds(0, N - 1)], ar_r.at[k])
        await_bytes(ARB.at[b, pl.ds(0, N - 1)], ar_s.at[k])
        return jnp.sum(ARB[b], axis=0)

    q_f, q_b = 64, 256
    if fused:
        OWNI[0:48, :] = w_in[:, 0:128]
        OWNI[48:96, :] = jnp.concatenate([w_in[:, 128:192], jnp.zeros((48, 64), BF)], axis=1)
        for j in range(3):
            OWNF[48 * j : 48 * j + 48, :] = w_fu[:, 128 * j : 128 * j + 128]
            part = w_out[:, 128 * j : 128 * j + 128].astype(F32)
            part = jnp.concatenate([part, jnp.zeros((8, 128), F32)], axis=0)
            OWNF[144 + 32 * j : 176 + 32 * j, :] = part.astype(BF)
            OWNB[576 + 144 * j : 720 + 144 * j, :] = w_lg[:, 128 * j : 128 * j + 128]
        OWNF[240:256, :] = jnp.zeros((16, 128), BF)
        OWNB[0:432, :] = w_gl[...]
        OWNB[432:576, :] = w_ll[...]
        OWNB[1008:1024, :] = jnp.zeros((16, 128), BF)
        own = gain_in.shape[1]
        both = jnp.concatenate([gain_in[...], bias_in[...]], axis=0).astype(F32)
        both = jnp.concatenate([both, jnp.zeros((2, 1152 - own), F32)], axis=1)
        both = jnp.concatenate([both, jnp.zeros((6, 1152), F32)], axis=0)
        both = pltpu.roll(both, own * dp, axis=1)
        GBB[dp] = jnp.zeros((24, 128), F32)
        for j in range(9):
            GBB[dp, j : j + 1, :] = both[0:1, 128 * j : 128 * j + 128]
            GBB[dp, 9 + j : 10 + j, :] = both[1:2, 128 * j : 128 * j + 128]
        WI[dp] = OWNI[...]
        WFO[dp, pl.ds(pl.multiple_of(rp * q_f, 16), q_f)] = OWNF[pl.ds(pl.multiple_of(rp * q_f, 16), q_f)]
        WB[dp, pl.ds(pl.multiple_of(rp * q_b, 16), q_b)] = OWNB[pl.ds(pl.multiple_of(rp * q_b, 16), q_b)]

    ring.barrier()

    def quarter(ref, q, index):
        return ref.at[:, pl.ds(pl.multiple_of(index * q, 16), q)]

    def spread(src, dst, ss, rs):
        def body(d, c):
            ring.send(src, dst, ss, rs, (lax.rem(dp + d, D), rp))
            return c

        lax.fori_loop(1, D, body, 0)

    class Gather:
        def __init__(self, own_ref, buf, q, base):
            self.own, self.buf, self.q, self.base = own_ref, buf, q, base

        def sem(self, i):
            return g_sem.at[self.base + i]

        def first(self):
            rows = pl.ds(pl.multiple_of(rp * self.q, 16), self.q)
            spread(self.own.at[rows], self.buf.at[dp, rows], self.sem(0), self.sem(1))

        def second(self):
            await_bytes(self.buf.at[pl.ds(0, D - 1), pl.ds(0, self.q)], self.sem(1))
            part = quarter(self.buf, self.q, rp)
            ring.send(part, part, self.sem(2), self.sem(3), ring.across())
            ring.send(part, part, self.sem(4), self.sem(5), ring.sibling())

        def third(self):
            one = self.buf.at[:, pl.ds(0, self.q)]
            await_bytes(one, self.sem(3))
            part = quarter(self.buf, self.q, lax.rem(rp + 2, 4))
            ring.send(part, part, self.sem(6), self.sem(7), ring.sibling())

        def last(self):
            one = self.buf.at[:, pl.ds(0, self.q)]
            await_bytes(one, self.sem(5))
            await_bytes(one, self.sem(7))
            await_bytes(self.buf.at[pl.ds(0, D - 1), pl.ds(0, self.q)], self.sem(0))
            await_bytes(one, self.sem(2))
            await_bytes(one, self.sem(4))
            await_bytes(one, self.sem(6))

    if fused:
        spread(OWNI, WI.at[dp], g_sem.at[0], g_sem.at[1])
        spread(GBB.at[dp], GBB.at[dp], g_sem.at[2], g_sem.at[3])
        gather_f = Gather(OWNF, WFO, q_f, 4)
        gather_b = Gather(OWNB, WB, q_b, 12)
        gather_f.first()
        gather_b.first()

    edge_row = jnp.zeros((SIDE, 384), BF)
    for ref in (F, Z3, D3):
        ref[0] = edge_row
        ref[65] = edge_row
    DC[0] = jnp.zeros((SIDE, ALL), BF)
    DC[65] = jnp.zeros((SIDE, ALL), BF)

    def make_wf(h, c):
        row = 0.25 + holes[pl.ds(h, 1), :].astype(F32)
        row = jnp.concatenate([row, row], axis=1)
        WF[h] = (jnp.broadcast_to(row, (128, 128)).T)[0:64].astype(BF)
        return c

    lax.fori_loop(0, SIDE, make_wf, 0)

    def shifted(x, lanes_mask_first, by):
        moved = pltpu.roll(x, by % x.shape[0], axis=0)
        at = lax.rem(lax.broadcasted_iota(jnp.int32, x.shape, 0), SIDE)
        return jnp.where(at == lanes_mask_first, 0.0, moved)

    copy_l.wait()

    def make_z3(h, c):
        x = Z3[h + 1, :, 128:256].astype(F32)
        Z3[h + 1, :, 0:128] = shifted(x, 0, 1).astype(BF)
        Z3[h + 1, :, 256:384] = shifted(x, 63, -1).astype(BF)
        return c

    lax.fori_loop(0, SIDE, make_z3, 0)
    copy_f.wait()

    if fused:
        await_bytes(WI.at[pl.ds(0, D - 1)], g_sem.at[1])
        first = jnp.concatenate([WI[s, 0:48] for s in range(D)], axis=0).astype(F32)
        WINT[0:128, :] = first.T.astype(BF)
        first = jnp.concatenate([WI[s, 48:96] for s in range(D)], axis=0).astype(F32)
        WINT[128:192, :] = (first.T)[0:64].astype(BF)

    def tile(ref, h0, lo, hi):
        return jnp.concatenate([ref[h0 + 16 * j + 1, :, lo:hi] for j in range(4)], axis=0)

    ACC[...] = jnp.zeros_like(ACC)

    def input_proj(h0, c):
        ps = dot(WINT[...], tile(F, h0, 0, GLO), 1, 1)
        PS[h0] = ps
        ACC[0:HALF] += lane_pair(ps)
        ACC[HALF : 2 * HALF] += lane_pair(ps * ps)
        return c

    lax.fori_loop(0, 16, input_proj, 0)

    def row_of(lo, hi):
        parts = []
        for r in range(lo, hi, 128):
            n = min(128, hi - r)
            x = ACF[r : r + n] if hi > 384 or lo >= 384 else ACC[r : r + n]
            parts.append(x)
        return parts

    def to_row(x):
        n = x.shape[0]
        if n < 128:
            x = jnp.concatenate([x, jnp.zeros((128 - n, 128), F32)], axis=0)
        return jnp.sum(x.T, axis=0, keepdims=True)

    def put_rows(k, at, rows):
        b = k % 2
        for i, row in enumerate(rows):
            ARB[b, me, at + i : at + i + 1, :] = row

    def put_zero(k, at):
        ARB[k % 2, me, at:8, :] = jnp.zeros((8 - at, 128), F32)

    def spec_rows():
        return [to_row(ACC[0:128]), to_row(ACC[128:192]), to_row(ACC[192:320]), to_row(ACC[320:384])]

    put_rows(0, 0, spec_rows())
    put_zero(0, 4)
    ar_start(0)

    if fused:
        gather_f.second()
        await_bytes(GBB.at[pl.ds(0, D - 1)], g_sem.at[3])
        gb = GBB[0]
        for s in range(1, D):
            gb = gb + GBB[s]
    else:
        gb = GBI[...]
    wide = []
    for kind in range(2):
        row = jnp.concatenate([gb[9 * kind + j : 9 * kind + j + 1, :] for j in range(9)], axis=1)
        wide.append(jnp.broadcast_to(row, (8, 1152)))

    def piece(kind, offset, width):
        return pltpu.roll(wide[kind], (1152 - offset) % 1152, axis=1)[0:1, 0:width]

    def col(row):
        return jnp.broadcast_to(row, (128, 128)).T

    for kind, at in ((0, 2), (1, 3)):
        spec = piece(kind, 0, 256)
        COLS[at, 0:128] = col(spec[:, 0:128])
        COLS[at, 128:192] = col(spec[:, 128:256])[0:64]
        freq = piece(kind, 192, 384)
        for j in range(3):
            COLF[at, 128 * j : 128 * j + 128] = col(freq[:, 128 * j : 128 * j + 128])
        ROWP[at : at + 1, 0:128] = piece(kind, 576, 128)
        ROWP[at : at + 1, 128:512] = piece(kind, 704, 384)

    def moments(total, square, n):
        mean = total / n
        scale = lax.rsqrt(square / n - mean * mean + EPS)
        return scale, mean * scale

    if fused:
        gather_b.second()
        gather_f.third()

    copy_a.wait()
    tot = ar_wait(0)
    for r, (lo, n) in enumerate(((0, 128), (128, 64))):
        scale, ms = moments(tot[r : r + 1], tot[r + 2 : r + 3], count)
        COLS[0, lo : lo + n] = col(scale)[0:n]
        COLS[1, lo : lo + n] = col(ms)[0:n]
    COLS[6] = COLS[0] * COLS[2]

    def two(x):
        return jnp.concatenate([x, x], axis=1)

    EXA[...] = jnp.zeros_like(EXA)

    def spec_front(h0, c):
        rows = pl.ds(pl.multiple_of(h0 * HALF, 8), HALF)
        xh = PS[h0] * two(COLS[0]) - two(COLS[1])
        sp = gelu_value(xh * two(COLS[2]) + two(COLS[3]))
        DY[rows, 0:256] = sp
        res = dot(sp.astype(BF), A[h0])
        DY[rows, 256:512] = res[:, 0:256]
        EXA[...] += res[:, 256:384]
        return c

    lax.fori_loop(0, 16, spec_front, 0)
    low_half = lax.broadcasted_iota(jnp.int32, (HALF, 128), 1) < 64

    def split_ext(x):
        re = jnp.where(low_half, x, 0.0)
        im = jnp.where(low_half, pltpu.roll(x, 64, axis=1), 0.0)
        return re, im

    def join_ext(re, im):
        return jnp.where(low_half, re, pltpu.roll(im, 64, axis=1))

    ext_re, ext_im = split_ext(EXA[...])
    ST[16, 0:HALF] = ext_re.astype(BF)
    ST[16, HALF : 2 * HALF] = ext_im.astype(BF)

    def grab(ref, g, base):
        z = []
        for a in range(16):
            rows = pl.ds(pl.multiple_of(a * HALF + g * 8, 8), 8)
            z.append((ref[rows, base : base + 128], ref[rows, base + 128 : base + 256]))
        return z

    def fwd_fft(i, c):
        halves = [dft16(grab(DY, 2 * i + s, 256), -1) for s in range(2)]
        for k in range(16):
            for comp in range(2):
                both = jnp.concatenate([halves[0][k][comp], halves[1][k][comp]], axis=0)
                ST[k, pl.ds(pl.multiple_of(comp * HALF + i * 16, 16), 16)] = both.astype(BF)
        return c

    lax.fori_loop(0, 12, fwd_fft, 0)

    if fused:
        gather_b.third()
        gather_f.last()
        for j in range(3):
            fu = jnp.concatenate([WFO[s, 48 * j : 48 * j + 48] for s in range(D)], axis=0)
            WFU[:, 128 * j : 128 * j + 128] = fu
            WFUT[128 * j : 128 * j + 128, :] = fu.astype(F32).T.astype(BF)
            wo = jnp.concatenate(
                [WFO[s, 144 + 32 * j : 176 + 32 * j].astype(F32)[0:24] for s in range(D)], axis=0
            )
            WOUT[:, 128 * j : 128 * j + 128] = wo.astype(BF)
    ACF[...] = jnp.zeros_like(ACF)

    def unit(t, c):
        pf = dot(WFUT[...], jnp.concatenate([ST[2 * t], ST[2 * t + 1]], axis=1))
        PF[2 * t] = pf[:, 0:128]
        PF[2 * t + 1] = pf[:, 128:256]
        ACF[0:384] += lane_pair(pf)
        ACF[384:768] += lane_pair(pf * pf)
        return c

    lax.fori_loop(0, 8, unit, 0)
    pf = dot(WFUT[...], ST[16])
    PF[16] = pf
    ACF[0:384] += pf
    ACF[384:768] += pf * pf

    def freq_rows():
        return [to_row(ACF[128 * j : 128 * j + 128]) for j in range(6)]

    put_rows(1, 0, freq_rows())
    put_zero(1, 6)
    ar_start(1)

    if fused:
        gather_b.last()
        for s in range(D):
            WCAT[144 * s : 144 * s + 144, 0:128] = WB[s, 432:576]
            for j in range(3):
                WCAT[144 * s : 144 * s + 144, 128 + 128 * j : 256 + 128 * j] = WB[s, 576 + 144 * j : 720 + 144 * j]

    def gl_runs():
        runs = []
        share = 3456 // D
        row = 0
        while row < 3456:
            n = min(384 - row % 384, share - row % share)
            runs.append((row // 384, row % 384, row // share, row % share, n))
            row += n
        return runs

    if fused:
        for tap, c0, s, r0, n in gl_runs():
            WGL[tap // 3, c0 : c0 + n, 128 * (tap % 3) : 128 * (tap % 3) + 128] = WB[s, r0 : r0 + n]
    else:
        for tap in range(9):
            WGL[tap // 3, :, 128 * (tap % 3) : 128 * (tap % 3) + 128] = WGLN[384 * tap : 384 * tap + 384]

    ROWP[8:16, :] = jnp.zeros((8, ALL), F32)
    ACCR = ROWP

    def slab(ref, i, off, n):
        return ref[pl.ds(8 * i + off, 8), :, 0:n].reshape(512, n)

    def conv_fwd(i, c):
        rows = pl.ds(pl.multiple_of(512 * i, 512), 512)
        lhs = jnp.concatenate([slab(Z3, i, a, 384) for a in range(3)], axis=1)
        res = dot(lhs, WCAT[...])
        PX[rows, 128:512] = res[:, 128:512]
        lhs = jnp.concatenate([slab(F, i, a, 384) for a in range(3)], axis=1)
        gl = dot(lhs, WGL[...].reshape(1152, 384))
        total = res[:, 0:128] + gl[:, 128:256] + shifted(gl[:, 0:128], 0, 1) + shifted(gl[:, 256:384], 63, -1)
        PX[rows, 0:128] = total
        ACCR[8:16, 0:128] += rows8(total)
        ACCR[8:16, 128:256] += rows8(total * total)
        return c

    lax.fori_loop(0, 8, conv_fwd, 0)
    put_rows(2, 0, [jnp.sum(ACCR[8:16, 128 * j : 128 * j + 128], axis=0, keepdims=True) for j in range(2)])
    put_zero(2, 2)

    tot = ar_wait(1)
    ar_start(2)
    for j in range(3):
        scale, ms = moments(tot[j : j + 1], tot[j + 3 : j + 4], fcount)
        COLF[0, 128 * j : 128 * j + 128] = col(scale)
        COLF[1, 128 * j : 128 * j + 128] = col(ms)
    COLF[6] = COLF[0] * COLF[2]
    lane = lax.broadcasted_iota(jnp.int32, (8, 128), 1)
    doubled = jnp.where(lax.rem(lane, 32) == 0, 1.0, 2.0).astype(F32)

    def freq_act(v, rows):
        xh = v * COLF[0, rows] - COLF[1, rows]
        return xh, xh * COLF[2, rows] + COLF[3, rows]

    def inv_fft(i, c):
        halves = []
        for s in range(2):
            z = []
            rr = pl.ds(pl.multiple_of(16 * i + 8 * s, 8), 8)
            ri = pl.ds(pl.multiple_of(HALF + 16 * i + 8 * s, 8), 8)
            for k in range(16):
                re = gelu_value(freq_act(PF[k, rr], rr)[1]) * doubled
                im = gelu_value(freq_act(PF[k, ri], ri)[1]) * doubled
                z.append((re, im))
            halves.append(dft16(z, 1))
        for a in range(16):
            for comp in range(2):
                both = jnp.concatenate([halves[0][a][comp], halves[1][a][comp]], axis=0)
                Y[a, pl.ds(pl.multiple_of(i * 16, 16), 16), 128 * comp : 128 * comp + 128] = both.astype(BF)
        return c

    lax.fori_loop(0, 12, inv_fft, 0)
    mixed = gelu_value((PF[16] * COLF[0] - COLF[1]) * COLF[2] + COLF[3])
    EXB[...] = join_ext(mixed[0:HALF], mixed[HALF : 2 * HALF]).astype(BF)
    ROWP[8:16, :] = jnp.zeros((8, ALL), F32)
    ROWP[16:24, :] = jnp.zeros((8, ALL), F32)

    def join(h0, c):
        rows = pl.ds(pl.multiple_of(h0 * HALF, 8), HALF)
        back = dot(jnp.concatenate([Y[h0], EXB[...]], axis=1), A[h0], 1, 1)
        joined = (DY[rows, 0:256] + back).astype(BF)
        J[h0] = joined
        pg = dot(joined, WOUT[...], 0, 0)
        for j in range(4):
            at = pl.ds(pl.multiple_of((h0 + 16 * j) * SIDE, SIDE), SIDE)
            v = PX[at, 128:512] + pg[64 * j : 64 * j + 64]
            PX[at, 128:512] = v
            ROWP[8:16, 128:512] += rows8(v)
            ROWP[16:24, 128:512] += rows8(v * v)
        return c

    lax.fori_loop(0, 16, join, 0)

    def put_norm_rows(k, lo, tiles):
        for j in range(tiles):
            at = lo + 128 * j
            put_rows(k, j, [jnp.sum(ROWP[8:16, at : at + 128], axis=0, keepdims=True)])
            put_rows(k, tiles + j, [jnp.sum(ROWP[16:24, at : at + 128], axis=0, keepdims=True)])
        put_zero(k, 2 * tiles)

    put_norm_rows(3, 128, 3)
    tot = ar_wait(2)
    ar_start(3)
    scale, ms = moments(tot[0:1], tot[1:2], count)
    ROWP[0:1, 0:128] = scale
    ROWP[1:2, 0:128] = ms

    def cot_copy(i, lo, hi):
        return pltpu.make_async_copy(
            cot_h.at[pl.ds(8 * i, 8), :, lo:hi], COTB.at[lax.rem(i, 2), :, :, lo:hi], cot_sem.at[lax.rem(i, 2)]
        )

    def out_copy(dst, i, lo, hi):
        return pltpu.make_async_copy(
            OUTB.at[lax.rem(i, 2), :, :, lo:hi], dst.at[pl.ds(8 * i, 8), :, lo:hi], out_sem.at[lax.rem(i, 2)]
        )

    def out_norm(lo, hi):
        cot_copy(0, lo, hi).start()
        ROWP[8:16, lo:hi] = jnp.zeros((8, hi - lo), F32)
        ROWP[16:24, lo:hi] = jnp.zeros((8, hi - lo), F32)

        def chunk(i, c):
            slot = lax.rem(i, 2)
            cot_copy(i, lo, hi).wait()

            @pl.when(i < 7)
            def _():
                cot_copy(i + 1, lo, hi).start()

            @pl.when(i > 1)
            def _():
                out_copy(block_out, i - 2, lo, hi).wait()

            def one(hh, c2):
                h = 8 * i + hh
                for r in (0, 32):
                    at = pl.ds(pl.multiple_of(h * SIDE + r, 32), 32)
                    wf = WF[h, r : r + 32].astype(F32)
                    for l0 in range(lo, hi, 128):
                        ls = slice(l0, l0 + 128)
                        xh = PX[at, ls] * ROWP[0:1, ls] - ROWP[1:2, ls]
                        value, slope = gelu_both(xh * ROWP[2:3, ls] + ROWP[3:4, ls])
                        dy = slope * (COTB[slot, hh, r : r + 32, ls].astype(F32) * wf)
                        DY[at, ls] = dy
                        if l0 == 0:
                            base = Z3[h + 1, r : r + 32, 128:256]
                        else:
                            base = F[h + 1, r : r + 32, l0 - 128 : l0]
                        OUTB[slot, hh, r : r + 32, ls] = (base.astype(F32) + value).astype(BF)
                        ROWP[8:16, ls] += rows8(dy)
                        ROWP[16:24, ls] += rows8(dy * xh)
                return c2

            lax.fori_loop(0, 8, one, 0)
            out_copy(block_out, i, lo, hi).start()
            return c

        lax.fori_loop(0, 8, chunk, 0)
        out_copy(block_out, 6, lo, hi).wait()
        out_copy(block_out, 7, lo, hi).wait()

    out_norm(0, 128)
    put_norm_rows(4, 0, 1)
    tot = ar_wait(3)
    ar_start(4)
    for j in range(3):
        scale, ms = moments(tot[j : j + 1], tot[j + 3 : j + 4], count)
        ROWP[0:1, 128 + 128 * j : 256 + 128 * j] = scale
        ROWP[1:2, 128 + 128 * j : 256 + 128 * j] = ms
    out_norm(128, 512)
    put_norm_rows(5, 128, 3)
    tot = ar_wait(4)
    ar_start(5)

    def set_back(tot, lo, tiles, out_at):
        for j in range(tiles):
            ls = slice(lo + 128 * j, lo + 128 * j + 128)
            ROWP[4:5, ls] = tot[j : j + 1] / count
            ROWP[5:6, ls] = tot[tiles + j : tiles + j + 1] / count
            ROWP[6:7, ls] = ROWP[0:1, ls] * ROWP[2:3, ls]
            norm_out[out_at + j : out_at + j + 1, :] = tot[tiles + j : tiles + j + 1]
            norm_out[16 + out_at + j : 17 + out_at + j, :] = tot[j : j + 1]

    def norm_back(lo, hi):
        def one(h, c):
            for r in (0, 32):
                at = pl.ds(pl.multiple_of(h * SIDE + r, 32), 32)
                for l0 in range(lo, hi, 128):
                    ls = slice(l0, l0 + 128)
                    xh = PX[at, ls] * ROWP[0:1, ls] - ROWP[1:2, ls]
                    d = ROWP[6:7, ls] * (DY[at, ls] - ROWP[4:5, ls] - xh * ROWP[5:6, ls])
                    DC[h + 1, r : r + 32, ls] = d.astype(BF)
            return c

        lax.fori_loop(0, SIDE, one, 0)

    set_back(tot, 0, 1, 5)
    norm_back(0, 128)

    def make_d3(h, c):
        x = DC[h + 1, :, 0:128].astype(F32)
        D3[h + 1, :, 0:128] = shifted(x, 63, -1).astype(BF)
        D3[h + 1, :, 128:256] = DC[h + 1, :, 0:128]
        D3[h + 1, :, 256:384] = shifted(x, 0, 1).astype(BF)
        return c

    lax.fori_loop(0, SIDE, make_d3, 0)

    for r in range(0, 3456, 384):
        DY[r : r + 384, 0:128] = jnp.zeros((384, 128), F32)

    def wgrad_gl(i, c):
        zt = slab(F, i, 1, 384).T
        for a in range(3):
            res = dot(zt, slab(D3, i, 2 - a, 384))
            for b in range(3):
                r = 384 * (3 * a + b)
                DY[r : r + 384, 0:128] += res[:, 128 * b : 128 * b + 128]
        return c

    lax.fori_loop(0, 8, wgrad_gl, 0)
    tot = ar_wait(5)
    set_back(tot, 128, 3, 6)
    norm_back(128, 512)

    EXA[...] = jnp.zeros_like(EXA)
    GOUT[...] = jnp.zeros_like(GOUT)

    def join_back(h0, c):
        rows = pl.ds(pl.multiple_of(h0 * HALF, 8), HALF)
        dg = tile(DC, h0, 128, 512)
        dj = dot(WOUT[...], dg, 1, 1)
        PX[rows, 0:256] = dj
        GOUT[...] += dot(J[h0], dg)
        res = dot(dj.astype(BF), A[h0])
        PX[rows, 256:512] = res[:, 0:256]
        EXA[...] += res[:, 256:384]
        return c

    lax.fori_loop(0, 16, join_back, 0)

    def freq_back(g, c):
        z = dft16(grab(PX, g, 256), -1)
        for comp in range(2):
            rows = pl.ds(pl.multiple_of(comp * HALF + 8 * g, 8), 8)
            s0 = jnp.zeros((8, 128), F32)
            s1 = jnp.zeros((8, 128), F32)
            for k in range(16):
                xh, y = freq_act(PF[k, rows], rows)
                dy = gelu_slope(y) * (z[k][comp] * doubled)
                r0, l0 = dyf_pos(k)
                DY[pl.ds(pl.multiple_of(r0 + comp * HALF + 8 * g, 8), 8), l0 : l0 + 128] = dy
                s0 = s0 + dy
                s1 = s1 + dy * xh
            ACF[rows] = s0
            ACF[pl.ds(pl.multiple_of(384 + comp * HALF + 8 * g, 8), 8)] = s1
        return c

    lax.fori_loop(0, 24, freq_back, 0)
    ext_re, ext_im = split_ext(EXA[...])
    xh = PF[16] * COLF[0] - COLF[1]
    dy = gelu_slope(xh * COLF[2] + COLF[3]) * jnp.concatenate([ext_re, ext_im], axis=0)
    DYX[...] = dy
    ACF[0:384] += dy
    ACF[384:768] += dy * xh
    put_rows(6, 0, freq_rows())
    put_zero(6, 6)
    ar_start(6)

    for r in range(0, 1152, 384):
        DY[r : r + 384, 128:512] = jnp.zeros((384, 384), F32)
        DY[1152 + r : 1536 + r, 128:256] = jnp.zeros((384, 128), F32)

    def wgrad_loc(i, c):
        zt = slab(Z3, i, 1, 384).T
        for a in range(3):
            res = dot(zt, slab(DC, i, 2 - a, 512))
            DY[1152 + 384 * a : 1536 + 384 * a, 128:256] += res[:, 0:128]
            DY[384 * a : 384 * a + 384, 128:512] += res[:, 128:512]
        return c

    lax.fori_loop(0, 8, wgrad_loc, 0)

    class Scatter:
        def __init__(self, buf, scratch, q, base):
            self.buf, self.q, self.base = buf, q, base
            self.one, self.two, self.three, self.four = scratch
            self.slot = 2 * ring.core + ring.x

        def sem(self, i):
            return rs_sem.at[self.base + i]

        def rows(self, index, n):
            return pl.ds(pl.multiple_of(index * self.q, 16), n * self.q)

        def first(self):
            there = self.buf.at[:, self.rows(2 * (1 - ring.core), 2)]
            ring.send(there, self.one, self.sem(0), self.sem(1), ring.sibling())

        def second(self):
            await_bytes(self.one, self.sem(1))
            q = self.q

            def add(s, c):
                for half in range(2):
                    at = self.rows(2 * ring.core + half, 1)
                    mine = self.buf[s, at].astype(F32) + self.one[s, half * q : half * q + q].astype(F32)
                    self.buf[s, at] = mine.astype(BF)
                return c

            lax.fori_loop(0, D, add, 0)
            there = self.buf.at[:, self.rows(2 * ring.core + 1 - ring.x, 1)]
            ring.send(there, self.two, self.sem(2), self.sem(3), ring.across())

        def third(self):
            await_bytes(self.two, self.sem(3))
            at = self.rows(self.slot, 1)

            def add(s, c):
                mine = self.buf[s, at].astype(F32) + self.two[s].astype(F32)
                self.buf[s, at] = mine.astype(BF)
                return c

            lax.fori_loop(0, D, add, 0)

            def body(d, c):
                s = lax.rem(dp + d, D)
                ring.send(self.buf.at[s, at], self.three.at[dp], self.sem(4), self.sem(5), (s, rp))
                return c

            lax.fori_loop(1, D, body, 0)
            self.three[dp] = self.buf[dp, at]

        def fourth(self):
            await_bytes(self.three.at[pl.ds(0, D - 1)], self.sem(5))
            total = self.three[0].astype(F32)
            for s in range(1, D):
                total = total + self.three[s].astype(F32)
            self.four[self.slot] = total.astype(BF)
            for d in range(1, 4):
                ring.send(
                    self.four.at[self.slot], self.four.at[self.slot], self.sem(6), self.sem(7), (dp, lax.rem(rp + d, 4))
                )

        def last(self):
            await_bytes(self.four.at[pl.ds(0, 3)], self.sem(7))
            await_bytes(self.one, self.sem(0))
            await_bytes(self.two, self.sem(2))
            await_bytes(self.three.at[pl.ds(0, D - 1)], self.sem(4))
            await_bytes(self.four.at[pl.ds(0, 3)], self.sem(6))

    if fused:
        for s in range(D):
            for tap, c0, shard, r0, n in gl_runs():
                if shard == s:
                    r = 384 * tap + c0
                    WB[s, r0 : r0 + n] = DY[r : r + n, 0:128].astype(BF)
            WB[s, 432:576] = DY[1152 + 144 * s : 1296 + 144 * s, 128:256].astype(BF)
            for j in range(3):
                ls = slice(128 + 128 * j, 256 + 128 * j)
                WB[s, 576 + 144 * j : 720 + 144 * j] = DY[144 * s : 144 * s + 144, ls].astype(BF)
            WB[s, 1008:1024] = jnp.zeros((16, 128), BF)
        scatter_b = Scatter(WB, RB, q_b, 0)
        scatter_f = Scatter(WFO, RF, q_f, 8)
        scatter_i = Scatter(GI, RI, 32, 16)
        scatter_b.first()
    else:
        out_gl[...] = DY[0:3456, 0:128]
        out_ll[...] = DY[1152:2304, 128:256]
        out_lg[...] = DY[0:1152, 128:512]

    tot = ar_wait(6)
    for j in range(3):
        COLF[4, 128 * j : 128 * j + 128] = col(tot[j : j + 1] / fcount)
        COLF[5, 128 * j : 128 * j + 128] = col(tot[j + 3 : j + 4] / fcount)
        norm_out[2 + j : 3 + j, :] = tot[j + 3 : j + 4]
        norm_out[18 + j : 19 + j, :] = tot[j : j + 1]
    GFU[...] = jnp.zeros_like(GFU)

    def dpf_tile(k, dy):
        xh = PF[k] * COLF[0] - COLF[1]
        return (COLF[6] * (dy - COLF[4] - xh * COLF[5])).astype(BF)

    for t in range(8):
        spots = [dyf_pos(2 * t), dyf_pos(2 * t + 1)]
        parts = [dpf_tile(2 * t + e, DY[r : r + 384, l : l + 128]) for e, (r, l) in enumerate(spots)]
        dpf = jnp.concatenate(parts, axis=1)
        GFU[...] += dot(jnp.concatenate([ST[2 * t], ST[2 * t + 1]], axis=1), dpf, 1, 1)
        ds = dot(WFU[...], dpf)
        for e, (r, l) in enumerate(spots):
            DY[r : r + 384, l : l + 128] = ds[:, 128 * e : 128 * e + 128]
    dpf = dpf_tile(16, DYX[...])
    GFU[...] += dot(ST[16], dpf, 1, 1)
    ds = dot(WFU[...], dpf)
    EXB[...] = join_ext(ds[0:HALF], ds[HALF : 2 * HALF]).astype(BF)
    if fused:
        scatter_b.second()

    def adj_fft(i, c):
        halves = []
        for s in range(2):
            z = []
            for k in range(16):
                r0, l0 = dyf_pos(k)
                z.append(
                    tuple(
                        DY[pl.ds(pl.multiple_of(r0 + comp * HALF + 16 * i + 8 * s, 8), 8), l0 : l0 + 128]
                        for comp in range(2)
                    )
                )
            halves.append(dft16(z, 1))
        for a in range(16):
            for comp in range(2):
                both = jnp.concatenate([halves[0][a][comp], halves[1][a][comp]], axis=0)
                Y[a, pl.ds(pl.multiple_of(i * 16, 16), 16), 128 * comp : 128 * comp + 128] = both.astype(BF)
        return c

    lax.fori_loop(0, 12, adj_fft, 0)
    ACC[...] = jnp.zeros_like(ACC)

    def spec_back(h0, c):
        rows = pl.ds(pl.multiple_of(h0 * HALF, 8), HALF)
        back = dot(jnp.concatenate([Y[h0], EXB[...]], axis=1), A[h0], 1, 1)
        xh = PS[h0] * two(COLS[0]) - two(COLS[1])
        dy = gelu_slope(xh * two(COLS[2]) + two(COLS[3])) * (PX[rows, 0:256] + back)
        DY[rows, 256:512] = dy
        ACC[0:HALF] += lane_pair(dy)
        ACC[HALF : 2 * HALF] += lane_pair(dy * xh)
        return c

    lax.fori_loop(0, 16, spec_back, 0)
    put_rows(7, 0, spec_rows())
    put_zero(7, 4)
    ar_start(7)
    if fused:
        for s in range(D):
            for j in range(3):
                ls = slice(128 * j, 128 * j + 128)
                WFO[s, 48 * j : 48 * j + 48] = GFU[48 * s : 48 * s + 48, ls].astype(BF)
                part = jnp.concatenate([GOUT[24 * s : 24 * s + 24, ls], jnp.zeros((8, 128), F32)], axis=0)
                WFO[s, 144 + 32 * j : 176 + 32 * j] = part.astype(BF)
            WFO[s, 240:256] = jnp.zeros((16, 128), BF)
        scatter_f.first()
        scatter_b.third()
    else:
        out_fu[...] = GFU[...]
        out_out[...] = GOUT[...]

    def dgrad(i, c):
        rows = pl.ds(pl.multiple_of(512 * i, 512), 512)
        lhs = jnp.concatenate([slab(DC, i, 2 - a, 512) for a in range(3)], axis=1)
        rhs = jnp.concatenate([WCAT[384 * a : 384 * a + 384] for a in range(3)], axis=1)
        res = dot(lhs, rhs, 1, 1)
        PX[rows, 0:128] = res[:, 128:256] + shifted(res[:, 0:128], 63, -1) + shifted(res[:, 256:384], 0, 1)
        lhs = jnp.concatenate([slab(D3, i, 2 - a, 384) for a in range(3)], axis=1)
        rhs = jnp.concatenate([WGL[a] for a in range(3)], axis=1)
        PX[rows, 128:512] = dot(lhs, rhs, 1, 1)
        return c

    lax.fori_loop(0, 8, dgrad, 0)
    if fused:
        scatter_b.fourth()
        scatter_f.second()

    tot = ar_wait(7)
    for r, (lo, n) in enumerate(((0, 128), (128, 64))):
        COLS[4, lo : lo + n] = col(tot[r : r + 1] / count)[0:n]
        COLS[5, lo : lo + n] = col(tot[r + 2 : r + 3] / count)[0:n]
        norm_out[r : r + 1, :] = tot[r + 2 : r + 3]
        norm_out[16 + r : 17 + r, :] = tot[r : r + 1]
    norm_out[9:16, :] = jnp.zeros((7, 128), F32)
    norm_out[25:32, :] = jnp.zeros((7, 128), F32)
    GIN[...] = jnp.zeros_like(GIN)

    def spec_grad(h0, c):
        rows = pl.ds(pl.multiple_of(h0 * HALF, 8), HALF)
        xh = PS[h0] * two(COLS[0]) - two(COLS[1])
        d = two(COLS[6]) * (DY[rows, 256:512] - two(COLS[4]) - xh * two(COLS[5]))
        d = d.astype(BF)
        J[h0] = d
        GIN[...] += dot(d, tile(F, h0, 0, GLO))
        return c

    lax.fori_loop(0, 16, spec_grad, 0)
    if fused:
        gin = jnp.concatenate([GIN[...], jnp.zeros((64, 384), F32)], axis=0).T
        for s in range(D):
            GI[s, 0:48] = gin[48 * s : 48 * s + 48, 0:128].astype(BF)
            GI[s, 48:96] = gin[48 * s : 48 * s + 48, 128:256].astype(BF)
            GI[s, 96:128] = jnp.zeros((32, 128), BF)
        scatter_i.first()
        scatter_f.third()
    else:
        out_in[...] = GIN[...]

    def spec_field(h0, c):
        dg = dot(J[h0], WINT[...], 0, 0)
        for j in range(4):
            at = pl.ds(pl.multiple_of((h0 + 16 * j) * SIDE, SIDE), SIDE)
            PX[at, 128:512] += dg[64 * j : 64 * j + 64]
        return c

    lax.fori_loop(0, 16, spec_field, 0)
    if fused:
        scatter_i.second()

    cot_copy(0, 0, ALL).start()

    def finish(i, c):
        slot = lax.rem(i, 2)
        cot_copy(i, 0, ALL).wait()

        @pl.when(i < 7)
        def _():
            cot_copy(i + 1, 0, ALL).start()

        @pl.when(i > 1)
        def _():
            out_copy(input_grad, i - 2, 0, ALL).wait()

        def one(hh, c2):
            h = 8 * i + hh
            for r in (0, 32):
                at = pl.ds(pl.multiple_of(h * SIDE + r, 32), 32)
                wf = WF[h, r : r + 32].astype(F32)
                for l0 in range(0, 512, 128):
                    ls = slice(l0, l0 + 128)
                    g = PX[at, ls] + COTB[slot, hh, r : r + 32, ls].astype(F32) * wf
                    OUTB[slot, hh, r : r + 32, ls] = g.astype(BF)
            return c2

        lax.fori_loop(0, 8, one, 0)
        out_copy(input_grad, i, 0, ALL).start()
        return c

    lax.fori_loop(0, 8, finish, 0)
    if fused:
        scatter_i.third()
        scatter_f.fourth()
        scatter_i.fourth()
        scatter_b.last()
        scatter_f.last()
        scatter_i.last()
        for at, q, four in ((0, q_b, RB[3]), (1024, q_f, RF[3]), (1280, 32, RI[3])):
            for r in range(4):
                flat_out[at + r * q : at + r * q + q, :] = four[r].astype(F32)
        await_bytes(WI.at[pl.ds(0, D - 1)], g_sem.at[0])
        await_bytes(GBB.at[pl.ds(0, D - 1)], g_sem.at[2])
    out_copy(input_grad, 6, 0, ALL).wait()
    out_copy(input_grad, 7, 0, ALL).wait()


def run_block(features, cotangent, holes, weights, gains, biases, fused):
    dps, reps = lax.axis_size("dp"), lax.axis_size("rep")
    N = dps * reps
    any_spec = pl.BlockSpec(memory_space=pl.ANY)
    vmem = pl.BlockSpec(memory_space=pltpu.VMEM)
    table = jnp.asarray(dft_table())
    args = [features, cotangent, holes, table] + list(weights) + list(gains)
    if fused:
        args = args + list(biases)
    out_shape = [
        jax.ShapeDtypeStruct((SIDE, SIDE, ALL), BF),
        jax.ShapeDtypeStruct((SIDE, SIDE, ALL), BF),
        jax.ShapeDtypeStruct((32, 128), F32),
    ]
    if fused:
        out_shape.append(jax.ShapeDtypeStruct((1408, 128), F32))
    else:
        for shape in ((1152, 128), (3456, 128), (1152, 384), (192, 384), (384, 384), (192, 384)):
            out_shape.append(jax.ShapeDtypeStruct(shape, F32))
    V = pltpu.VMEM
    dma = pltpu.SemaphoreType.DMA
    scratch = [
        V((66, SIDE, 384), BF),
        V((SIDE, SIDE, 128), BF),
        V((66, SIDE, 384), BF),
        V((66, SIDE, 384), BF),
        V((POS, ALL), F32),
        V((POS, ALL), F32),
        V((16, HALF, 256), F32),
        V((17, 384, 128), BF),
        V((17, 384, 128), F32),
        V((16, HALF, 256), BF),
        V((16, HALF, 256), BF),
        V((66, SIDE, ALL), BF),
        V((16, 256, 384), BF),
        V((HALF, 128), F32),
        V((HALF, 128), BF),
        V((384, 128), F32),
        V((384, 128), F32),
        V((768, 128), F32),
        V((7, HALF, 128), F32),
        V((7, 384, 128), F32),
        V((24, ALL), F32),
        V((384, 384), F32),
        V((HALF, 384), F32),
        V((HALF, 384), F32),
        V((2, N, 8, 128), F32),
        dma((8,)),
        dma((8,)),
        V((2, 8, SIDE, ALL), BF),
        V((2, 8, SIDE, ALL), BF),
        dma((2,)),
        dma((2,)),
        dma((3,)),
        V((3, 384, 384), BF),
    ]
    if fused:
        scratch += [
            V((1152, ALL), BF),
            V((HALF, 384), BF),
            V((384, 384), BF),
            V((384, 384), BF),
            V((HALF, 384), BF),
            V((dps, 96, 128), BF),
            V((dps, 24, 128), F32),
            V((dps, 256, 128), BF),
            V((dps, 1024, 128), BF),
            V((96, 128), BF),
            V((256, 128), BF),
            V((1024, 128), BF),
            dma((20,)),
        ]
        for q in (256, 64, 32):
            scratch += [V((dps, 2 * q, 128), BF), V((dps, q, 128), BF), V((dps, q, 128), BF), V((4, q, 128), BF)]
        scratch += [V((dps, 128, 128), BF), dma((24,))]
    return pl.pallas_call(
        functools.partial(kernel, dps, reps, fused),
        out_shape=out_shape,
        in_specs=[any_spec, any_spec, vmem, any_spec] + [vmem] * (len(args) - 4),
        out_specs=[any_spec, any_spec] + [vmem] * (len(out_shape) - 2),
        scratch_shapes=scratch,
        compiler_params=pltpu.CompilerParams(
            collective_id=0, has_side_effects=True, vmem_limit_bytes=64 * 1024 * 1024 - 65536
        ),
        cost_estimate=pl.CostEstimate(flops=40_000_000_000, bytes_accessed=30_000_000, transcendentals=10_000_000),
    )(*args)


def on_device(features, cotangent, holes, w_ll, w_gl, w_lg, w_in, w_fu, w_out, gains, biases):
    dps, reps = lax.axis_size("dp"), lax.axis_size("rep")
    share = gains.shape[1]
    first = lax.axis_index("dp") * share
    shards = (w_ll, w_gl, w_lg, w_in, w_fu, w_out)
    rows = [w.shape[1] for w in shards]
    fused = dps == 8 and reps == 4
    if fused:
        weights = [w[0] for w in shards]
        block_out, input_grad, norms, flat = run_block(
            features[0], cotangent[0], holes[0], weights, [gains], [biases], True
        )
        cut = lambda at, n: flat[at : at + n]
        grads = [
            cut(432, 144),
            cut(0, 432),
            jnp.concatenate([cut(576 + 144 * j, 144) for j in range(3)], axis=1),
            jnp.concatenate([cut(1280, 48), cut(1328, 48)[:, 0:64]], axis=1),
            jnp.concatenate([cut(1024 + 48 * j, 48) for j in range(3)], axis=1),
            jnp.concatenate([cut(1168 + 32 * j, 24) for j in range(3)], axis=1),
        ]
        grads = [g[None] for g in grads]
    else:
        full = [lax.all_gather(w, "dp", axis=1, tiled=True)[0] for w in shards]
        table = jnp.concatenate([gains, biases], axis=0).astype(F32)
        table = lax.all_gather(table, "dp", axis=1, tiled=True)
        table = jnp.pad(table, ((0, 0), (0, 1152 - table.shape[1]))).reshape(18, 128)
        table = jnp.pad(table, ((0, 6), (0, 0)))
        weights = [jnp.concatenate([full[0], full[2]], axis=1), full[1], full[3].T, full[4], full[4].T, full[5]]
        block_out, input_grad, norms, g_ll, g_gl, g_lg, g_in, g_fu, g_out = run_block(
            features[0], cotangent[0], holes[0], weights, [table], None, False
        )
        grads = []
        for g in (g_ll, g_gl, g_lg, g_in.T, g_fu, g_out):
            g = lax.psum(g[None], "rep")
            grads.append(lax.psum_scatter(g, "dp", scatter_dimension=1, tiled=True))
    norm_rows = []
    for at in (0, 16):
        part = norms[at : at + 9].reshape(1, 1152)
        part = jnp.concatenate([part[:, 0:192], part[:, 256:1152]], axis=1)
        norm_rows.append(lax.dynamic_slice_in_dim(part, first, share, 1))
    return (block_out[None], input_grad[None], *grads, *norm_rows)


def solution(mesh):
    whole = P(("dp", "rep"), None, None, None)
    rows = P(None, "dp", None)
    in_specs = (whole, whole, P(("dp", "rep"), None, None)) + (rows,) * 6 + (P(None, "dp"),) * 2
    out_specs = (whole, whole) + (rows,) * 6 + (P(None, "dp"),) * 2
    return jax.shard_map(on_device, mesh=mesh, in_specs=in_specs, out_specs=out_specs, check_vma=False)
```

time: 1300 us -> 199 us (0.15)
  blocking collectives: 450 us -> 0 us
  waiting for transfers between devices: 396 us -> 0 us
  matrix products: 294 us -> 0 us
  Pallas kernels: 0 us -> 181 us
  other arithmetic: 76.3 us -> 3.25 us
  local copies, waits for them, and re-layouts: 59.9 us -> 13.2 us
  between operations: 17.1 us -> 0.69 us
    reduce_scatter x4 -> x0, waiting for transfers between devices: 269 us -> none  [the longest x1 69.4 us: on_device(): lax.psum_scatter(grad_gl, 'dp', scatter_dimension=1, tiled=True)]
    psum x6 -> x0, blocking collectives: 239 us -> none  [the longest x3 124 us: norm_back(): totals = lax.psum(jnp.concatenate(pieces), ('dp', 'rep'))]
    all_gather x6 -> x0, blocking collectives: 188 us -> none  [the longest x1 32.4 us: on_device(): lax.all_gather(w_lg, 'dp', axis=1, tiled=True)]
    pallas_call x0 -> x1, Pallas kernels: none -> 181 us  [run_block(): pl.pallas_call(functools.partial(kernel, dps, reps, fused), out_shape=out...]
    dot_general x39 -> x0, matrix products: 141 us -> none  [the longest x20 55.3 us: over_rows(): return jnp.einsum('hk,bhlc->bklc', table, values, precision=HIGH)]
    transpose x3 -> x0, matrix products: 113 us -> none  [conv_backward(): jnp.transpose(taps, (1, 2, 0, 3)).reshape(9 * channels, outputs)]
    unnamed x9 -> x0, waiting for transfers between devices: 66.4 us -> none
    psum x1 -> x0, waiting for transfers between devices: 60.9 us -> none  [on_device(): lax.psum(grad_in.astype(jnp.bfloat16), 'rep').astype(jnp.float32)]
  transfers between devices with their start and end apart: 7 -> 0, of which waited for: 7 -> 0; matrix products, arithmetic and copies ran while one was open for 5% -> 0% of each run, Pallas kernels for 0% -> 0%
where the time goes in v1:
time: 199 us; the launch traced here: 198 us
  Pallas kernels  181 us (91%)
  local copies, waits for them, and re-layouts  13.2 us (7%)
  other arithmetic  3.25 us (2%)
    pallas_call x1, Pallas kernels, run_block(): pl.pallas_call(functools.partial(kernel, dps, reps, fused), out_shape=out...  181 us
    unnamed x7, local copies, waits for them, and re-layouts  7.59 us

profile of v1, /device:TPU:0, one launch (start us, length us, event | category | flops | bytes accessed | tf_op | source)
XLA Modules:
  0.0 198.2 jit_solution(5972071308781701708)
XLA Ops:
  0.6 181.1 %shard_map.195 = (bf16[64,64,512]{2,1,0:T(8,128)(2,1)}, bf16[64,64,512]{2,1,0:T(8,128)(2,1)}, f32[32,128]{1,0:T(8,128)}, f32[1408,128]{1,0:T(8,128)}) custom-call(bf16[64,64,512]{2,1,0:T(8,128)(2,1)} %bitcast.41, bf16[64,64,512]{2,1,0:T(8,128)(2,1)} %bitcast.42, s32[64,64]{1,0:T(8,128)} %bitcast.47, bf16[16,256,384]{2,1,0:T(8,128)(2,1)} %constant.14.clone.refs_3_, ...), custom_call_target="tpu_custom_call" | custom-call | flops 40000000000 | bytes 30000000 | tf_op jit(solution)/shard_map/pallas_call | solution.py:1131
  181.8 0.8 fusion.3
  182.6 0.6 maximum_bitcast_fusion.1
  183.2 1.6 fusion.4
  184.8 0.7 maximum_bitcast_fusion
  185.5 0.7 slice_bitcast_fusion.2
  186.3 0.7 fusion
  187.0 0.7 fusion.2
  187.7 0.6 maximum_bitcast_fusion.3
  188.3 0.7 slice.65
  189.1 0.6 maximum_bitcast_fusion.2
  189.7 1.6 slice_bitcast_fusion
  191.3 0.0 copy-start
  191.3 4.8 %copy.30 = bf16[1,64,64,512]{3,2,1,0:T(8,128)(2,1)} copy(bf16[1,64,64,512]{3,2,1,0:T(8,128)(2,1)} %bitcast.36) | data formatting | bytes 8388608
  196.2 0.0 copy-done
  196.2 2.0 %copy.31 = bf16[1,64,64,512]{3,2,1,0:T(8,128)(2,1)} copy(bf16[1,64,64,512]{3,2,1,0:T(8,128)(2,1)S(1)} %bitcast.35) | data formatting | bytes 8388608
  (6 shorter events, 0.0 us)
Async XLA Ops:
  191.3 4.9 %copy-start = (bf16[64,64,512]{2,1,0:T(8,128)(2,1)S(1)}, bf16[64,64,512]{2,1,0:T(8,128)(2,1)}, u32[]{:S(2)}) copy-start(bf16[64,64,512]{2,1,0:T(8,128)(2,1)} %get-tuple-element.15) | copy-start | bytes 12582916

commit v2 on v1

v2 whole, which is shorter than its diff:
```python
import functools
import math

import jax
import jax.numpy as jnp
import ml_dtypes
import numpy as np
from jax import lax
from jax.experimental import pallas as pl
from jax.experimental.pallas import tpu as pltpu
from jax.sharding import PartitionSpec as P

EPS = 1e-05
K0 = math.sqrt(2.0 / math.pi)
K1 = 0.044715
MESH = pl.DeviceIdType.MESH
F32 = jnp.float32
BF = jnp.bfloat16
SIDE = 64
LOC = 128
GLO = 384
HALF = 192
ALL = LOC + GLO
WIDTHS = (HALF, GLO, LOC, GLO)
POS = SIDE * SIDE
FREQ = SIDE * (SIDE // 2 + 1)


def dft_table():
    a = np.arange(16)[:, None, None, None, None]
    j = np.arange(4)[None, :, None, None, None]
    w = np.arange(64)[None, None, :, None, None]
    k1 = np.arange(4)[None, None, None, :, None]
    l = np.arange(32)[None, None, None, None, :]
    angle = 2 * np.pi / 64 * (((a + 16 * j) * k1 + w * l) % 64)
    main_re = np.cos(angle).reshape(16, 256, 128) / 64
    main_im = -np.sin(angle).reshape(16, 256, 128) / 64
    k = np.arange(64)[None, None, None, :]
    a, j, w = a[..., 0], j[..., 0], w[..., 0]
    angle = 2 * np.pi / 64 * (((a + 16 * j) * k + 32 * w) % 64)
    ext_re = np.cos(angle).reshape(16, 256, 64) / 64
    ext_im = -np.sin(angle).reshape(16, 256, 64) / 64
    return np.concatenate([main_re, main_im, ext_re, ext_im], axis=-1).astype(ml_dtypes.bfloat16)


def dot(a, b, ca=1, cb=0):
    return lax.dot_general(a, b, (((ca,), (cb,)), ((), ())), preferred_element_type=F32)


def gate(y):
    y2 = y * y
    return y2, 0.5 + 0.5 * jnp.tanh(y * (K0 + K0 * K1 * y2))


def gelu_value(y):
    return y * gate(y)[1]


def gelu_both(y):
    y2, s = gate(y)
    value = y * s
    return value, s + value * (1.0 - s) * (2.0 * K0 + 6.0 * K0 * K1 * y2)


def gelu_slope(y):
    return gelu_both(y)[1]


def cmul(z, c, s):
    return (z[0] * c - z[1] * s, z[0] * s + z[1] * c)


def dft4(z, sign):
    (ar, ai), (br, bi), (cr, ci), (dr, di) = z
    pr, pi, qr, qi = ar + cr, ai + ci, ar - cr, ai - ci
    rr, ri, sr, si = br + dr, bi + di, br - dr, bi - di
    tr, ti = (si, -sr) if sign < 0 else (-si, sr)
    return [(pr + rr, pi + ri), (qr + tr, qi + ti), (pr - rr, pi - ri), (qr - tr, qi - ti)]


def dft16(z, sign):
    cols = []
    for n2 in range(4):
        part = dft4([z[4 * n1 + n2] for n1 in range(4)], sign)
        for k1 in range(1, 4):
            e = n2 * k1
            if e == 0:
                continue
            if e == 4:
                re, im = part[k1]
                part[k1] = (im, -re) if sign < 0 else (-im, re)
            else:
                ang = sign * 2 * math.pi * e / 16
                part[k1] = cmul(part[k1], math.cos(ang), math.sin(ang))
        cols.append(part)
    out = [None] * 16
    for k1 in range(4):
        part = dft4([cols[n2][k1] for n2 in range(4)], sign)
        for k2 in range(4):
            out[k1 + 4 * k2] = part[k2]
    return out


def dyf_pos(t):
    if t < 12:
        return 2304 + 384 * (t // 3), 128 + 128 * (t % 3)
    u = t - 12
    return 1152 + 384 * (u // 2), 256 + 128 * (u % 2)


def rows8(x):
    acc = x[0:8]
    for r in range(8, x.shape[0], 8):
        acc = acc + x[r : r + 8]
    return acc


def lane_pair(x):
    return x[:, 0:128] + x[:, 128:256]


def await_bytes(ref, sem):
    pltpu.make_async_copy(ref, ref, sem).wait()


class Ring:
    def __init__(self, dps, reps):
        self.D, self.R = dps, reps
        self.N = dps * reps
        self.dp = lax.axis_index("dp")
        self.rp = lax.axis_index("rep")
        self.me = self.dp * reps + self.rp
        self.core = lax.rem(self.rp, 2)
        self.x = lax.div(self.rp, 2)
        self.y = lax.rem(self.dp, 2)
        self.z = lax.div(self.dp, 2)

    def dev(self, i):
        return (lax.div(i, self.R), lax.rem(i, self.R))

    def barrier(self):
        sem = pltpu.get_barrier_semaphore()

        def body(d, c):
            peer = lax.rem(self.me + d, self.N)
            pl.semaphore_signal(sem, inc=1, device_id=self.dev(peer), device_id_type=MESH)
            return c

        lax.fori_loop(1, self.N, body, 0)
        pl.semaphore_wait(sem, self.N - 1)

    def send(self, src, dst, ss, rs, device):
        pltpu.make_async_remote_copy(
            src_ref=src, dst_ref=dst, send_sem=ss, recv_sem=rs, device_id=device, device_id_type=MESH
        ).start()

    def sibling(self):
        return (self.dp, self.rp + 1 - 2 * self.core)

    def across(self):
        return (self.dp, lax.rem(self.rp + 2, 4))

    def beside(self):
        return (self.dp + 1 - 2 * self.y, self.rp)


class Gather:
    def __init__(self, ring, own, buf, sems, base):
        self.ring, self.own, self.buf, self.sems, self.base = ring, own, buf, sems, base
        self.q = own.shape[0] // 4

    def sem(self, i):
        return self.sems.at[self.base + i]

    def rows(self, i):
        return pl.ds(pl.multiple_of(i * self.q, 16), self.q)

    def place(self):
        rows = self.rows(self.ring.rp)
        self.buf[self.ring.z, self.ring.y, rows] = self.own[rows]

    def along_z(self):
        g = self.ring
        rows = self.rows(g.rp)
        for d in range(1, 4):
            there = (2 * lax.rem(g.z + d, 4) + g.y, g.rp)
            g.send(self.own.at[rows], self.buf.at[g.z, g.y, rows], self.sem(0), self.sem(1), there)

    def along_y(self):
        g = self.ring
        await_bytes(self.buf.at[pl.ds(0, 3), 0, pl.ds(0, self.q)], self.sem(1))
        part = self.buf.at[:, g.y, self.rows(g.rp)]
        g.send(part, part, self.sem(2), self.sem(3), g.beside())

    def along_x(self):
        g = self.ring
        await_bytes(self.buf.at[:, 0, pl.ds(0, self.q)], self.sem(3))
        part = self.buf.at[:, :, self.rows(g.rp)]
        g.send(part, part, self.sem(4), self.sem(5), g.across())
        g.send(part, part, self.sem(6), self.sem(7), g.sibling())

    def between(self):
        g = self.ring
        await_bytes(self.buf.at[:, :, pl.ds(0, self.q)], self.sem(5))
        part = self.buf.at[:, :, self.rows(lax.rem(g.rp + 2, 4))]
        g.send(part, part, self.sem(8), self.sem(9), g.sibling())

    def last(self):
        one = self.buf.at[:, :, pl.ds(0, self.q)]
        for i in (7, 9, 4, 6, 8):
            await_bytes(one, self.sem(i))
        await_bytes(self.buf.at[pl.ds(0, 3), 0, pl.ds(0, self.q)], self.sem(0))
        await_bytes(self.buf.at[:, 0, pl.ds(0, self.q)], self.sem(2))


class Scatter:
    def __init__(self, ring, buf, scratch, sems, base):
        self.ring, self.buf, self.sems, self.base = ring, buf, sems, base
        self.one, self.two, self.three, self.four, self.done = scratch
        self.q = buf.shape[2] // 4
        self.slot = 2 * ring.core + ring.x

    def sem(self, i):
        return self.sems.at[self.base + i]

    def rows(self, index, n):
        return pl.ds(pl.multiple_of(index * self.q, 16), n * self.q)

    def between(self):
        g = self.ring
        there = self.buf.at[:, :, self.rows(2 * (1 - g.core), 2)]
        g.send(there, self.one, self.sem(0), self.sem(1), g.sibling())

    def add(self, zi, yi, at, other):
        self.buf[zi, yi, at] = (self.buf[zi, yi, at].astype(F32) + other.astype(F32)).astype(BF)

    def along_x(self):
        g = self.ring
        await_bytes(self.one, self.sem(1))

        def body(s, c):
            zi, yi = lax.div(s, 2), lax.rem(s, 2)
            self.add(zi, yi, self.rows(2 * g.core, 2), self.one[zi, yi])
            return c

        lax.fori_loop(0, 8, body, 0)
        there = self.buf.at[:, :, self.rows(2 * g.core + 1 - g.x, 1)]
        g.send(there, self.two, self.sem(2), self.sem(3), g.across())

    def along_y(self):
        g = self.ring
        await_bytes(self.two, self.sem(3))
        at = self.rows(self.slot, 1)

        def body(s, c):
            zi, yi = lax.div(s, 2), lax.rem(s, 2)
            self.add(zi, yi, at, self.two[zi, yi])
            return c

        lax.fori_loop(0, 8, body, 0)
        g.send(self.buf.at[:, 1 - g.y, at], self.three, self.sem(4), self.sem(5), g.beside())

    def along_z(self):
        g = self.ring
        await_bytes(self.three, self.sem(5))
        at = self.rows(self.slot, 1)
        for k in range(4):
            self.add(k, g.y, at, self.three[k])
        for d in range(1, 4):
            zz = lax.rem(g.z + d, 4)
            g.send(self.buf.at[zz, g.y, at], self.four.at[g.z], self.sem(6), self.sem(7), (2 * zz + g.y, g.rp))
        self.four[g.z] = self.buf[g.z, g.y, at]

    def to_copies(self):
        g = self.ring
        await_bytes(self.four.at[pl.ds(0, 3)], self.sem(7))
        total = self.four[0].astype(F32)
        for k in range(1, 4):
            total = total + self.four[k].astype(F32)
        self.done[self.slot] = total.astype(BF)
        mine = self.done.at[self.slot]
        for d in range(1, 4):
            g.send(mine, mine, self.sem(8), self.sem(9), (g.dp, lax.rem(g.rp + d, 4)))

    def last(self):
        three = self.done.at[pl.ds(0, 3)]
        await_bytes(three, self.sem(9))
        await_bytes(self.one, self.sem(0))
        await_bytes(self.two, self.sem(2))
        await_bytes(self.three, self.sem(4))
        await_bytes(self.four.at[pl.ds(0, 3)], self.sem(6))
        await_bytes(three, self.sem(8))


AR_ROWS = (4, 6, 2, 6, 2, 6, 6, 4)
CHUNKS = (448, 576, 256, 128)
STARTS = (0, 448, 1024, 1280)


def mask_tile(row):
    at0 = lax.broadcasted_iota(jnp.int32, (SIDE, SIDE), 0)
    at1 = lax.broadcasted_iota(jnp.int32, (SIDE, SIDE), 1)
    diag = jnp.where(at0 == at1, jnp.broadcast_to(row, (SIDE, SIDE)), 0.0)
    return dot(diag.astype(BF), jnp.ones((SIDE, 128), BF))


def shifted(x, edge, by):
    moved = pltpu.roll(x, by % x.shape[0], axis=0)
    at = lax.rem(lax.broadcasted_iota(jnp.int32, x.shape, 0), SIDE)
    return jnp.where(at == edge, 0.0, moved)


def gl_runs(shards):
    runs = []
    share = 9 * GLO // shards
    row = 0
    while row < 9 * GLO:
        n = min(GLO - row % GLO, share - row % share)
        runs.append((row // GLO, row % GLO, row // share, row % share, n))
        row += n
    return runs


def col(row):
    return jnp.broadcast_to(row, (128, 128)).T


def two(x):
    return jnp.concatenate([x, x], axis=1)


def to_row(x):
    n = x.shape[0]
    if n < 128:
        x = jnp.concatenate([x, jnp.zeros((128 - n, 128), F32)], axis=0)
    return jnp.sum(x.T, axis=0, keepdims=True)


def moments(total, square, n):
    mean = total / n
    scale = lax.rsqrt(square / n - mean * mean + EPS)
    return scale, mean * scale


def kernel(dps, reps, fused, *refs):
    it = iter(refs)

    def take(n):
        return [next(it) for _ in range(n)]

    feat_h, cot_h, holes, tab_h = take(4)
    if fused:
        w_ll, w_gl, w_lg, w_in, w_fu, w_out, gain_in, bias_in = take(8)
    else:
        WCAT, WGLN, WINT, WFU, WFUT, WOUT, GBI = take(7)
    block_out, field_out, norm_out = take(3)
    if fused:
        (flat_out,) = take(1)
    else:
        out_ll, out_gl, out_lg, out_in, out_fu, out_out = take(6)
    F, WF, Z3, D3, PX, DY, PS, ST, PF, Y, J, DC, A, COT = take(14)
    EXA, EXB, DYX, ACC, ACF, COLS, COLF, ROWP, GBR, GOUT, WGL = take(11)
    ARB = take(8)
    ar_s, ar_r, io_sem = take(3)
    if fused:
        WCAT, WINT, WFU, WFUT, WOUT, WI, GBB, OWNI, g_sem, rs_sem = take(10)
        OWN, WB, RS = take(3), take(4), [take(5) for _ in range(4)]
    ring = Ring(dps, reps)
    D, R, N = ring.D, ring.R, ring.N
    me, dp, rp = ring.me, ring.dp, ring.rp
    count = float(POS * N)
    fcount = float(FREQ * N)

    copy_l = pltpu.make_async_copy(feat_h.at[:, :, 0:LOC], Z3.at[1:65, :, 128:256], io_sem.at[0])
    copy_l.start()
    copy_f = pltpu.make_async_copy(feat_h.at[:, :, LOC:ALL], F.at[1:65], io_sem.at[1])
    copy_f.start()
    copy_a = pltpu.make_async_copy(tab_h, A, io_sem.at[2])
    copy_a.start()
    copy_c = pltpu.make_async_copy(cot_h, COT, io_sem.at[3])
    copy_c.start()

    def put(src, dst):
        copy = pltpu.make_async_copy(src, dst, io_sem.at[7])
        copy.start()
        copy.wait()

    def ar_start(k):
        def body(d, c):
            peer = lax.rem(me + d, N)
            ring.send(ARB[k].at[me], ARB[k].at[me], ar_s.at[k], ar_r.at[k], ring.dev(peer))
            return c

        lax.fori_loop(1, N, body, 0)

    def ar_wait(k):
        await_bytes(ARB[k].at[pl.ds(0, N - 1)], ar_r.at[k])
        await_bytes(ARB[k].at[pl.ds(0, N - 1)], ar_s.at[k])
        return jnp.sum(ARB[k][...], axis=0)

    def put_rows(k, at, rows):
        for i, row in enumerate(rows):
            ARB[k][me, at + i : at + i + 1, :] = row

    if fused:
        O1, O2, OF = OWN
        OWNI[0:48, :] = w_in[:, 0:128]
        OWNI[48:96, :] = jnp.concatenate([w_in[:, 128:192], jnp.zeros((48, 64), BF)], axis=1)
        own = gain_in.shape[1]
        for kind, ref in ((0, gain_in), (1, bias_in)):
            row = jnp.concatenate([ref[...].astype(F32), jnp.zeros((1, 256 - own), F32)], axis=1)
            for j in range(2):
                GBB[dp, 2 * kind + j : 2 * kind + j + 1, :] = row[:, 128 * j : 128 * j + 128]
        WI[dp] = OWNI[...]
        for j in range(3):
            OF[48 * j : 48 * j + 48, :] = w_fu[:, 128 * j : 128 * j + 128]
            part = w_out[:, 128 * j : 128 * j + 128].astype(F32)
            part = jnp.concatenate([part, jnp.zeros((8, 128), F32)], axis=0)
            OF[144 + 32 * j : 176 + 32 * j, :] = part.astype(BF)
            O2[144 + 144 * j : 288 + 144 * j, :] = w_lg[:, 128 * j : 128 * j + 128]
        OF[240:256, :] = jnp.zeros((16, 128), BF)
        O2[0:144, :] = w_ll[...]
        O1[0:432, :] = w_gl[...]
        O1[432:448, :] = jnp.zeros((16, 128), BF)
        W1, W2, WFO, GI = WB
        gather_1 = Gather(ring, O1, W1, g_sem, 4)
        gather_2 = Gather(ring, O2, W2, g_sem, 14)
        gather_f = Gather(ring, OF, WFO, g_sem, 24)
        for g in (gather_f, gather_2, gather_1):
            g.place()

    ring.barrier()

    def spread(src, dst, ss, rs):
        def body(d, c):
            ring.send(src, dst, ss, rs, (lax.rem(dp + d, D), rp))
            return c

        lax.fori_loop(1, D, body, 0)

    if fused:
        spread(OWNI, WI.at[dp], g_sem.at[0], g_sem.at[1])
        gather_f.along_z()
        spread(GBB.at[dp], GBB.at[dp], g_sem.at[2], g_sem.at[3])
        gather_2.along_z()
        gather_1.along_z()

    edge_row = jnp.zeros((SIDE, 384), BF)
    for ref in (F, Z3, D3):
        ref[0] = edge_row
        ref[65] = edge_row
    DC[0] = jnp.zeros((SIDE, ALL), BF)
    DC[65] = jnp.zeros((SIDE, ALL), BF)

    def make_wf(i, c):
        for e in range(4):
            WF[4 * i + e] = mask_tile(0.25 + holes[pl.ds(4 * i + e, 1), :].astype(F32)).astype(BF)
        return c

    lax.fori_loop(0, 16, make_wf, 0)
    copy_l.wait()

    def make_z3(i, c):
        for e in range(2):
            h = 2 * i + e + 1
            x = Z3[h, :, 128:256].astype(F32)
            Z3[h, :, 0:128] = shifted(x, 0, 1).astype(BF)
            Z3[h, :, 256:384] = shifted(x, 63, -1).astype(BF)
        return c

    lax.fori_loop(0, 32, make_z3, 0)
    copy_f.wait()

    if fused:
        await_bytes(WI.at[pl.ds(0, D - 1)], g_sem.at[1])
        first = jnp.concatenate([WI[s, 0:48] for s in range(D)], axis=0).astype(F32)
        WINT[0:128, :] = first.T.astype(BF)
        first = jnp.concatenate([WI[s, 48:96] for s in range(D)], axis=0).astype(F32)
        WINT[128:192, :] = (first.T)[0:64].astype(BF)

    def tile(ref, h0, lo, hi):
        return jnp.concatenate([ref[h0 + 16 * j + 1, :, lo:hi] for j in range(4)], axis=0)

    def rows_of(h0):
        return pl.ds(pl.multiple_of(h0 * HALF, 8), HALF)

    ACC[...] = jnp.zeros_like(ACC)

    def input_proj(i, c):
        w = WINT[...]
        res = [dot(w, tile(F, 4 * i + e, 0, GLO), 1, 1) for e in range(4)]
        for e in range(4):
            PS[4 * i + e] = res[e]
        ACC[0:HALF] += sum(lane_pair(ps) for ps in res)
        ACC[HALF : 2 * HALF] += sum(lane_pair(ps * ps) for ps in res)
        return c

    lax.fori_loop(0, 4, input_proj, 0)

    def spec_rows():
        return [to_row(ACC[0:128]), to_row(ACC[128:192]), to_row(ACC[192:320]), to_row(ACC[320:384])]

    put_rows(0, 0, spec_rows())
    ar_start(0)

    if fused:
        gather_f.along_y()
        await_bytes(GBB.at[pl.ds(0, D - 1)], g_sem.at[3])
        wide = []
        for kind in range(2):
            parts = []
            for s in range(D):
                parts.append(GBB[s, 2 * kind : 2 * kind + 1, :])
                parts.append(GBB[s, 2 * kind + 1 : 2 * kind + 2, 0 : own - 128])
            row = jnp.concatenate(parts + [jnp.ones((1, 1152 - own * D), F32)], axis=1)
            wide.append(jnp.broadcast_to(row, (8, 1152)))
    else:
        wide = []
        for kind in range(2):
            row = jnp.concatenate([GBI[9 * kind + j : 9 * kind + j + 1, :] for j in range(9)], axis=1)
            wide.append(jnp.broadcast_to(row, (8, 1152)))

    def piece(kind, offset, width):
        return pltpu.roll(wide[kind], (1152 - offset) % 1152, axis=1)[0:1, 0:width]

    for kind in range(2):
        at = 2 + kind
        spec = piece(kind, 0, 256)
        freq = piece(kind, HALF, 384)
        glo = piece(kind, HALF + GLO + LOC, 384)
        COLS[at, 0:128] = col(spec[:, 0:128])
        COLS[at, 128:192] = col(spec[:, 128:256])[0:64]
        for j in range(2):
            GBR[kind, j : j + 1, :] = spec[:, 128 * j : 128 * j + 128]
        for j in range(3):
            COLF[at, 128 * j : 128 * j + 128] = col(freq[:, 128 * j : 128 * j + 128])
            GBR[kind, 2 + j : 3 + j, :] = freq[:, 128 * j : 128 * j + 128]
            GBR[kind, 6 + j : 7 + j, :] = glo[:, 128 * j : 128 * j + 128]
        loc = piece(kind, HALF + GLO, 128)
        GBR[kind, 5:6, :] = loc
        ROWP[at : at + 1, 0:128] = loc
        ROWP[at : at + 1, 128:512] = glo

    def fold(ref):
        ref[4] = ref[0] * ref[2]
        ref[5] = ref[3] - ref[1] * ref[2]

    if fused:
        gather_2.along_y()
        gather_f.along_x()
        gather_1.along_y()

    copy_a.wait()
    tot = ar_wait(0)
    for r, (lo, n) in enumerate(((0, 128), (128, 64))):
        scale, ms = moments(tot[r : r + 1], tot[r + 2 : r + 3], count)
        COLS[0, lo : lo + n] = col(scale)[0:n]
        COLS[1, lo : lo + n] = col(ms)[0:n]
    fold(COLS)

    EXA[...] = jnp.zeros_like(EXA)

    def spec_front(i, c):
        gain, bias = two(COLS[4]), two(COLS[5])
        ext = None
        for e in range(4):
            h0 = 4 * i + e
            sp = gelu_value(PS[h0] * gain + bias)
            DY[rows_of(h0), 0:256] = sp
            res = dot(sp.astype(BF), A[h0])
            DY[rows_of(h0), 256:512] = res[:, 0:256]
            ext = res[:, 256:384] if ext is None else ext + res[:, 256:384]
        EXA[...] += ext
        return c

    lax.fori_loop(0, 4, spec_front, 0)
    if fused:
        gather_2.along_x()
        gather_f.between()
    low_half = lax.broadcasted_iota(jnp.int32, (HALF, 128), 1) < 64

    def split_ext(x):
        re = jnp.where(low_half, x, 0.0)
        im = jnp.where(low_half, pltpu.roll(x, 64, axis=1), 0.0)
        return re, im

    def join_ext(re, im):
        return jnp.where(low_half, re, pltpu.roll(im, 64, axis=1))

    ext_re, ext_im = split_ext(EXA[...])
    ST[16, 0:HALF] = ext_re.astype(BF)
    ST[16, HALF : 2 * HALF] = ext_im.astype(BF)

    def grab(ref, g, base):
        z = []
        for a in range(16):
            rows = pl.ds(pl.multiple_of(a * HALF + g * 8, 8), 8)
            z.append((ref[rows, base : base + 128], ref[rows, base + 128 : base + 256]))
        return z

    def fwd_fft(i, c):
        halves = [dft16(grab(DY, 2 * i + s, 256), -1) for s in range(2)]
        for k in range(16):
            for comp in range(2):
                both = jnp.concatenate([halves[0][k][comp], halves[1][k][comp]], axis=0)
                ST[k, pl.ds(pl.multiple_of(comp * HALF + i * 16, 16), 16)] = both.astype(BF)
        return c

    lax.fori_loop(0, 12, fwd_fft, 0)

    if fused:
        gather_1.along_x()
        gather_2.between()
        gather_f.last()
        for j in range(3):
            parts = [WFO[s // 2, s % 2, 48 * j : 48 * j + 48] for s in range(D)]
            fu = jnp.concatenate(parts, axis=0)
            WFU[:, 128 * j : 128 * j + 128] = fu
            WFUT[128 * j : 128 * j + 128, :] = fu.astype(F32).T.astype(BF)
            parts = [WFO[s // 2, s % 2, 144 + 32 * j : 176 + 32 * j].astype(F32)[0:24] for s in range(D)]
            WOUT[:, 128 * j : 128 * j + 128] = jnp.concatenate(parts, axis=0).astype(BF)

    def unit(ts):
        w = WFUT[...]
        s0 = s1 = None
        for t in ts:
            pf = dot(w, jnp.concatenate([ST[2 * t], ST[2 * t + 1]], axis=1))
            PF[2 * t] = pf[:, 0:128]
            PF[2 * t + 1] = pf[:, 128:256]
            s0 = lane_pair(pf) if s0 is None else s0 + lane_pair(pf)
            s1 = lane_pair(pf * pf) if s1 is None else s1 + lane_pair(pf * pf)
        return s0, s1

    pf = dot(WFUT[...], ST[16])
    PF[16] = pf
    ACF[0:384] = pf
    ACF[384:768] = pf * pf

    def unit_step(i, c):
        s0, s1 = unit([4 * i + e for e in range(4)])
        ACF[0:384] += s0
        ACF[384:768] += s1
        return c

    lax.fori_loop(0, 2, unit_step, 0)

    def freq_rows():
        return [to_row(ACF[128 * j : 128 * j + 128]) for j in range(6)]

    put_rows(1, 0, freq_rows())
    ar_start(1)

    if fused:
        gather_1.between()
        gather_2.last()
        for s in range(D):
            for j in range(4):
                WCAT[144 * s : 144 * s + 144, 128 * j : 128 * j + 128] = W2[s // 2, s % 2, 144 * j : 144 * j + 144]

    def slab(ref, i, off, lo, hi, n=8):
        return ref[pl.ds(n * i + off, n), :, lo:hi].reshape(n * SIDE, hi - lo)

    def block_rows(i):
        return pl.ds(pl.multiple_of(512 * i, 512), 512)

    def conv_loc(i, c):
        lhs = jnp.concatenate([slab(Z3, i, a, 0, 384) for a in range(3)], axis=1)
        PX[block_rows(i), :] = dot(lhs, WCAT[...])
        return c

    lax.fori_loop(0, 8, conv_loc, 0)

    tot = ar_wait(1)
    for j in range(3):
        scale, ms = moments(tot[j : j + 1], tot[j + 3 : j + 4], fcount)
        COLF[0, 128 * j : 128 * j + 128] = col(scale)
        COLF[1, 128 * j : 128 * j + 128] = col(ms)
    fold(COLF)
    lane = lax.broadcasted_iota(jnp.int32, (8, 128), 1)
    doubled = jnp.where(lax.rem(lane, 32) == 0, 1.0, 2.0).astype(F32)

    def freq_act(v, rows):
        return v * COLF[4, rows] + COLF[5, rows]

    def inv_fft(i, c):
        halves = []
        for s in range(2):
            z = []
            rr = pl.ds(pl.multiple_of(16 * i + 8 * s, 8), 8)
            ri = pl.ds(pl.multiple_of(HALF + 16 * i + 8 * s, 8), 8)
            for k in range(16):
                re = gelu_value(freq_act(PF[k, rr], rr)) * doubled
                im = gelu_value(freq_act(PF[k, ri], ri)) * doubled
                z.append((re, im))
            halves.append(dft16(z, 1))
        for a in range(16):
            for comp in range(2):
                both = jnp.concatenate([halves[0][a][comp], halves[1][a][comp]], axis=0)
                Y[a, pl.ds(pl.multiple_of(i * 16, 16), 16), 128 * comp : 128 * comp + 128] = both.astype(BF)
        return c

    lax.fori_loop(0, 12, inv_fft, 0)
    mixed = gelu_value(PF[16] * COLF[4] + COLF[5])
    EXB[...] = join_ext(mixed[0:HALF], mixed[HALF : 2 * HALF]).astype(BF)
    ROWP[8:24, :] = jnp.zeros((16, ALL), F32)

    def slab_rows(h0, j):
        return pl.ds(pl.multiple_of((h0 + 16 * j) * SIDE, SIDE), SIDE)

    def join(i, c):
        ext, w = EXB[...], WOUT[...]
        s0 = s1 = None
        for e in range(4):
            h0 = 4 * i + e
            back = dot(jnp.concatenate([Y[h0], ext], axis=1), A[h0], 1, 1)
            joined = (DY[rows_of(h0), 0:256] + back).astype(BF)
            J[h0] = joined
            pg = dot(joined, w, 0, 0)
            for j in range(4):
                v = PX[slab_rows(h0, j), 128:512] + pg[64 * j : 64 * j + 64]
                PX[slab_rows(h0, j), 128:512] = v
                s0 = rows8(v) if s0 is None else s0 + rows8(v)
                s1 = rows8(v * v) if s1 is None else s1 + rows8(v * v)
        ROWP[8:16, 128:512] += s0
        ROWP[16:24, 128:512] += s1
        return c

    lax.fori_loop(0, 4, join, 0)

    def put_norm_rows(k, lo, tiles):
        for j in range(tiles):
            at = lo + 128 * j
            put_rows(k, j, [jnp.sum(ROWP[8:16, at : at + 128], axis=0, keepdims=True)])
            put_rows(k, tiles + j, [jnp.sum(ROWP[16:24, at : at + 128], axis=0, keepdims=True)])

    put_norm_rows(3, 128, 3)
    ar_start(3)

    if fused:
        gather_1.last()
        for tap, c0, s, r0, n in gl_runs(D):
            WGL[tap // 3, c0 : c0 + n, 128 * (tap % 3) : 128 * (tap % 3) + 128] = W1[s // 2, s % 2, r0 : r0 + n]
    else:
        for tap in range(9):
            WGL[tap // 3, 0:384, 128 * (tap % 3) : 128 * (tap % 3) + 128] = WGLN[384 * tap : 384 * tap + 384]
    for tap in range(9):
        WGL[tap // 3, 384:512, 128 * (tap % 3) : 128 * (tap % 3) + 128] = WCAT[128 * tap : 128 * tap + 128, 0:128]

    def conv_glo(i, c):
        lhs = jnp.concatenate([slab(F, i, a, 0, 384) for a in range(3)], axis=1)
        gl = dot(lhs, jnp.concatenate([WGL[a, 0:384] for a in range(3)], axis=0))
        total = PX[block_rows(i), 0:128] + gl[:, 128:256] + shifted(gl[:, 0:128], 0, 1) + shifted(gl[:, 256:384], 63, -1)
        PX[block_rows(i), 0:128] = total
        ROWP[8:16, 0:128] += rows8(total)
        ROWP[16:24, 0:128] += rows8(total * total)
        return c

    lax.fori_loop(0, 8, conv_glo, 0)
    put_norm_rows(2, 0, 1)
    ar_start(2)

    def set_norm(tot, lo, tiles):
        for j in range(tiles):
            ls = slice(lo + 128 * j, lo + 128 * j + 128)
            scale, ms = moments(tot[j : j + 1], tot[tiles + j : tiles + j + 1], count)
            ROWP[0:1, ls] = scale
            ROWP[1:2, ls] = ms
            ROWP[4:5, ls] = scale * ROWP[2:3, ls]
            ROWP[5:6, ls] = ROWP[3:4, ls] - ms * ROWP[2:3, ls]

    def out_norm(lo, hi, sem):
        ROWP[8:24, lo:hi] = jnp.zeros((16, hi - lo), F32)

        def chunk(i, c):
            def one(hh, c2):
                h = 16 * i + hh
                for l0 in range(lo, hi, 128):
                    ls = slice(l0, l0 + 128)
                    s0 = s1 = None
                    for r in (0, 32):
                        at = pl.ds(pl.multiple_of(h * SIDE + r, 32), 32)
                        y = PX[at, ls] * ROWP[4:5, ls] + ROWP[5:6, ls]
                        value, slope = gelu_both(y)
                        dy = slope * (COT[h, r : r + 32, ls].astype(F32) * WF[h, r : r + 32].astype(F32))
                        DY[at, ls] = dy
                        if l0 == 0:
                            base = Z3[h + 1, r : r + 32, 128:256]
                        else:
                            base = F[h + 1, r : r + 32, l0 - 128 : l0]
                        DC[h + 1, r : r + 32, ls] = (base.astype(F32) + value).astype(BF)
                        s0 = rows8(dy) if s0 is None else s0 + rows8(dy)
                        s1 = rows8(dy * y) if s1 is None else s1 + rows8(dy * y)
                    ROWP[8:16, ls] += s0
                    ROWP[16:24, ls] += s1
                return c2

            lax.fori_loop(0, 16, one, 0)
            pltpu.make_async_copy(
                DC.at[pl.ds(16 * i + 1, 16), :, lo:hi], block_out.at[pl.ds(16 * i, 16), :, lo:hi], sem
            ).start()
            return c

        lax.fori_loop(0, 4, chunk, 0)

    copy_c.wait()
    set_norm(ar_wait(3), 128, 3)
    out_norm(128, 512, io_sem.at[4])
    put_norm_rows(5, 128, 3)
    ar_start(5)
    set_norm(ar_wait(2), 0, 1)
    out_norm(0, 128, io_sem.at[5])
    put_norm_rows(4, 0, 1)
    ar_start(4)

    def back_sums(tot, tiles, at):
        out = []
        for j in range(tiles):
            s1 = tot[j : j + 1]
            s2 = (tot[tiles + j : tiles + j + 1] - GBR[1, at + j : at + j + 1, :] * s1) / GBR[0, at + j : at + j + 1, :]
            norm_out[at + j : at + j + 1, :] = s2
            norm_out[16 + at + j : 17 + at + j, :] = s1
            out.append((s1, s2))
        return out

    norm_out[9:16, :] = jnp.zeros((7, 128), F32)
    norm_out[25:32, :] = jnp.zeros((7, 128), F32)

    def set_back(tot, lo, tiles, at):
        for j, (s1, s2) in enumerate(back_sums(tot, tiles, at)):
            ls = slice(lo + 128 * j, lo + 128 * j + 128)
            ROWP[6:7, ls] = ROWP[4:5, ls] * ROWP[0:1, ls] * (s2 / count)
            ROWP[7:8, ls] = ROWP[4:5, ls] * (ROWP[1:2, ls] * (s2 / count) - s1 / count)

    def norm_back(lo, hi, sem):
        pltpu.make_async_copy(DC.at[1:65, :, lo:hi], block_out.at[:, :, lo:hi], sem).wait()

        def one(h, c):
            for l0 in range(lo, hi, 128):
                ls = slice(l0, l0 + 128)
                for r in (0, 32):
                    at = pl.ds(pl.multiple_of(h * SIDE + r, 32), 32)
                    d = ROWP[4:5, ls] * DY[at, ls] - ROWP[6:7, ls] * PX[at, ls] + ROWP[7:8, ls]
                    DC[h + 1, r : r + 32, ls] = d.astype(BF)
            return c

        lax.fori_loop(0, SIDE, one, 0)

    set_back(ar_wait(5), 128, 3, 6)
    norm_back(128, 512, io_sem.at[4])

    EXA[...] = jnp.zeros_like(EXA)
    GOUT[...] = jnp.zeros_like(GOUT)

    def join_back(i, c):
        w = WOUT[...]
        dgs = []
        ext = None
        for e in range(4):
            h0 = 4 * i + e
            dg = tile(DC, h0, 128, 512)
            dgs.append(dg)
            dj = dot(w, dg, 1, 1)
            PX[rows_of(h0), 0:256] = dj
            res = dot(dj.astype(BF), A[h0])
            PX[rows_of(h0), 256:512] = res[:, 0:256]
            ext = res[:, 256:384] if ext is None else ext + res[:, 256:384]
        EXA[...] += ext
        lhs = jnp.concatenate([J[4 * i + e] for e in range(4)], axis=1)
        GOUT[...] += dot(lhs, jnp.concatenate(dgs, axis=0))
        return c

    set_back(ar_wait(4), 0, 1, 5)
    norm_back(0, 128, io_sem.at[5])
    lax.fori_loop(0, 4, join_back, 0)

    def freq_back(g, c):
        z = dft16(grab(PX, g, 256), -1)
        for comp in range(2):
            rows = pl.ds(pl.multiple_of(comp * HALF + 8 * g, 8), 8)
            s0 = s1 = None
            for k in range(16):
                y = freq_act(PF[k, rows], rows)
                dy = gelu_slope(y) * (z[k][comp] * doubled)
                r0, l0 = dyf_pos(k)
                DY[pl.ds(pl.multiple_of(r0 + comp * HALF + 8 * g, 8), 8), l0 : l0 + 128] = dy
                s0 = dy if s0 is None else s0 + dy
                s1 = dy * y if s1 is None else s1 + dy * y
            ACF[rows] = s0
            ACF[pl.ds(pl.multiple_of(384 + comp * HALF + 8 * g, 8), 8)] = s1
        return c

    lax.fori_loop(0, 24, freq_back, 0)
    ext_re, ext_im = split_ext(EXA[...])
    y = PF[16] * COLF[4] + COLF[5]
    dy = gelu_slope(y) * jnp.concatenate([ext_re, ext_im], axis=0)
    DYX[...] = dy
    ACF[0:384] += dy
    ACF[384:768] += dy * y
    put_rows(6, 0, freq_rows())
    ar_start(6)

    def make_d3(i, c):
        for e in range(2):
            h = 2 * i + e + 1
            x = DC[h, :, 0:128]
            D3[h, :, 0:128] = shifted(x.astype(F32), 63, -1).astype(BF)
            D3[h, :, 128:256] = x
            D3[h, :, 256:384] = shifted(x.astype(F32), 0, 1).astype(BF)
        return c

    lax.fori_loop(0, 32, make_d3, 0)

    def wgrad_glo(i, first):
        zt = slab(F, i, 1, 0, 384, 16).T
        res = dot(zt, jnp.concatenate([slab(D3, i, 2 - a, 0, 384, 16) for a in range(3)], axis=1))
        for tap in range(9):
            r = 384 * tap
            part = res[:, 128 * tap : 128 * tap + 128]
            DY[r : r + 384, 0:128] = part if first else DY[r : r + 384, 0:128] + part

    def wgrad_loc(i, first):
        zt = slab(Z3, i, 1, 0, 384, 16).T
        for a in range(3):
            res = dot(zt, slab(DC, i, 2 - a, 0, 512, 16))
            r = 384 * a
            if first:
                DY[1152 + r : 1536 + r, 128:256] = res[:, 0:128]
                DY[r : r + 384, 128:512] = res[:, 128:512]
            else:
                DY[1152 + r : 1536 + r, 128:256] += res[:, 0:128]
                DY[r : r + 384, 128:512] += res[:, 128:512]

    def rest(f):
        def body(i, c):
            f(i, False)
            return c

        f(0, True)
        lax.fori_loop(1, 4, body, 0)

    rest(wgrad_glo)
    if fused:
        for tap, c0, s, r0, n in gl_runs(D):
            r = 384 * tap + c0
            W1[s // 2, s % 2, r0 : r0 + n] = DY[r : r + n, 0:128].astype(BF)
        for s in range(D):
            W1[s // 2, s % 2, 432:448] = jnp.zeros((16, 128), BF)
        scatter_1 = Scatter(ring, W1, RS[0], rs_sem, 0)
        scatter_2 = Scatter(ring, W2, RS[1], rs_sem, 10)
        scatter_f = Scatter(ring, WFO, RS[2], rs_sem, 20)
        scatter_i = Scatter(ring, GI, RS[3], rs_sem, 30)
        scatter_1.between()
    rest(wgrad_loc)
    if fused:
        scatter_1.along_x()
        for s in range(D):
            W2[s // 2, s % 2, 0:144] = DY[1152 + 144 * s : 1296 + 144 * s, 128:256].astype(BF)
            for j in range(3):
                ls = slice(128 + 128 * j, 256 + 128 * j)
                W2[s // 2, s % 2, 144 + 144 * j : 288 + 144 * j] = DY[144 * s : 144 * s + 144, ls].astype(BF)
        scatter_2.between()
    else:
        put(DY.at[0:3456, 0:128], out_gl)
        put(DY.at[1152:2304, 128:256], out_ll)
        put(DY.at[0:1152, 128:512], out_lg)

    tot = ar_wait(6)
    for j, (s1, s2) in enumerate(back_sums(tot, 3, 2)):
        at = slice(128 * j, 128 * j + 128)
        COLF[6, at] = COLF[4, at] * COLF[0, at] * col(s2 / fcount)
        COLF[7, at] = COLF[4, at] * (COLF[1, at] * col(s2 / fcount) - col(s1 / fcount))

    def gfu_at(j, lo=0, n=384):
        return (slice(384 * (j // 2) + lo, 384 * (j // 2) + lo + n), slice(256 + 128 * (j % 2), 384 + 128 * (j % 2)))

    def dpf_tile(k, dy):
        return (COLF[4] * dy - COLF[6] * PF[k] + COLF[7]).astype(BF)

    dpf = dpf_tile(16, DYX[...])
    res = dot(ST[16], dpf, 1, 1)
    for j in range(3):
        PX[gfu_at(j)] = res[:, 128 * j : 128 * j + 128]
    ds = dot(WFU[...], dpf)
    EXB[...] = join_ext(ds[0:HALF], ds[HALF : 2 * HALF]).astype(BF)
    for t in range(4):
        spots = [dyf_pos(4 * t + e) for e in range(4)]
        parts = [dpf_tile(4 * t + e, DY[r : r + 384, l : l + 128]) for e, (r, l) in enumerate(spots)]
        dpf = jnp.concatenate(parts, axis=1)
        res = dot(jnp.concatenate([ST[4 * t + e] for e in range(4)], axis=1), dpf, 1, 1)
        for j in range(3):
            PX[gfu_at(j)] += res[:, 128 * j : 128 * j + 128]
        ds = dot(WFU[...], dpf)
        for e, (r, l) in enumerate(spots):
            DY[r : r + 384, l : l + 128] = ds[:, 128 * e : 128 * e + 128]
    if fused:
        scatter_1.along_y()
        scatter_2.along_x()
        for s in range(D):
            for j in range(3):
                ls = slice(128 * j, 128 * j + 128)
                WFO[s // 2, s % 2, 48 * j : 48 * j + 48] = PX[gfu_at(j, 48 * s, 48)].astype(BF)
                part = jnp.concatenate([GOUT[24 * s : 24 * s + 24, ls], jnp.zeros((8, 128), F32)], axis=0)
                WFO[s // 2, s % 2, 144 + 32 * j : 176 + 32 * j] = part.astype(BF)
            WFO[s // 2, s % 2, 240:256] = jnp.zeros((16, 128), BF)
        scatter_f.between()
    else:
        for j in range(3):
            put(PX.at[gfu_at(j)], out_fu.at[:, 128 * j : 128 * j + 128])
        put(GOUT, out_out)

    def adj_fft(i, c):
        halves = []
        for s in range(2):
            z = []
            for k in range(16):
                r0, l0 = dyf_pos(k)
                pair = []
                for comp in range(2):
                    at = pl.ds(pl.multiple_of(r0 + comp * HALF + 16 * i + 8 * s, 8), 8)
                    pair.append(DY[at, l0 : l0 + 128])
                z.append(tuple(pair))
            halves.append(dft16(z, 1))
        for a in range(16):
            for comp in range(2):
                both = jnp.concatenate([halves[0][a][comp], halves[1][a][comp]], axis=0)
                Y[a, pl.ds(pl.multiple_of(i * 16, 16), 16), 128 * comp : 128 * comp + 128] = both.astype(BF)
        return c

    lax.fori_loop(0, 12, adj_fft, 0)
    if fused:
        scatter_1.along_z()
        scatter_f.along_x()
    ACC[...] = jnp.zeros_like(ACC)

    def spec_back(i, c):
        gain, bias, ext = two(COLS[4]), two(COLS[5]), EXB[...]
        s0 = s1 = None
        for e in range(4):
            h0 = 4 * i + e
            back = dot(jnp.concatenate([Y[h0], ext], axis=1), A[h0], 1, 1)
            y = PS[h0] * gain + bias
            dy = gelu_slope(y) * (PX[rows_of(h0), 0:256] + back)
            DY[rows_of(h0), 256:512] = dy
            s0 = lane_pair(dy) if s0 is None else s0 + lane_pair(dy)
            s1 = lane_pair(dy * y) if s1 is None else s1 + lane_pair(dy * y)
        ACC[0:HALF] += s0
        ACC[HALF : 2 * HALF] += s1
        return c

    lax.fori_loop(0, 4, spec_back, 0)
    put_rows(7, 0, spec_rows())
    ar_start(7)
    if fused:
        scatter_2.along_y()
        scatter_1.to_copies()

    def dgrad(i, c):
        lhs = jnp.concatenate([slab(DC, i, 2 - a, 128, 512) for a in range(3)], axis=1)
        rhs = jnp.concatenate([WCAT[384 * a : 384 * a + 384, 128:512] for a in range(3)], axis=1)
        res = dot(lhs, rhs, 1, 1)
        lhs = jnp.concatenate([slab(D3, i, 2 - a, 0, 384) for a in range(3)], axis=1)
        both = dot(lhs, jnp.concatenate([WGL[a] for a in range(3)], axis=1), 1, 1)
        PX[block_rows(i), 128:512] = both[:, 0:384]
        loc = both[:, 384:512] + res[:, 128:256] + shifted(res[:, 0:128], 63, -1) + shifted(res[:, 256:384], 0, 1)
        DC[pl.ds(8 * i + 1, 8), :, 0:128] = loc.astype(BF).reshape(8, SIDE, 128)
        return c

    lax.fori_loop(0, 4, dgrad, 0)
    if fused:
        scatter_2.along_z()
        scatter_f.along_y()

    tot = ar_wait(7)
    for r, (s1, s2) in enumerate(back_sums(tot, 2, 0)):
        n = 128 - 64 * r
        at = slice(128 * r, 128 * r + n)
        COLS[6, at] = COLS[4, at] * COLS[0, at] * col(s2 / count)[0:n]
        COLS[7, at] = COLS[4, at] * (COLS[1, at] * col(s2 / count)[0:n] - col(s1 / count)[0:n])
    GOUT[...] = jnp.zeros_like(GOUT)

    def spec_grad(i, c):
        f4, f6, f7 = two(COLS[4]), two(COLS[6]), two(COLS[7])
        ds = []
        for e in range(4):
            h0 = 4 * i + e
            d = (f4 * DY[rows_of(h0), 256:512] - f6 * PS[h0] + f7).astype(BF)
            J[h0] = d
            ds.append(d)
        rhs = jnp.concatenate([tile(F, 4 * i + e, 0, GLO) for e in range(4)], axis=0)
        GOUT[...] += dot(jnp.concatenate(ds, axis=1), rhs)
        return c

    lax.fori_loop(0, 4, spec_grad, 0)
    if fused:
        gin = jnp.concatenate([GOUT[...], jnp.zeros((64, 384), F32)], axis=0).T
        for s in range(D):
            GI[s // 2, s % 2, 0:48] = gin[48 * s : 48 * s + 48, 0:128].astype(BF)
            GI[s // 2, s % 2, 48:96] = gin[48 * s : 48 * s + 48, 128:256].astype(BF)
            GI[s // 2, s % 2, 96:128] = jnp.zeros((32, 128), BF)
        scatter_i.between()
        scatter_f.along_z()
    else:
        put(GOUT, out_in)
    lax.fori_loop(4, 6, dgrad, 0)
    if fused:
        scatter_i.along_x()
        scatter_2.to_copies()
    lax.fori_loop(6, 8, dgrad, 0)
    if fused:
        scatter_i.along_y()
        scatter_f.to_copies()

    def field_copy(h):
        return pltpu.make_async_copy(DC.at[pl.ds(h + 1, 4)], field_out.at[pl.ds(h, 4)], io_sem.at[6])

    def spec_field(i, c):
        w = WINT[...]
        for e in range(4):
            h0 = 4 * i + e
            dg = dot(J[h0], w, 0, 0)
            for j in range(4):
                total = PX[slab_rows(h0, j), 128:512] + dg[64 * j : 64 * j + 64]
                DC[h0 + 16 * j + 1, :, 128:512] = total.astype(BF)
        for j in range(4):
            field_copy(4 * i + 16 * j).start()
        return c

    lax.fori_loop(0, 2, spec_field, 0)
    if fused:
        scatter_i.along_z()
    lax.fori_loop(2, 4, spec_field, 0)
    if fused:
        scatter_i.to_copies()
        for n, sc in enumerate((scatter_1, scatter_2, scatter_f, scatter_i)):
            sc.last()
            for r in range(4):
                at = STARTS[n] + r * sc.q
                flat_out[at : at + sc.q, :] = sc.done[r]
        await_bytes(WI.at[pl.ds(0, D - 1)], g_sem.at[0])
        await_bytes(GBB.at[pl.ds(0, D - 1)], g_sem.at[2])
    pltpu.make_async_copy(DC.at[1:65], field_out, io_sem.at[6]).wait()


def run_block(features, cotangent, holes, weights, gains, biases, fused):
    dps, reps = lax.axis_size("dp"), lax.axis_size("rep")
    N = dps * reps
    any_spec = pl.BlockSpec(memory_space=pl.ANY)
    vmem = pl.BlockSpec(memory_space=pltpu.VMEM)
    table = jnp.asarray(dft_table())
    args = [features, cotangent, holes, table] + list(weights) + list(gains)
    if fused:
        args = args + list(biases)
    out_shape = [
        jax.ShapeDtypeStruct((SIDE, SIDE, ALL), BF),
        jax.ShapeDtypeStruct((SIDE, SIDE, ALL), BF),
        jax.ShapeDtypeStruct((32, 128), F32),
    ]
    if fused:
        out_shape.append(jax.ShapeDtypeStruct((1408, 128), BF))
    else:
        for shape in ((1152, 128), (3456, 128), (1152, 384), (192, 384), (384, 384), (192, 384)):
            out_shape.append(jax.ShapeDtypeStruct(shape, F32))
    V = pltpu.VMEM
    dma = pltpu.SemaphoreType.DMA
    scratch = [
        V((66, SIDE, 384), BF),
        V((SIDE, SIDE, 128), BF),
        V((66, SIDE, 384), BF),
        V((66, SIDE, 384), BF),
        V((POS, ALL), F32),
        V((POS, ALL), F32),
        V((16, HALF, 256), F32),
        V((17, 384, 128), BF),
        V((17, 384, 128), F32),
        V((16, HALF, 256), BF),
        V((16, HALF, 256), BF),
        V((66, SIDE, ALL), BF),
        V((16, 256, 384), BF),
        V((SIDE, SIDE, ALL), BF),
        V((HALF, 128), F32),
        V((HALF, 128), BF),
        V((384, 128), F32),
        V((384, 128), F32),
        V((768, 128), F32),
        V((8, HALF, 128), F32),
        V((8, 384, 128), F32),
        V((24, ALL), F32),
        V((2, 16, 128), F32),
        V((HALF, 384), F32),
        V((3, ALL, 384), BF),
    ]
    scratch += [V((N, n, 128), F32) for n in AR_ROWS]
    scratch += [dma((8,)), dma((8,)), dma((8,))]
    if fused:
        scratch += [
            V((1152, ALL), BF),
            V((HALF, 384), BF),
            V((384, 384), BF),
            V((384, 384), BF),
            V((HALF, 384), BF),
            V((dps, 96, 128), BF),
            V((dps, 4, 128), F32),
            V((96, 128), BF),
            dma((34,)),
            dma((40,)),
        ]
        scratch += [V((n, 128), BF) for n in CHUNKS[:3]]
        scratch += [V((4, 2, n, 128), BF) for n in CHUNKS]
        for n in CHUNKS:
            q = n // 4
            scratch += [V((4, 2, 2 * q, 128), BF), V((4, 2, q, 128), BF)] + [V((4, q, 128), BF)] * 3
    return pl.pallas_call(
        functools.partial(kernel, dps, reps, fused),
        out_shape=out_shape,
        in_specs=[any_spec, any_spec, vmem, any_spec] + [vmem] * (len(args) - 4),
        out_specs=[any_spec, any_spec, vmem] + ([vmem] if fused else [any_spec] * 6),
        scratch_shapes=scratch,
        compiler_params=pltpu.CompilerParams(
            collective_id=0, has_side_effects=True, vmem_limit_bytes=64 * 1024 * 1024 - 65536
        ),
        cost_estimate=pl.CostEstimate(flops=40_000_000_000, bytes_accessed=30_000_000, transcendentals=10_000_000),
    )(*args)


def finish_kernel(share, fused, *refs):
    it = iter(refs)
    cot, field, block, holes, norms = (next(it) for _ in range(5))
    flat = next(it) if fused else None
    o_block, o_input = next(it), next(it)
    grads = [next(it) for _ in range(6)] if fused else []
    o_gain, o_bias = next(it), next(it)
    o_block[...] = block[...]
    for h in range(8):
        wf = mask_tile(0.25 + holes[h : h + 1, :].astype(F32))
        for l0 in range(0, ALL, 128):
            ls = slice(l0, l0 + 128)
            o_input[h, :, ls] = (cot[h, :, ls].astype(F32) * wf + field[h, :, ls].astype(F32)).astype(BF)

    @pl.when(pl.program_id(0) == 0)
    def _():
        if fused:
            g_ll, g_gl, g_lg, g_in, g_fu, g_out = grads
            g_gl[0] = flat[0:432].astype(F32)
            g_ll[0] = flat[448:592].astype(F32)
            for j in range(3):
                ls = slice(128 * j, 128 * j + 128)
                g_lg[0, :, ls] = flat[592 + 144 * j : 736 + 144 * j].astype(F32)
                g_fu[0, :, ls] = flat[1024 + 48 * j : 1072 + 48 * j].astype(F32)
                g_out[0, :, ls] = flat[1168 + 32 * j : 1200 + 32 * j].astype(F32)[0:24]
            g_in[0, :, 0:128] = flat[1280:1328].astype(F32)
            g_in[0, :, 128:192] = flat[1328:1376].astype(F32)[:, 0:64]
        first = share * lax.axis_index("dp")
        lane = lax.broadcasted_iota(jnp.int32, (8, 1152), 1)
        for at, ref in ((0, o_gain), (16, o_bias)):
            row = jnp.concatenate([norms[at + j : at + j + 1, :] for j in range(9)], axis=1)
            row = jnp.broadcast_to(row, (8, 1152))
            row = jnp.where(lane < HALF, row, pltpu.roll(row, 1152 - 64, axis=1))
            row = pltpu.roll(row, lax.rem(1152 - first, 1152), axis=1)
            ref[...] = row[0:1, 0:share]


def finish(cotangent, field, block, holes, norms, flat, share, shapes):
    fused = flat is not None
    maps = pl.BlockSpec((8, SIDE, ALL), lambda i: (i, 0, 0))

    def whole(shape):
        return pl.BlockSpec(shape, lambda i, n=len(shape): (0,) * n)

    args = [cotangent, field, block, holes, norms] + ([flat] if fused else [])
    in_specs = [maps, maps, maps, pl.BlockSpec((8, SIDE), lambda i: (i, 0))]
    in_specs += [whole(a.shape) for a in args[4:]]
    out_shape = [jax.ShapeDtypeStruct((SIDE, SIDE, ALL), BF)] * 2
    out_specs = [maps, maps]
    small = (list(shapes) if fused else []) + [(1, share), (1, share)]
    out_shape += [jax.ShapeDtypeStruct(shape, F32) for shape in small]
    out_specs += [whole(shape) for shape in small]
    return pl.pallas_call(
        functools.partial(finish_kernel, share, fused),
        grid=(8,),
        out_shape=out_shape,
        in_specs=in_specs,
        out_specs=out_specs,
        compiler_params=pltpu.CompilerParams(vmem_limit_bytes=64 * 1024 * 1024 - 65536),
    )(*args)


def on_device(features, cotangent, holes, w_ll, w_gl, w_lg, w_in, w_fu, w_out, gains, biases):
    dps, reps = lax.axis_size("dp"), lax.axis_size("rep")
    share = gains.shape[1]
    shards = (w_ll, w_gl, w_lg, w_in, w_fu, w_out)
    if dps == 8 and reps == 4:
        weights = [w[0] for w in shards]
        block, field, norms, flat = run_block(features[0], cotangent[0], holes[0], weights, [gains], [biases], True)
        block_out, input_grad, *small = finish(
            cotangent[0], field, block, holes[0], norms, flat, share, [w.shape for w in shards]
        )
        return (block_out[None], input_grad[None], *small)
    full = [lax.all_gather(w, "dp", axis=1, tiled=True)[0] for w in shards]
    table = jnp.concatenate([gains, biases], axis=0).astype(F32)
    table = lax.all_gather(table, "dp", axis=1, tiled=True)
    table = jnp.pad(table, ((0, 0), (0, 1152 - table.shape[1])), constant_values=1.0).reshape(18, 128)
    table = jnp.pad(table, ((0, 6), (0, 0)))
    weights = [jnp.concatenate([full[0], full[2]], axis=1), full[1], full[3].T, full[4], full[4].T, full[5]]
    block, field, norms, g_ll, g_gl, g_lg, g_in, g_fu, g_out = run_block(
        features[0], cotangent[0], holes[0], weights, [table], None, False
    )
    grads = []
    for g in (g_ll, g_gl, g_lg, g_in.T, g_fu, g_out):
        g = lax.psum(g[None], "rep")
        grads.append(lax.psum_scatter(g, "dp", scatter_dimension=1, tiled=True))
    block_out, input_grad, *small = finish(cotangent[0], field, block, holes[0], norms, None, share, ())
    return (block_out[None], input_grad[None], *grads, *small)


def solution(mesh):
    whole = P(("dp", "rep"), None, None, None)
    rows = P(None, "dp", None)
    in_specs = (whole, whole, P(("dp", "rep"), None, None)) + (rows,) * 6 + (P(None, "dp"),) * 2
    out_specs = (whole, whole) + (rows,) * 6 + (P(None, "dp"),) * 2
    return jax.shard_map(on_device, mesh=mesh, in_specs=in_specs, out_specs=out_specs, check_vma=False)
```

time: 199 us -> 152 us (0.76)
  Pallas kernels: 181 us -> 150 us
  local copies, waits for them, and re-layouts: 13.2 us -> 0 us
  other arithmetic: 3.25 us -> 0 us
    pallas_call x1, Pallas kernels: 181 us -> 139 us  [run_block(): pl.pallas_call(functools.partial(kernel, dps, reps, fused), out_shape=out...]
    pallas_call x0 -> x1, Pallas kernels: none -> 11.3 us  [finish(): pl.pallas_call(functools.partial(finish_kernel, share, fused), grid=(8,),...]
    unnamed x7 -> x0, local copies, waits for them, and re-layouts: 7.59 us -> none
    slice x8 -> x0, local copies, waits for them, and re-layouts: 3.94 us -> none  [the longest x3 3.19 us: on_device(): cut = lambda at, n: flat[at:at + n]]
    broadcast_in_dim x4 -> x0, other arithmetic: 2.59 us -> none  [on_device(): grads = [g[None] for g in grads]]
where the time goes in v2:
time: 152 us; the launch traced here: 151 us
  Pallas kernels  150 us (99%)
    pallas_call x1, Pallas kernels, run_block(): pl.pallas_call(functools.partial(kernel, dps, reps, fused), out_shape=out...  139 us
    pallas_call x1, Pallas kernels, finish(): pl.pallas_call(functools.partial(finish_kernel, share, fused), grid=(8,),...  11.3 us

profile of v2, /device:TPU:0, one launch (start us, length us, event | category | flops | bytes accessed | tf_op | source)
XLA Modules:
  0.0 151.3 jit_solution(15301945627694198402)
XLA Ops:
  0.6 139.2 %shard_map.195 = (bf16[64,64,512]{2,1,0:T(8,128)(2,1)}, bf16[64,64,512]{2,1,0:T(8,128)(2,1)}, f32[32,128]{1,0:T(8,128)}, bf16[1408,128]{1,0:T(8,128)(2,1)}) custom-call(bf16[64,64,512]{2,1,0:T(8,128)(2,1)} %bitcast.15, bf16[64,64,512]{2,1,0:T(8,128)(2,1)} %bitcast.11, s32[64,64]{1,0:T(8,128)} %bitcast.13, bf16[16,256,384]{2,1,0:T(8,128)(2,1)} %constant.2.clone.refs_3_, ...), custom_call_target="tpu_custom_call" | custom-call | flops 40000000000 | bytes 30000000 | tf_op jit(solution)/shard_map/pallas_call | solution.py:1212
  139.8 11.3 %shard_map.196 = (bf16[64,64,512]{2,1,0:T(8,128)(2,1)}, bf16[64,64,512]{2,1,0:T(8,128)(2,1)}, f32[1,144,128]{2,1,0:T(8,128)}, f32[1,432,128]{2,1,0:T(8,128)}, f3...) custom-call(bf16[64,64,512]{2,1,0:T(8,128)(2,1)} %bitcast.12, ...), custom_call_target="tpu_custom_call" | custom-call | tf_op jit(solution)/shard_map/pallas_call | solution.py:1277

commit v3 on v2

--- a/solution.py
+++ b/solution.py
@@ -292,6 +292,112 @@
         await_bytes(three, self.sem(8))
 
 
+class GatherHalf(Gather):
+    def __init__(self, ring, own, buf, sems, base):
+        super().__init__(ring, own, buf, sems, base)
+        self.q = own.shape[0] // 2
+
+    def place(self):
+        rows = self.rows(self.ring.core)
+        self.buf[self.ring.z, self.ring.y, rows] = self.own[rows]
+
+    def along_z(self):
+        g = self.ring
+        rows = self.rows(g.core)
+        for d in range(1, 4):
+            there = (2 * lax.rem(g.z + d, 4) + g.y, g.rp)
+            g.send(self.own.at[rows], self.buf.at[g.z, g.y, rows], self.sem(0), self.sem(1), there)
+
+    def along_y(self):
+        g = self.ring
+        await_bytes(self.buf.at[pl.ds(0, 3), 0, pl.ds(0, self.q)], self.sem(1))
+        part = self.buf.at[:, g.y, self.rows(g.core)]
+        g.send(part, part, self.sem(2), self.sem(3), g.beside())
+
+    def between(self):
+        g = self.ring
+        await_bytes(self.buf.at[:, 0, pl.ds(0, self.q)], self.sem(3))
+        part = self.buf.at[:, :, self.rows(g.core)]
+        g.send(part, part, self.sem(4), self.sem(5), g.sibling())
+
+    def last(self):
+        one = self.buf.at[:, :, pl.ds(0, self.q)]
+        await_bytes(one, self.sem(5))
+        await_bytes(one, self.sem(4))
+        await_bytes(self.buf.at[pl.ds(0, 3), 0, pl.ds(0, self.q)], self.sem(0))
+        await_bytes(self.buf.at[:, 0, pl.ds(0, self.q)], self.sem(2))
+
+
+class ScatterHalf:
+    def __init__(self, ring, buf, scratch, sems, base):
+        self.ring, self.buf, self.sems, self.base = ring, buf, sems, base
+        self.one, self.three, self.four, self.part, self.two, self.done = scratch
+        self.q = buf.shape[2] // 2
+
+    def sem(self, i):
+        return self.sems.at[self.base + i]
+
+    def rows(self, index):
+        return pl.ds(pl.multiple_of(index * self.q, 16), self.q)
+
+    def between(self):
+        g = self.ring
+        g.send(self.buf.at[:, :, self.rows(1 - g.core)], self.one, self.sem(0), self.sem(1), g.sibling())
+
+    def add(self, zi, yi, other):
+        at = self.rows(self.ring.core)
+        self.buf[zi, yi, at] = (self.buf[zi, yi, at].astype(F32) + other.astype(F32)).astype(BF)
+
+    def along_y(self):
+        g = self.ring
+        await_bytes(self.one, self.sem(1))
+
+        def body(s, c):
+            zi, yi = lax.div(s, 2), lax.rem(s, 2)
+            self.add(zi, yi, self.one[zi, yi])
+            return c
+
+        lax.fori_loop(0, 8, body, 0)
+        there = self.buf.at[:, 1 - g.y, self.rows(g.core)]
+        g.send(there, self.three, self.sem(2), self.sem(3), g.beside())
+
+    def along_z(self):
+        g = self.ring
+        await_bytes(self.three, self.sem(3))
+        at = self.rows(g.core)
+        for k in range(4):
+            self.add(k, g.y, self.three[k])
+        for d in range(1, 4):
+            zz = lax.rem(g.z + d, 4)
+            g.send(self.buf.at[zz, g.y, at], self.four.at[g.z], self.sem(4), self.sem(5), (2 * zz + g.y, g.rp))
+        self.four[g.z] = self.buf[g.z, g.y, at]
+
+    def along_x(self):
+        g = self.ring
+        await_bytes(self.four.at[pl.ds(0, 3)], self.sem(5))
+        total = self.four[0].astype(F32)
+        for k in range(1, 4):
+            total = total + self.four[k].astype(F32)
+        self.part[...] = total.astype(BF)
+        g.send(self.part, self.two, self.sem(6), self.sem(7), g.across())
+
+    def back(self):
+        g = self.ring
+        await_bytes(self.two, self.sem(7))
+        self.done[g.core] = (self.part[...].astype(F32) + self.two[...].astype(F32)).astype(BF)
+        mine = self.done.at[g.core]
+        g.send(mine, mine, self.sem(8), self.sem(9), g.sibling())
+
+    def last(self):
+        half = self.done.at[0]
+        await_bytes(half, self.sem(9))
+        await_bytes(self.one, self.sem(0))
+        await_bytes(self.three, self.sem(2))
+        await_bytes(self.four.at[pl.ds(0, 3)], self.sem(4))
+        await_bytes(self.part, self.sem(6))
+        await_bytes(half, self.sem(8))
+
+
 AR_ROWS = (4, 6, 2, 6, 2, 6, 6, 4)
 CHUNKS = (448, 576, 256, 128)
 STARTS = (0, 448, 1024, 1280)
@@ -364,7 +470,7 @@
     ar_s, ar_r, io_sem = take(3)
     if fused:
         WCAT, WINT, WFU, WFUT, WOUT, WI, GBB, OWNI, g_sem, rs_sem = take(10)
-        OWN, WB, RS = take(3), take(4), [take(5) for _ in range(4)]
+        OWN, WB, RS = take(3), take(4), [take(n) for n in (6, 5, 5, 5)]
     ring = Ring(dps, reps)
     D, R, N = ring.D, ring.R, ring.N
     me, dp, rp = ring.me, ring.dp, ring.rp
@@ -404,6 +510,7 @@
 
     if fused:
         O1, O2, OF = OWN
+        half = pl.ds(pl.multiple_of(48 * ring.core, 16), 48)
         OWNI[0:48, :] = w_in[:, 0:128]
         OWNI[48:96, :] = jnp.concatenate([w_in[:, 128:192], jnp.zeros((48, 64), BF)], axis=1)
         own = gain_in.shape[1]
@@ -411,7 +518,7 @@
             row = jnp.concatenate([ref[...].astype(F32), jnp.zeros((1, 256 - own), F32)], axis=1)
             for j in range(2):
                 GBB[dp, 2 * kind + j : 2 * kind + j + 1, :] = row[:, 128 * j : 128 * j + 128]
-        WI[dp] = OWNI[...]
+        WI[dp, half] = OWNI[half]
         for j in range(3):
             OF[48 * j : 48 * j + 48, :] = w_fu[:, 128 * j : 128 * j + 128]
             part = w_out[:, 128 * j : 128 * j + 128].astype(F32)
@@ -423,9 +530,9 @@
         O1[0:432, :] = w_gl[...]
         O1[432:448, :] = jnp.zeros((16, 128), BF)
         W1, W2, WFO, GI = WB
-        gather_1 = Gather(ring, O1, W1, g_sem, 4)
-        gather_2 = Gather(ring, O2, W2, g_sem, 14)
-        gather_f = Gather(ring, OF, WFO, g_sem, 24)
+        gather_1 = GatherHalf(ring, O1, W1, g_sem, 6)
+        gather_2 = Gather(ring, O2, W2, g_sem, 12)
+        gather_f = Gather(ring, OF, WFO, g_sem, 22)
         for g in (gather_f, gather_2, gather_1):
             g.place()
 
@@ -439,11 +546,8 @@
         lax.fori_loop(1, D, body, 0)
 
     if fused:
-        spread(OWNI, WI.at[dp], g_sem.at[0], g_sem.at[1])
-        gather_f.along_z()
-        spread(GBB.at[dp], GBB.at[dp], g_sem.at[2], g_sem.at[3])
-        gather_2.along_z()
-        gather_1.along_z()
+        spread(OWNI.at[half], WI.at[dp, half], g_sem.at[0], g_sem.at[1])
+        spread(GBB.at[dp], GBB.at[dp], g_sem.at[4], g_sem.at[5])
 
     edge_row = jnp.zeros((SIDE, 384), BF)
     for ref in (F, Z3, D3):
@@ -458,6 +562,9 @@
         return c
 
     lax.fori_loop(0, 16, make_wf, 0)
+    if fused:
+        gather_f.along_z()
+        gather_2.along_z()
     copy_l.wait()
 
     def make_z3(i, c):
@@ -472,7 +579,10 @@
     copy_f.wait()
 
     if fused:
-        await_bytes(WI.at[pl.ds(0, D - 1)], g_sem.at[1])
+        await_bytes(WI.at[pl.ds(0, D - 1), pl.ds(0, 48)], g_sem.at[1])
+        part = WI.at[:, half]
+        ring.send(part, part, g_sem.at[2], g_sem.at[3], ring.sibling())
+        await_bytes(part, g_sem.at[3])
         first = jnp.concatenate([WI[s, 0:48] for s in range(D)], axis=0).astype(F32)
         WINT[0:128, :] = first.T.astype(BF)
         first = jnp.concatenate([WI[s, 48:96] for s in range(D)], axis=0).astype(F32)
@@ -505,7 +615,8 @@
 
     if fused:
         gather_f.along_y()
-        await_bytes(GBB.at[pl.ds(0, D - 1)], g_sem.at[3])
+        gather_2.along_y()
+        await_bytes(GBB.at[pl.ds(0, D - 1)], g_sem.at[5])
         wide = []
         for kind in range(2):
             parts = []
@@ -546,9 +657,9 @@
         ref[5] = ref[3] - ref[1] * ref[2]
 
     if fused:
-        gather_2.along_y()
         gather_f.along_x()
-        gather_1.along_y()
+        gather_2.along_x()
+        gather_1.along_z()
 
     copy_a.wait()
     tot = ar_wait(0)
@@ -575,7 +686,6 @@
 
     lax.fori_loop(0, 4, spec_front, 0)
     if fused:
-        gather_2.along_x()
         gather_f.between()
     low_half = lax.broadcasted_iota(jnp.int32, (HALF, 128), 1) < 64
 
@@ -609,8 +719,6 @@
     lax.fori_loop(0, 12, fwd_fft, 0)
 
     if fused:
-        gather_1.along_x()
-        gather_2.between()
         gather_f.last()
         for j in range(3):
             parts = [WFO[s // 2, s % 2, 48 * j : 48 * j + 48] for s in range(D)]
@@ -651,7 +759,8 @@
     ar_start(1)
 
     if fused:
-        gather_1.between()
+        gather_1.along_y()
+        gather_2.between()
         gather_2.last()
         for s in range(D):
             for j in range(4):
@@ -669,6 +778,8 @@
         return c
 
     lax.fori_loop(0, 8, conv_loc, 0)
+    if fused:
+        gather_1.between()
 
     tot = ar_wait(1)
     for j in range(3):
@@ -930,12 +1041,14 @@
                 DY[1152 + r : 1536 + r, 128:256] += res[:, 0:128]
                 DY[r : r + 384, 128:512] += res[:, 128:512]
 
-    def rest(f):
+    def rest(f, after_first=None):
         def body(i, c):
             f(i, False)
             return c
 
         f(0, True)
+        if after_first is not None:
+            after_first()
         lax.fori_loop(1, 4, body, 0)
 
     rest(wgrad_glo)
@@ -945,14 +1058,13 @@
             W1[s // 2, s % 2, r0 : r0 + n] = DY[r : r + n, 0:128].astype(BF)
         for s in range(D):
             W1[s // 2, s % 2, 432:448] = jnp.zeros((16, 128), BF)
-        scatter_1 = Scatter(ring, W1, RS[0], rs_sem, 0)
+        scatter_1 = ScatterHalf(ring, W1, RS[0], rs_sem, 0)
         scatter_2 = Scatter(ring, W2, RS[1], rs_sem, 10)
         scatter_f = Scatter(ring, WFO, RS[2], rs_sem, 20)
         scatter_i = Scatter(ring, GI, RS[3], rs_sem, 30)
         scatter_1.between()
-    rest(wgrad_loc)
-    if fused:
-        scatter_1.along_x()
+    rest(wgrad_loc, scatter_1.along_y if fused else None)
+    if fused:
         for s in range(D):
             W2[s // 2, s % 2, 0:144] = DY[1152 + 144 * s : 1296 + 144 * s, 128:256].astype(BF)
             for j in range(3):
@@ -992,9 +1104,10 @@
         ds = dot(WFU[...], dpf)
         for e, (r, l) in enumerate(spots):
             DY[r : r + 384, l : l + 128] = ds[:, 128 * e : 128 * e + 128]
-    if fused:
-        scatter_1.along_y()
-        scatter_2.along_x()
+        if fused and t == 1:
+            scatter_1.along_z()
+            scatter_2.along_x()
+    if fused:
         for s in range(D):
             for j in range(3):
                 ls = slice(128 * j, 128 * j + 128)
@@ -1027,9 +1140,6 @@
         return c
 
     lax.fori_loop(0, 12, adj_fft, 0)
-    if fused:
-        scatter_1.along_z()
-        scatter_f.along_x()
     ACC[...] = jnp.zeros_like(ACC)
 
     def spec_back(i, c):
@@ -1051,8 +1161,7 @@
     put_rows(7, 0, spec_rows())
     ar_start(7)
     if fused:
-        scatter_2.along_y()
-        scatter_1.to_copies()
+        scatter_f.along_x()
 
     def dgrad(i, c):
         lhs = jnp.concatenate([slab(DC, i, 2 - a, 128, 512) for a in range(3)], axis=1)
@@ -1062,13 +1171,17 @@
         both = dot(lhs, jnp.concatenate([WGL[a] for a in range(3)], axis=1), 1, 1)
         PX[block_rows(i), 128:512] = both[:, 0:384]
         loc = both[:, 384:512] + res[:, 128:256] + shifted(res[:, 0:128], 63, -1) + shifted(res[:, 256:384], 0, 1)
-        DC[pl.ds(8 * i + 1, 8), :, 0:128] = loc.astype(BF).reshape(8, SIDE, 128)
-        return c
-
-    lax.fori_loop(0, 4, dgrad, 0)
-    if fused:
-        scatter_2.along_z()
-        scatter_f.along_y()
+        loc = loc.reshape(8, SIDE, 128)
+        at = pl.ds(8 * i, 8)
+        COT[at, :, 0:128] = (loc + COT[at, :, 0:128].astype(F32) * WF[at].astype(F32)).astype(BF)
+        return c
+
+    lax.fori_loop(0, 2, dgrad, 0)
+    if fused:
+        scatter_1.along_x()
+    lax.fori_loop(2, 4, dgrad, 0)
+    if fused:
+        scatter_2.along_y()
 
     tot = ar_wait(7)
     for r, (s1, s2) in enumerate(back_sums(tot, 2, 0)):
@@ -1098,20 +1211,22 @@
             GI[s // 2, s % 2, 48:96] = gin[48 * s : 48 * s + 48, 128:256].astype(BF)
             GI[s // 2, s % 2, 96:128] = jnp.zeros((32, 128), BF)
         scatter_i.between()
-        scatter_f.along_z()
+        scatter_1.back()
     else:
         put(GOUT, out_in)
-    lax.fori_loop(4, 6, dgrad, 0)
+    lax.fori_loop(4, 5, dgrad, 0)
     if fused:
         scatter_i.along_x()
-        scatter_2.to_copies()
-    lax.fori_loop(6, 8, dgrad, 0)
+        scatter_2.along_z()
+        scatter_f.along_y()
+    lax.fori_loop(5, 7, dgrad, 0)
     if fused:
         scatter_i.along_y()
-        scatter_f.to_copies()
+        scatter_f.along_z()
+    lax.fori_loop(7, 8, dgrad, 0)
 
     def field_copy(h):
-        return pltpu.make_async_copy(DC.at[pl.ds(h + 1, 4)], field_out.at[pl.ds(h, 4)], io_sem.at[6])
+        return pltpu.make_async_copy(COT.at[pl.ds(h, 4)], field_out.at[pl.ds(h, 4)], io_sem.at[6])
 
     def spec_field(i, c):
         w = WINT[...]
@@ -1119,8 +1234,12 @@
             h0 = 4 * i + e
             dg = dot(J[h0], w, 0, 0)
             for j in range(4):
+                h = h0 + 16 * j
                 total = PX[slab_rows(h0, j), 128:512] + dg[64 * j : 64 * j + 64]
-                DC[h0 + 16 * j + 1, :, 128:512] = total.astype(BF)
+                wf = WF[h].astype(F32)
+                for l0 in range(0, 384, 128):
+                    ls = slice(128 + l0, 256 + l0)
+                    COT[h, :, ls] = (total[:, l0 : l0 + 128] + COT[h, :, ls].astype(F32) * wf).astype(BF)
         for j in range(4):
             field_copy(4 * i + 16 * j).start()
         return c
@@ -1128,17 +1247,21 @@
     lax.fori_loop(0, 2, spec_field, 0)
     if fused:
         scatter_i.along_z()
+        scatter_2.to_copies()
     lax.fori_loop(2, 4, spec_field, 0)
     if fused:
+        scatter_f.to_copies()
         scatter_i.to_copies()
         for n, sc in enumerate((scatter_1, scatter_2, scatter_f, scatter_i)):
             sc.last()
-            for r in range(4):
+            for r in range(CHUNKS[n] // sc.q):
                 at = STARTS[n] + r * sc.q
-                flat_out[at : at + sc.q, :] = sc.done[r]
-        await_bytes(WI.at[pl.ds(0, D - 1)], g_sem.at[0])
-        await_bytes(GBB.at[pl.ds(0, D - 1)], g_sem.at[2])
-    pltpu.make_async_copy(DC.at[1:65], field_out, io_sem.at[6]).wait()
+                pltpu.make_async_copy(sc.done.at[r], flat_out.at[at : at + sc.q], io_sem.at[7]).start()
+        await_bytes(WI.at[pl.ds(0, D - 1), pl.ds(0, 48)], g_sem.at[0])
+        await_bytes(WI.at[:, half], g_sem.at[2])
+        await_bytes(GBB.at[pl.ds(0, D - 1)], g_sem.at[4])
+        await_bytes(flat_out, io_sem.at[7])
+    pltpu.make_async_copy(COT, field_out, io_sem.at[6]).wait()
 
 
 def run_block(features, cotangent, holes, weights, gains, biases, fused):
@@ -1201,19 +1324,22 @@
             V((dps, 96, 128), BF),
             V((dps, 4, 128), F32),
             V((96, 128), BF),
-            dma((34,)),
+            dma((32,)),
             dma((40,)),
         ]
         scratch += [V((n, 128), BF) for n in CHUNKS[:3]]
         scratch += [V((4, 2, n, 128), BF) for n in CHUNKS]
-        for n in CHUNKS:
+        h = CHUNKS[0] // 2
+        scratch += [V((4, 2, h, 128), BF), V((4, h, 128), BF), V((4, h, 128), BF)]
+        scratch += [V((h, 128), BF), V((h, 128), BF), V((2, h, 128), BF)]
+        for n in CHUNKS[1:]:
             q = n // 4
             scratch += [V((4, 2, 2 * q, 128), BF), V((4, 2, q, 128), BF)] + [V((4, q, 128), BF)] * 3
     return pl.pallas_call(
         functools.partial(kernel, dps, reps, fused),
         out_shape=out_shape,
         in_specs=[any_spec, any_spec, vmem, any_spec] + [vmem] * (len(args) - 4),
-        out_specs=[any_spec, any_spec, vmem] + ([vmem] if fused else [any_spec] * 6),
+        out_specs=[any_spec, any_spec, vmem] + [any_spec] * (1 if fused else 6),
         scratch_shapes=scratch,
         compiler_params=pltpu.CompilerParams(
             collective_id=0, has_side_effects=True, vmem_limit_bytes=64 * 1024 * 1024 - 65536
@@ -1222,64 +1348,95 @@
     )(*args)
 
 
+COPIES = 4
+
+
 def finish_kernel(share, fused, *refs):
     it = iter(refs)
-    cot, field, block, holes, norms = (next(it) for _ in range(5))
-    flat = next(it) if fused else None
-    o_block, o_input = next(it), next(it)
-    grads = [next(it) for _ in range(6)] if fused else []
-    o_gain, o_bias = next(it), next(it)
-    o_block[...] = block[...]
-    for h in range(8):
-        wf = mask_tile(0.25 + holes[h : h + 1, :].astype(F32))
-        for l0 in range(0, ALL, 128):
-            ls = slice(l0, l0 + 128)
-            o_input[h, :, ls] = (cot[h, :, ls].astype(F32) * wf + field[h, :, ls].astype(F32)).astype(BF)
-
-    @pl.when(pl.program_id(0) == 0)
-    def _():
-        if fused:
-            g_ll, g_gl, g_lg, g_in, g_fu, g_out = grads
-            g_gl[0] = flat[0:432].astype(F32)
-            g_ll[0] = flat[448:592].astype(F32)
-            for j in range(3):
-                ls = slice(128 * j, 128 * j + 128)
-                g_lg[0, :, ls] = flat[592 + 144 * j : 736 + 144 * j].astype(F32)
-                g_fu[0, :, ls] = flat[1024 + 48 * j : 1072 + 48 * j].astype(F32)
-                g_out[0, :, ls] = flat[1168 + 32 * j : 1200 + 32 * j].astype(F32)[0:24]
-            g_in[0, :, 0:128] = flat[1280:1328].astype(F32)
-            g_in[0, :, 128:192] = flat[1328:1376].astype(F32)[:, 0:64]
-        first = share * lax.axis_index("dp")
-        lane = lax.broadcasted_iota(jnp.int32, (8, 1152), 1)
-        for at, ref in ((0, o_gain), (16, o_bias)):
-            row = jnp.concatenate([norms[at + j : at + j + 1, :] for j in range(9)], axis=1)
-            row = jnp.broadcast_to(row, (8, 1152))
-            row = jnp.where(lane < HALF, row, pltpu.roll(row, 1152 - 64, axis=1))
-            row = pltpu.roll(row, lax.rem(1152 - first, 1152), axis=1)
-            ref[...] = row[0:1, 0:share]
-
-
-def finish(cotangent, field, block, holes, norms, flat, share, shapes):
+
+    def take(n):
+        return [next(it) for _ in range(n)]
+
+    maps = take(2)
+    (norms,) = take(1)
+    flat = take(1)[0] if fused else None
+    outs = take(2)
+    grads = take(6) if fused else []
+    o_gain, o_bias = take(2)
+    buf, in_sem, out_sem = take(3)
+    n = SIDE // COPIES
+    copies = []
+    for i in range(2):
+        for c in range(COPIES):
+            at = pl.ds(n * c, n)
+            back = pltpu.make_async_copy(buf.at[i, at], outs[i].at[at], out_sem.at[i, c])
+            copy = pltpu.make_async_copy(maps[i].at[at], buf.at[i, at], in_sem.at[i, c])
+            copy.start()
+            copies.append((copy, back))
+    if fused:
+        flat_v, sems = take(2)
+        grads_v = take(6)
+        copy = pltpu.make_async_copy(flat, flat_v, sems.at[0])
+        copy.start()
+    for copy_in, copy_out in copies[: len(copies) // 2]:
+        copy_in.wait()
+        copy_out.start()
+    if fused:
+        copy.wait()
+        g_ll, g_gl, g_lg, g_in, g_fu, g_out = grads_v
+        g_gl[0] = flat_v[0:432].astype(F32)
+        g_ll[0] = flat_v[448:592].astype(F32)
+        for j in range(3):
+            ls = slice(128 * j, 128 * j + 128)
+            g_lg[0, :, ls] = flat_v[592 + 144 * j : 736 + 144 * j].astype(F32)
+            g_fu[0, :, ls] = flat_v[1024 + 48 * j : 1072 + 48 * j].astype(F32)
+            g_out[0, :, ls] = flat_v[1168 + 32 * j : 1200 + 32 * j].astype(F32)[0:24]
+        g_in[0, :, 0:128] = flat_v[1280:1328].astype(F32)
+        g_in[0, :, 128:192] = flat_v[1328:1376].astype(F32)[:, 0:64]
+        small = [pltpu.make_async_copy(v, o, sems.at[1 + i]) for i, (v, o) in enumerate(zip(grads_v, grads))]
+        for c in small:
+            c.start()
+    for copy_in, copy_out in copies[len(copies) // 2 :]:
+        copy_in.wait()
+        copy_out.start()
+    first = share * lax.axis_index("dp")
+    lane = lax.broadcasted_iota(jnp.int32, (8, 1152), 1)
+    for at, ref in ((0, o_gain), (16, o_bias)):
+        row = jnp.concatenate([norms[at + j : at + j + 1, :] for j in range(9)], axis=1)
+        row = jnp.broadcast_to(row, (8, 1152))
+        row = jnp.where(lane < HALF, row, pltpu.roll(row, 1152 - 64, axis=1))
+        row = pltpu.roll(row, lax.rem(1152 - first, 1152), axis=1)
+        ref[...] = row[0:1, 0:share]
+    if fused:
+        for c in small:
+            c.wait()
+    for _, copy_out in copies:
+        copy_out.wait()
+
+
+def finish(block, field, norms, flat, share, shapes):
     fused = flat is not None
-    maps = pl.BlockSpec((8, SIDE, ALL), lambda i: (i, 0, 0))
-
-    def whole(shape):
-        return pl.BlockSpec(shape, lambda i, n=len(shape): (0,) * n)
-
-    args = [cotangent, field, block, holes, norms] + ([flat] if fused else [])
-    in_specs = [maps, maps, maps, pl.BlockSpec((8, SIDE), lambda i: (i, 0))]
-    in_specs += [whole(a.shape) for a in args[4:]]
+    any_spec = pl.BlockSpec(memory_space=pl.ANY)
+    vmem = pl.BlockSpec(memory_space=pltpu.VMEM)
+    args = [block, field, norms] + ([flat] if fused else [])
+    in_specs = [any_spec, any_spec, vmem] + ([any_spec] if fused else [])
     out_shape = [jax.ShapeDtypeStruct((SIDE, SIDE, ALL), BF)] * 2
-    out_specs = [maps, maps]
-    small = (list(shapes) if fused else []) + [(1, share), (1, share)]
-    out_shape += [jax.ShapeDtypeStruct(shape, F32) for shape in small]
-    out_specs += [whole(shape) for shape in small]
+    out_specs = [any_spec, any_spec]
+    dma = pltpu.SemaphoreType.DMA
+    scratch = [pltpu.VMEM((2, SIDE, SIDE, ALL), BF), dma((2, COPIES)), dma((2, COPIES))]
+    if fused:
+        out_shape += [jax.ShapeDtypeStruct(shape, F32) for shape in shapes]
+        out_specs += [any_spec] * len(shapes)
+        scratch += [pltpu.VMEM(flat.shape, BF), dma((1 + len(shapes),))]
+        scratch += [pltpu.VMEM(shape, F32) for shape in shapes]
+    out_shape += [jax.ShapeDtypeStruct((1, share), F32)] * 2
+    out_specs += [vmem, vmem]
     return pl.pallas_call(
         functools.partial(finish_kernel, share, fused),
-        grid=(8,),
         out_shape=out_shape,
         in_specs=in_specs,
         out_specs=out_specs,
+        scratch_shapes=scratch,
         compiler_params=pltpu.CompilerParams(vmem_limit_bytes=64 * 1024 * 1024 - 65536),
     )(*args)
 
@@ -1291,9 +1448,7 @@
     if dps == 8 and reps == 4:
         weights = [w[0] for w in shards]
         block, field, norms, flat = run_block(features[0], cotangent[0], holes[0], weights, [gains], [biases], True)
-        block_out, input_grad, *small = finish(
-            cotangent[0], field, block, holes[0], norms, flat, share, [w.shape for w in shards]
-        )
+        block_out, input_grad, *small = finish(block, field, norms, flat, share, [w.shape for w in shards])
         return (block_out[None], input_grad[None], *small)
     full = [lax.all_gather(w, "dp", axis=1, tiled=True)[0] for w in shards]
     table = jnp.concatenate([gains, biases], axis=0).astype(F32)
@@ -1308,7 +1463,7 @@
     for g in (g_ll, g_gl, g_lg, g_in.T, g_fu, g_out):
         g = lax.psum(g[None], "rep")
         grads.append(lax.psum_scatter(g, "dp", scatter_dimension=1, tiled=True))
-    block_out, input_grad, *small = finish(cotangent[0], field, block, holes[0], norms, None, share, ())
+    block_out, input_grad, *small = finish(block, field, norms, None, share, ())
     return (block_out[None], input_grad[None], *grads, *small)
 
 

time: 152 us -> 134 us (0.88)
  Pallas kernels: 150 us -> 133 us
    pallas_call x1, Pallas kernels: 139 us -> 124 us  [run_block(): pl.pallas_call(functools.partial(kernel, dps, reps, fused), out_shape=out...]
    pallas_call x1, Pallas kernels: 11.3 us -> 8.69 us  [finish(): pl.pallas_call(functools.partial(finish_kernel, share, fused), out_shape=...]
where the time goes in v3:
time: 134 us; the launch traced here: 133 us
  Pallas kernels  133 us (99%)
    pallas_call x1, Pallas kernels, run_block(): pl.pallas_call(functools.partial(kernel, dps, reps, fused), out_shape=out...  124 us
    pallas_call x1, Pallas kernels, finish(): pl.pallas_call(functools.partial(finish_kernel, share, fused), out_shape=...  8.69 us

profile of v3, /device:TPU:0, one launch (start us, length us, event | category | flops | bytes accessed | tf_op | source)
XLA Modules:
  0.0 133.4 jit_solution(16900502323769994053)
XLA Ops:
  0.6 123.9 %shard_map.195 = (bf16[64,64,512]{2,1,0:T(8,128)(2,1)}, bf16[64,64,512]{2,1,0:T(8,128)(2,1)}, f32[32,128]{1,0:T(8,128)}, bf16[1408,128]{1,0:T(8,128)(2,1)}) custom-call(bf16[64,64,512]{2,1,0:T(8,128)(2,1)} %bitcast.11, bf16[64,64,512]{2,1,0:T(8,128)(2,1)} %bitcast.12, s32[64,64]{1,0:T(8,128)} %bitcast.19, bf16[16,256,384]{2,1,0:T(8,128)(2,1)} %constant.2.clone.refs_3_, ...), custom_call_target="tpu_custom_call" | custom-call | flops 40000000000 | bytes 30000000 | tf_op jit(solution)/shard_map/pallas_call | solution.py:1338
  124.5 8.7 %shard_map.196 = (bf16[64,64,512]{2,1,0:T(8,128)(2,1)}, bf16[64,64,512]{2,1,0:T(8,128)(2,1)}, f32[1,144,128]{2,1,0:T(8,128)}, f32[1,432,128]{2,1,0:T(8,128)}, f3...) custom-call(bf16[64,64,512]{2,1,0:T(8,128)(2,1)} %get-tuple-element., ...), custom_call_target="tpu_custom_call" | custom-call | tf_op jit(solution)/shard_map/pallas_call | solution.py:1434

commit v4 on v3

--- a/solution.py
+++ b/solution.py
@@ -167,13 +167,13 @@
 class Gather:
     def __init__(self, ring, own, buf, sems, base):
         self.ring, self.own, self.buf, self.sems, self.base = ring, own, buf, sems, base
-        self.q = own.shape[0] // 4
+        self.lo, self.q = 0, own.shape[0] // 4
 
     def sem(self, i):
         return self.sems.at[self.base + i]
 
     def rows(self, i):
-        return pl.ds(pl.multiple_of(i * self.q, 16), self.q)
+        return pl.ds(pl.multiple_of(self.lo + i * self.q, 16), self.q)
 
     def place(self):
         rows = self.rows(self.ring.rp)
@@ -293,9 +293,9 @@
 
 
 class GatherHalf(Gather):
-    def __init__(self, ring, own, buf, sems, base):
+    def __init__(self, ring, own, buf, sems, base, lo, n):
         super().__init__(ring, own, buf, sems, base)
-        self.q = own.shape[0] // 2
+        self.lo, self.q = lo, n // 2
 
     def place(self):
         rows = self.rows(self.ring.core)
@@ -398,8 +398,49 @@
         await_bytes(half, self.sem(8))
 
 
+class ScatterDirect(ScatterHalf):
+    def __init__(self, ring, buf, scratch, sems, base):
+        self.ring, self.buf, self.sems, self.base = ring, buf, sems, base
+        self.one, self.eight, self.part, self.two, self.done = scratch
+        self.q = buf.shape[2] // 2
+
+    def along_yz(self):
+        g = self.ring
+        await_bytes(self.one, self.sem(1))
+        at = self.rows(g.core)
+        for zi in range(4):
+            for yi in range(2):
+                self.add(zi, yi, self.one[zi, yi])
+
+        def body(d, c):
+            there = lax.rem(g.dp + d, 8)
+            src = self.buf.at[lax.div(there, 2), lax.rem(there, 2), at]
+            g.send(src, self.eight.at[g.dp], self.sem(2), self.sem(3), (there, g.rp))
+            return c
+
+        lax.fori_loop(1, 8, body, 0)
+        self.eight[g.dp] = self.buf[g.z, g.y, at]
+
+    def along_x(self):
+        g = self.ring
+        await_bytes(self.eight.at[pl.ds(0, 7)], self.sem(3))
+        total = self.eight[0].astype(F32)
+        for k in range(1, 8):
+            total = total + self.eight[k].astype(F32)
+        self.part[...] = total.astype(BF)
+        g.send(self.part, self.two, self.sem(6), self.sem(7), g.across())
+
+    def last(self):
+        half = self.done.at[0]
+        await_bytes(half, self.sem(9))
+        await_bytes(self.one, self.sem(0))
+        await_bytes(self.eight.at[pl.ds(0, 7)], self.sem(2))
+        await_bytes(self.part, self.sem(6))
+        await_bytes(half, self.sem(8))
+
+
 AR_ROWS = (4, 6, 2, 6, 2, 6, 6, 4)
-CHUNKS = (448, 576, 256, 128)
+CHUNKS = (448, 576, 256, 96)
 STARTS = (0, 448, 1024, 1280)
 
 
@@ -530,10 +571,11 @@
         O1[0:432, :] = w_gl[...]
         O1[432:448, :] = jnp.zeros((16, 128), BF)
         W1, W2, WFO, GI = WB
-        gather_1 = GatherHalf(ring, O1, W1, g_sem, 6)
-        gather_2 = Gather(ring, O2, W2, g_sem, 12)
-        gather_f = Gather(ring, OF, WFO, g_sem, 22)
-        for g in (gather_f, gather_2, gather_1):
+        gather_1 = Gather(ring, O1, W1, g_sem, 6)
+        gather_2a = GatherHalf(ring, O2, W2, g_sem, 26, 0, 288)
+        gather_2b = GatherHalf(ring, O2, W2, g_sem, 32, 288, 288)
+        gather_f = Gather(ring, OF, WFO, g_sem, 16)
+        for g in (gather_f, gather_2a, gather_2b, gather_1):
             g.place()
 
     ring.barrier()
@@ -564,7 +606,7 @@
     lax.fori_loop(0, 16, make_wf, 0)
     if fused:
         gather_f.along_z()
-        gather_2.along_z()
+        gather_2a.along_z()
     copy_l.wait()
 
     def make_z3(i, c):
@@ -583,6 +625,7 @@
         part = WI.at[:, half]
         ring.send(part, part, g_sem.at[2], g_sem.at[3], ring.sibling())
         await_bytes(part, g_sem.at[3])
+        gather_f.along_y()
         first = jnp.concatenate([WI[s, 0:48] for s in range(D)], axis=0).astype(F32)
         WINT[0:128, :] = first.T.astype(BF)
         first = jnp.concatenate([WI[s, 48:96] for s in range(D)], axis=0).astype(F32)
@@ -614,8 +657,8 @@
     ar_start(0)
 
     if fused:
-        gather_f.along_y()
-        gather_2.along_y()
+        gather_2a.along_y()
+        gather_2b.along_z()
         await_bytes(GBB.at[pl.ds(0, D - 1)], g_sem.at[5])
         wide = []
         for kind in range(2):
@@ -658,11 +701,12 @@
 
     if fused:
         gather_f.along_x()
-        gather_2.along_x()
-        gather_1.along_z()
 
     copy_a.wait()
     tot = ar_wait(0)
+    if fused:
+        gather_2b.along_y()
+        gather_1.along_z()
     for r, (lo, n) in enumerate(((0, 128), (128, 64))):
         scale, ms = moments(tot[r : r + 1], tot[r + 2 : r + 3], count)
         COLS[0, lo : lo + n] = col(scale)[0:n]
@@ -686,6 +730,7 @@
 
     lax.fori_loop(0, 4, spec_front, 0)
     if fused:
+        gather_2a.between()
         gather_f.between()
     low_half = lax.broadcasted_iota(jnp.int32, (HALF, 128), 1) < 64
 
@@ -719,6 +764,7 @@
     lax.fori_loop(0, 12, fwd_fft, 0)
 
     if fused:
+        gather_2b.between()
         gather_f.last()
         for j in range(3):
             parts = [WFO[s // 2, s % 2, 48 * j : 48 * j + 48] for s in range(D)]
@@ -760,8 +806,8 @@
 
     if fused:
         gather_1.along_y()
-        gather_2.between()
-        gather_2.last()
+        gather_2a.last()
+        gather_2b.last()
         for s in range(D):
             for j in range(4):
                 WCAT[144 * s : 144 * s + 144, 128 * j : 128 * j + 128] = W2[s // 2, s % 2, 144 * j : 144 * j + 144]
@@ -779,7 +825,7 @@
 
     lax.fori_loop(0, 8, conv_loc, 0)
     if fused:
-        gather_1.between()
+        gather_1.along_x()
 
     tot = ar_wait(1)
     for j in range(3):
@@ -848,6 +894,7 @@
     ar_start(3)
 
     if fused:
+        gather_1.between()
         gather_1.last()
         for tap, c0, s, r0, n in gl_runs(D):
             WGL[tap // 3, c0 : c0 + n, 128 * (tap % 3) : 128 * (tap % 3) + 128] = W1[s // 2, s % 2, r0 : r0 + n]
@@ -1061,7 +1108,7 @@
         scatter_1 = ScatterHalf(ring, W1, RS[0], rs_sem, 0)
         scatter_2 = Scatter(ring, W2, RS[1], rs_sem, 10)
         scatter_f = Scatter(ring, WFO, RS[2], rs_sem, 20)
-        scatter_i = Scatter(ring, GI, RS[3], rs_sem, 30)
+        scatter_i = ScatterDirect(ring, GI, RS[3], rs_sem, 30)
         scatter_1.between()
     rest(wgrad_loc, scatter_1.along_y if fused else None)
     if fused:
@@ -1140,6 +1187,8 @@
         return c
 
     lax.fori_loop(0, 12, adj_fft, 0)
+    if fused:
+        scatter_f.along_x()
     ACC[...] = jnp.zeros_like(ACC)
 
     def spec_back(i, c):
@@ -1160,8 +1209,6 @@
     lax.fori_loop(0, 4, spec_back, 0)
     put_rows(7, 0, spec_rows())
     ar_start(7)
-    if fused:
-        scatter_f.along_x()
 
     def dgrad(i, c):
         lhs = jnp.concatenate([slab(DC, i, 2 - a, 128, 512) for a in range(3)], axis=1)
@@ -1176,12 +1223,13 @@
         COT[at, :, 0:128] = (loc + COT[at, :, 0:128].astype(F32) * WF[at].astype(F32)).astype(BF)
         return c
 
-    lax.fori_loop(0, 2, dgrad, 0)
+    lax.fori_loop(0, 1, dgrad, 0)
     if fused:
         scatter_1.along_x()
-    lax.fori_loop(2, 4, dgrad, 0)
+    lax.fori_loop(1, 3, dgrad, 0)
     if fused:
         scatter_2.along_y()
+        scatter_f.along_y()
 
     tot = ar_wait(7)
     for r, (s1, s2) in enumerate(back_sums(tot, 2, 0)):
@@ -1209,21 +1257,24 @@
         for s in range(D):
             GI[s // 2, s % 2, 0:48] = gin[48 * s : 48 * s + 48, 0:128].astype(BF)
             GI[s // 2, s % 2, 48:96] = gin[48 * s : 48 * s + 48, 128:256].astype(BF)
-            GI[s // 2, s % 2, 96:128] = jnp.zeros((32, 128), BF)
         scatter_i.between()
         scatter_1.back()
     else:
         put(GOUT, out_in)
+    lax.fori_loop(3, 4, dgrad, 0)
+    if fused:
+        scatter_i.along_yz()
+        scatter_f.along_z()
     lax.fori_loop(4, 5, dgrad, 0)
     if fused:
+        scatter_2.along_z()
+    lax.fori_loop(5, 7, dgrad, 0)
+    if fused:
         scatter_i.along_x()
-        scatter_2.along_z()
-        scatter_f.along_y()
-    lax.fori_loop(5, 7, dgrad, 0)
-    if fused:
-        scatter_i.along_y()
-        scatter_f.along_z()
+        scatter_f.to_copies()
     lax.fori_loop(7, 8, dgrad, 0)
+    if fused:
+        scatter_2.to_copies()
 
     def field_copy(h):
         return pltpu.make_async_copy(COT.at[pl.ds(h, 4)], field_out.at[pl.ds(h, 4)], io_sem.at[6])
@@ -1246,12 +1297,9 @@
 
     lax.fori_loop(0, 2, spec_field, 0)
     if fused:
-        scatter_i.along_z()
-        scatter_2.to_copies()
+        scatter_i.back()
     lax.fori_loop(2, 4, spec_field, 0)
     if fused:
-        scatter_f.to_copies()
-        scatter_i.to_copies()
         for n, sc in enumerate((scatter_1, scatter_2, scatter_f, scatter_i)):
             sc.last()
             for r in range(CHUNKS[n] // sc.q):
@@ -1260,7 +1308,7 @@
         await_bytes(WI.at[pl.ds(0, D - 1), pl.ds(0, 48)], g_sem.at[0])
         await_bytes(WI.at[:, half], g_sem.at[2])
         await_bytes(GBB.at[pl.ds(0, D - 1)], g_sem.at[4])
-        await_bytes(flat_out, io_sem.at[7])
+        pltpu.make_async_copy(flat_out, flat_out, io_sem.at[7]).wait()
     pltpu.make_async_copy(COT, field_out, io_sem.at[6]).wait()
 
 
@@ -1279,7 +1327,7 @@
         jax.ShapeDtypeStruct((32, 128), F32),
     ]
     if fused:
-        out_shape.append(jax.ShapeDtypeStruct((1408, 128), BF))
+        out_shape.append(jax.ShapeDtypeStruct((sum(CHUNKS), 128), BF))
     else:
         for shape in ((1152, 128), (3456, 128), (1152, 384), (192, 384), (384, 384), (192, 384)):
             out_shape.append(jax.ShapeDtypeStruct(shape, F32))
@@ -1324,7 +1372,7 @@
             V((dps, 96, 128), BF),
             V((dps, 4, 128), F32),
             V((96, 128), BF),
-            dma((32,)),
+            dma((38,)),
             dma((40,)),
         ]
         scratch += [V((n, 128), BF) for n in CHUNKS[:3]]
@@ -1332,9 +1380,12 @@
         h = CHUNKS[0] // 2
         scratch += [V((4, 2, h, 128), BF), V((4, h, 128), BF), V((4, h, 128), BF)]
         scratch += [V((h, 128), BF), V((h, 128), BF), V((2, h, 128), BF)]
-        for n in CHUNKS[1:]:
+        for n in CHUNKS[1:3]:
             q = n // 4
             scratch += [V((4, 2, 2 * q, 128), BF), V((4, 2, q, 128), BF)] + [V((4, q, 128), BF)] * 3
+        h = CHUNKS[3] // 2
+        scratch += [V((4, 2, h, 128), BF), V((8, h, 128), BF)]
+        scratch += [V((h, 128), BF), V((h, 128), BF), V((2, h, 128), BF)]
     return pl.pallas_call(
         functools.partial(kernel, dps, reps, fused),
         out_shape=out_shape,
@@ -1363,8 +1414,9 @@
     outs = take(2)
     grads = take(6) if fused else []
     o_gain, o_bias = take(2)
-    buf, in_sem, out_sem = take(3)
+    buf, in_sem, out_sem, norms_v, gain_v, bias_v, row_sem = take(7)
     n = SIDE // COPIES
+    norm_copy = pltpu.make_async_copy(norms, norms_v, row_sem.at[0])
     copies = []
     for i in range(2):
         for c in range(COPIES):
@@ -1373,6 +1425,7 @@
             copy = pltpu.make_async_copy(maps[i].at[at], buf.at[i, at], in_sem.at[i, c])
             copy.start()
             copies.append((copy, back))
+    norm_copy.start()
     if fused:
         flat_v, sems = take(2)
         grads_v = take(6)
@@ -1401,12 +1454,18 @@
         copy_out.start()
     first = share * lax.axis_index("dp")
     lane = lax.broadcasted_iota(jnp.int32, (8, 1152), 1)
-    for at, ref in ((0, o_gain), (16, o_bias)):
-        row = jnp.concatenate([norms[at + j : at + j + 1, :] for j in range(9)], axis=1)
+    norm_copy.wait()
+    rows = []
+    for at, ref, out in ((0, gain_v, o_gain), (16, bias_v, o_bias)):
+        row = jnp.concatenate([norms_v[at + j : at + j + 1, :] for j in range(9)], axis=1)
         row = jnp.broadcast_to(row, (8, 1152))
         row = jnp.where(lane < HALF, row, pltpu.roll(row, 1152 - 64, axis=1))
         row = pltpu.roll(row, lax.rem(1152 - first, 1152), axis=1)
         ref[...] = row[0:1, 0:share]
+        rows.append(pltpu.make_async_copy(ref, out, row_sem.at[1 + at // 16]))
+        rows[-1].start()
+    for c in rows:
+        c.wait()
     if fused:
         for c in small:
             c.wait()
@@ -1417,20 +1476,20 @@
 def finish(block, field, norms, flat, share, shapes):
     fused = flat is not None
     any_spec = pl.BlockSpec(memory_space=pl.ANY)
-    vmem = pl.BlockSpec(memory_space=pltpu.VMEM)
     args = [block, field, norms] + ([flat] if fused else [])
-    in_specs = [any_spec, any_spec, vmem] + ([any_spec] if fused else [])
+    in_specs = [any_spec] * len(args)
     out_shape = [jax.ShapeDtypeStruct((SIDE, SIDE, ALL), BF)] * 2
     out_specs = [any_spec, any_spec]
     dma = pltpu.SemaphoreType.DMA
-    scratch = [pltpu.VMEM((2, SIDE, SIDE, ALL), BF), dma((2, COPIES)), dma((2, COPIES))]
+    scratch = [pltpu.VMEM((2, SIDE, SIDE, ALL), BF), dma((2, COPIES)), dma((2, COPIES)), pltpu.VMEM(norms.shape, F32)]
+    scratch += [pltpu.VMEM((1, share), F32), pltpu.VMEM((1, share), F32), dma((3,))]
     if fused:
         out_shape += [jax.ShapeDtypeStruct(shape, F32) for shape in shapes]
         out_specs += [any_spec] * len(shapes)
         scratch += [pltpu.VMEM(flat.shape, BF), dma((1 + len(shapes),))]
         scratch += [pltpu.VMEM(shape, F32) for shape in shapes]
     out_shape += [jax.ShapeDtypeStruct((1, share), F32)] * 2
-    out_specs += [vmem, vmem]
+    out_specs += [any_spec] * 2
     return pl.pallas_call(
         functools.partial(finish_kernel, share, fused),
         out_shape=out_shape,

time: 134 us -> 129 us (0.963)
  Pallas kernels: 133 us -> 128 us
    pallas_call x1, Pallas kernels: 124 us -> 121 us  [run_block(): pl.pallas_call(functools.partial(kernel, dps, reps, fused), out_shape=out...]
where the time goes in v4:
time: 129 us
  Pallas kernels  128 us (99%)
    pallas_call x1, Pallas kernels, run_block(): pl.pallas_call(functools.partial(kernel, dps, reps, fused), out_shape=out...  121 us
    pallas_call x1, Pallas kernels, finish(): pl.pallas_call(functools.partial(finish_kernel, share, fused), out_shape=...  7.44 us

profile of v4, /device:TPU:0, one launch (start us, length us, event | category | flops | bytes accessed | tf_op | source)
XLA Modules:
  0.0 128.8 jit_solution(10659309461123508500)
XLA Ops:
  0.6 120.6 %shard_map.195 = (bf16[64,64,512]{2,1,0:T(8,128)(2,1)}, bf16[64,64,512]{2,1,0:T(8,128)(2,1)}, f32[32,128]{1,0:T(8,128)}, bf16[1376,128]{1,0:T(8,128)(2,1)}) custom-call(bf16[64,64,512]{2,1,0:T(8,128)(2,1)} %bitcast.11, bf16[64,64,512]{2,1,0:T(8,128)(2,1)} %bitcast.12, s32[64,64]{1,0:T(8,128)} %bitcast.19, bf16[16,256,384]{2,1,0:T(8,128)(2,1)} %constant.2.clone.refs_3_, ...), custom_call_target="tpu_custom_call" | custom-call | flops 40000000000 | bytes 30000000 | tf_op jit(solution)/shard_map/pallas_call | solution.py:1389
  121.2 7.4 %shard_map.196 = (bf16[64,64,512]{2,1,0:T(8,128)(2,1)}, bf16[64,64,512]{2,1,0:T(8,128)(2,1)}, f32[1,144,128]{2,1,0:T(8,128)}, f32[1,432,128]{2,1,0:T(8,128)}, f3...) custom-call(bf16[64,64,512]{2,1,0:T(8,128)(2,1)} %get-tuple-element., ...), custom_call_target="tpu_custom_call" | custom-call | tf_op jit(solution)/shard_map/pallas_call | solution.py:1493

commit v5 on v4

--- a/solution.py
+++ b/solution.py
@@ -439,7 +439,7 @@
         await_bytes(half, self.sem(8))
 
 
-AR_ROWS = (4, 6, 2, 6, 2, 6, 6, 4)
+AR_ROWS = (4, 6, 2, 6, 2, 4, 6, 4, 2)
 CHUNKS = (448, 576, 256, 96)
 STARTS = (0, 448, 1024, 1280)
 
@@ -476,11 +476,11 @@
     return jnp.concatenate([x, x], axis=1)
 
 
-def to_row(x):
-    n = x.shape[0]
-    if n < 128:
-        x = jnp.concatenate([x, jnp.zeros((128 - n, 128), F32)], axis=0)
-    return jnp.sum(x.T, axis=0, keepdims=True)
+def lane_sums(x):
+    ones = jnp.ones((8, 128), F32)
+    dims = (((1,), (1,)), ((), ()))
+    sums = lax.dot_general(ones, x, dims, precision=lax.Precision.HIGHEST, preferred_element_type=F32)
+    return [sums[0:1, r : r + 128] for r in range(0, x.shape[0], 128)]
 
 
 def moments(total, square, n):
@@ -506,12 +506,12 @@
     else:
         out_ll, out_gl, out_lg, out_in, out_fu, out_out = take(6)
     F, WF, Z3, D3, PX, DY, PS, ST, PF, Y, J, DC, A, COT = take(14)
-    EXA, EXB, DYX, ACC, ACF, COLS, COLF, ROWP, GBR, GOUT, WGL = take(11)
-    ARB = take(8)
+    EXA, EXB, DYX, ACF, COLS, COLF, ROWP, GBR, GOUT, WGL = take(10)
+    ARB = take(9)
     ar_s, ar_r, io_sem = take(3)
     if fused:
-        WCAT, WINT, WFU, WFUT, WOUT, WI, GBB, OWNI, g_sem, rs_sem = take(10)
-        OWN, WB, RS = take(3), take(4), [take(n) for n in (6, 5, 5, 5)]
+        WCAT, WINT, WFU, WFUT, WOUT, WI, GBB, g_sem, rs_sem = take(9)
+        OWN, WB, RS = take(3), take(4), [take(n) for n in (6, 5, 6, 5)]
     ring = Ring(dps, reps)
     D, R, N = ring.D, ring.R, ring.N
     me, dp, rp = ring.me, ring.dp, ring.rp
@@ -552,14 +552,14 @@
     if fused:
         O1, O2, OF = OWN
         half = pl.ds(pl.multiple_of(48 * ring.core, 16), 48)
-        OWNI[0:48, :] = w_in[:, 0:128]
-        OWNI[48:96, :] = jnp.concatenate([w_in[:, 128:192], jnp.zeros((48, 64), BF)], axis=1)
+        O1[0:48, :] = w_in[:, 0:128]
+        O1[48:96, :] = jnp.concatenate([w_in[:, 128:192], jnp.zeros((48, 64), BF)], axis=1)
         own = gain_in.shape[1]
         for kind, ref in ((0, gain_in), (1, bias_in)):
             row = jnp.concatenate([ref[...].astype(F32), jnp.zeros((1, 256 - own), F32)], axis=1)
             for j in range(2):
                 GBB[dp, 2 * kind + j : 2 * kind + j + 1, :] = row[:, 128 * j : 128 * j + 128]
-        WI[dp, half] = OWNI[half]
+        WI[dp, half] = O1[half]
         for j in range(3):
             OF[48 * j : 48 * j + 48, :] = w_fu[:, 128 * j : 128 * j + 128]
             part = w_out[:, 128 * j : 128 * j + 128].astype(F32)
@@ -588,7 +588,7 @@
         lax.fori_loop(1, D, body, 0)
 
     if fused:
-        spread(OWNI.at[half], WI.at[dp, half], g_sem.at[0], g_sem.at[1])
+        spread(WI.at[dp, half], WI.at[dp, half], g_sem.at[0], g_sem.at[1])
         spread(GBB.at[dp], GBB.at[dp], g_sem.at[4], g_sem.at[5])
 
     edge_row = jnp.zeros((SIDE, 384), BF)
@@ -637,21 +637,21 @@
     def rows_of(h0):
         return pl.ds(pl.multiple_of(h0 * HALF, 8), HALF)
 
-    ACC[...] = jnp.zeros_like(ACC)
+    ACF[0:512] = jnp.zeros((512, 128), F32)
 
     def input_proj(i, c):
         w = WINT[...]
         res = [dot(w, tile(F, 4 * i + e, 0, GLO), 1, 1) for e in range(4)]
         for e in range(4):
             PS[4 * i + e] = res[e]
-        ACC[0:HALF] += sum(lane_pair(ps) for ps in res)
-        ACC[HALF : 2 * HALF] += sum(lane_pair(ps * ps) for ps in res)
+        ACF[0:HALF] += sum(lane_pair(ps) for ps in res)
+        ACF[256 : 256 + HALF] += sum(lane_pair(ps * ps) for ps in res)
         return c
 
     lax.fori_loop(0, 4, input_proj, 0)
 
     def spec_rows():
-        return [to_row(ACC[0:128]), to_row(ACC[128:192]), to_row(ACC[192:320]), to_row(ACC[320:384])]
+        return lane_sums(ACF[0:512])
 
     put_rows(0, 0, spec_rows())
     ar_start(0)
@@ -799,7 +799,7 @@
     lax.fori_loop(0, 2, unit_step, 0)
 
     def freq_rows():
-        return [to_row(ACF[128 * j : 128 * j + 128]) for j in range(6)]
+        return lane_sums(ACF[...])
 
     put_rows(1, 0, freq_rows())
     ar_start(1)
@@ -962,9 +962,12 @@
 
     copy_c.wait()
     set_norm(ar_wait(3), 128, 3)
-    out_norm(128, 512, io_sem.at[4])
-    put_norm_rows(5, 128, 3)
+    out_norm(128, 384, io_sem.at[4])
+    put_norm_rows(5, 128, 2)
     ar_start(5)
+    out_norm(384, 512, io_sem.at[8])
+    put_norm_rows(8, 384, 1)
+    ar_start(8)
     set_norm(ar_wait(2), 0, 1)
     out_norm(0, 128, io_sem.at[5])
     put_norm_rows(4, 0, 1)
@@ -1003,8 +1006,10 @@
 
         lax.fori_loop(0, SIDE, one, 0)
 
-    set_back(ar_wait(5), 128, 3, 6)
-    norm_back(128, 512, io_sem.at[4])
+    set_back(ar_wait(5), 128, 2, 6)
+    norm_back(128, 384, io_sem.at[4])
+    set_back(ar_wait(8), 384, 1, 8)
+    norm_back(384, 512, io_sem.at[8])
 
     EXA[...] = jnp.zeros_like(EXA)
     GOUT[...] = jnp.zeros_like(GOUT)
@@ -1018,36 +1023,42 @@
             dg = tile(DC, h0, 128, 512)
             dgs.append(dg)
             dj = dot(w, dg, 1, 1)
-            PX[rows_of(h0), 0:256] = dj
+            PX[rows_of(h0), 128:384] = dj
             res = dot(dj.astype(BF), A[h0])
-            PX[rows_of(h0), 256:512] = res[:, 0:256]
+            D3[pl.ds(3 * h0 + 1, 3), :, 0:256] = res[:, 0:256].astype(BF).reshape(3, SIDE, 256)
             ext = res[:, 256:384] if ext is None else ext + res[:, 256:384]
         EXA[...] += ext
         lhs = jnp.concatenate([J[4 * i + e] for e in range(4)], axis=1)
         GOUT[...] += dot(lhs, jnp.concatenate(dgs, axis=0))
         return c
 
-    set_back(ar_wait(4), 0, 1, 5)
-    norm_back(0, 128, io_sem.at[5])
     lax.fori_loop(0, 4, join_back, 0)
 
-    def freq_back(g, c):
-        z = dft16(grab(PX, g, 256), -1)
-        for comp in range(2):
-            rows = pl.ds(pl.multiple_of(comp * HALF + 8 * g, 8), 8)
-            s0 = s1 = None
-            for k in range(16):
-                y = freq_act(PF[k, rows], rows)
-                dy = gelu_slope(y) * (z[k][comp] * doubled)
-                r0, l0 = dyf_pos(k)
-                DY[pl.ds(pl.multiple_of(r0 + comp * HALF + 8 * g, 8), 8), l0 : l0 + 128] = dy
-                s0 = dy if s0 is None else s0 + dy
-                s1 = dy * y if s1 is None else s1 + dy * y
-            ACF[rows] = s0
-            ACF[pl.ds(pl.multiple_of(384 + comp * HALF + 8 * g, 8), 8)] = s1
-        return c
-
-    lax.fori_loop(0, 24, freq_back, 0)
+    def freq_back(i, c):
+        z = []
+        for a in range(16):
+            at = pl.ds(pl.multiple_of(16 * lax.rem(i, 4), 16), 16)
+            part = D3[3 * a + 1 + lax.div(i, 4), at, 0:256].astype(F32)
+            z.append((part[:, 0:128], part[:, 128:256]))
+        for half in range(2):
+            hs = slice(8 * half, 8 * half + 8)
+            w = dft16([(re[hs], im[hs]) for re, im in z], -1)
+            for comp in range(2):
+                row = comp * HALF + 16 * i + 8 * half
+                rows = pl.ds(pl.multiple_of(row, 8), 8)
+                s0 = s1 = None
+                for k in range(16):
+                    y = freq_act(PF[k, rows], rows)
+                    dy = gelu_slope(y) * (w[k][comp] * doubled)
+                    r0, l0 = dyf_pos(k)
+                    DY[pl.ds(pl.multiple_of(r0 + row, 8), 8), l0 : l0 + 128] = dy
+                    s0 = dy if s0 is None else s0 + dy
+                    s1 = dy * y if s1 is None else s1 + dy * y
+                ACF[rows] = s0
+                ACF[pl.ds(pl.multiple_of(384 + row, 8), 8)] = s1
+        return c
+
+    lax.fori_loop(0, 12, freq_back, 0)
     ext_re, ext_im = split_ext(EXA[...])
     y = PF[16] * COLF[4] + COLF[5]
     dy = gelu_slope(y) * jnp.concatenate([ext_re, ext_im], axis=0)
@@ -1056,6 +1067,9 @@
     ACF[384:768] += dy * y
     put_rows(6, 0, freq_rows())
     ar_start(6)
+
+    set_back(ar_wait(4), 0, 1, 5)
+    norm_back(0, 128, io_sem.at[5])
 
     def make_d3(i, c):
         for e in range(2):
@@ -1107,7 +1121,7 @@
             W1[s // 2, s % 2, 432:448] = jnp.zeros((16, 128), BF)
         scatter_1 = ScatterHalf(ring, W1, RS[0], rs_sem, 0)
         scatter_2 = Scatter(ring, W2, RS[1], rs_sem, 10)
-        scatter_f = Scatter(ring, WFO, RS[2], rs_sem, 20)
+        scatter_f = ScatterHalf(ring, WFO, RS[2], rs_sem, 20)
         scatter_i = ScatterDirect(ring, GI, RS[3], rs_sem, 30)
         scatter_1.between()
     rest(wgrad_loc, scatter_1.along_y if fused else None)
@@ -1130,7 +1144,7 @@
         COLF[7, at] = COLF[4, at] * (COLF[1, at] * col(s2 / fcount) - col(s1 / fcount))
 
     def gfu_at(j, lo=0, n=384):
-        return (slice(384 * (j // 2) + lo, 384 * (j // 2) + lo + n), slice(256 + 128 * (j % 2), 384 + 128 * (j % 2)))
+        return (slice(384 * j + lo, 384 * j + lo + n), slice(384, 512))
 
     def dpf_tile(k, dy):
         return (COLF[4] * dy - COLF[6] * PF[k] + COLF[7]).astype(BF)
@@ -1188,8 +1202,8 @@
 
     lax.fori_loop(0, 12, adj_fft, 0)
     if fused:
-        scatter_f.along_x()
-    ACC[...] = jnp.zeros_like(ACC)
+        scatter_f.along_y()
+    ACF[0:512] = jnp.zeros((512, 128), F32)
 
     def spec_back(i, c):
         gain, bias, ext = two(COLS[4]), two(COLS[5]), EXB[...]
@@ -1198,12 +1212,12 @@
             h0 = 4 * i + e
             back = dot(jnp.concatenate([Y[h0], ext], axis=1), A[h0], 1, 1)
             y = PS[h0] * gain + bias
-            dy = gelu_slope(y) * (PX[rows_of(h0), 0:256] + back)
+            dy = gelu_slope(y) * (PX[rows_of(h0), 128:384] + back)
             DY[rows_of(h0), 256:512] = dy
             s0 = lane_pair(dy) if s0 is None else s0 + lane_pair(dy)
             s1 = lane_pair(dy * y) if s1 is None else s1 + lane_pair(dy * y)
-        ACC[0:HALF] += s0
-        ACC[HALF : 2 * HALF] += s1
+        ACF[0:HALF] += s0
+        ACF[256 : 256 + HALF] += s1
         return c
 
     lax.fori_loop(0, 4, spec_back, 0)
@@ -1226,10 +1240,9 @@
     lax.fori_loop(0, 1, dgrad, 0)
     if fused:
         scatter_1.along_x()
+        scatter_2.along_y()
+        scatter_f.along_z()
     lax.fori_loop(1, 3, dgrad, 0)
-    if fused:
-        scatter_2.along_y()
-        scatter_f.along_y()
 
     tot = ar_wait(7)
     for r, (s1, s2) in enumerate(back_sums(tot, 2, 0)):
@@ -1258,20 +1271,18 @@
             GI[s // 2, s % 2, 0:48] = gin[48 * s : 48 * s + 48, 0:128].astype(BF)
             GI[s // 2, s % 2, 48:96] = gin[48 * s : 48 * s + 48, 128:256].astype(BF)
         scatter_i.between()
+        scatter_f.along_x()
         scatter_1.back()
     else:
         put(GOUT, out_in)
     lax.fori_loop(3, 4, dgrad, 0)
     if fused:
         scatter_i.along_yz()
-        scatter_f.along_z()
-    lax.fori_loop(4, 5, dgrad, 0)
-    if fused:
+        scatter_f.back()
         scatter_2.along_z()
-    lax.fori_loop(5, 7, dgrad, 0)
+    lax.fori_loop(4, 7, dgrad, 0)
     if fused:
         scatter_i.along_x()
-        scatter_f.to_copies()
     lax.fori_loop(7, 8, dgrad, 0)
     if fused:
         scatter_2.to_copies()
@@ -1351,7 +1362,6 @@
         V((HALF, 128), F32),
         V((HALF, 128), BF),
         V((384, 128), F32),
-        V((384, 128), F32),
         V((768, 128), F32),
         V((8, HALF, 128), F32),
         V((8, 384, 128), F32),
@@ -1361,7 +1371,7 @@
         V((3, ALL, 384), BF),
     ]
     scratch += [V((N, n, 128), F32) for n in AR_ROWS]
-    scratch += [dma((8,)), dma((8,)), dma((8,))]
+    scratch += [dma((9,)), dma((9,)), dma((9,))]
     if fused:
         scratch += [
             V((1152, ALL), BF),
@@ -1371,21 +1381,21 @@
             V((HALF, 384), BF),
             V((dps, 96, 128), BF),
             V((dps, 4, 128), F32),
-            V((96, 128), BF),
             dma((38,)),
             dma((40,)),
         ]
         scratch += [V((n, 128), BF) for n in CHUNKS[:3]]
         scratch += [V((4, 2, n, 128), BF) for n in CHUNKS]
-        h = CHUNKS[0] // 2
-        scratch += [V((4, 2, h, 128), BF), V((4, h, 128), BF), V((4, h, 128), BF)]
-        scratch += [V((h, 128), BF), V((h, 128), BF), V((2, h, 128), BF)]
-        for n in CHUNKS[1:3]:
-            q = n // 4
-            scratch += [V((4, 2, 2 * q, 128), BF), V((4, 2, q, 128), BF)] + [V((4, q, 128), BF)] * 3
-        h = CHUNKS[3] // 2
-        scratch += [V((4, 2, h, 128), BF), V((8, h, 128), BF)]
-        scratch += [V((h, 128), BF), V((h, 128), BF), V((2, h, 128), BF)]
+        for n, route in zip(CHUNKS, "hqhd"):
+            h, q = n // 2, n // 4
+            if route == "h":
+                scratch += [V((4, 2, h, 128), BF), V((4, h, 128), BF), V((4, h, 128), BF)]
+            elif route == "q":
+                scratch += [V((4, 2, h, 128), BF), V((4, 2, q, 128), BF)] + [V((4, q, 128), BF)] * 3
+            else:
+                scratch += [V((4, 2, h, 128), BF), V((8, h, 128), BF)]
+            if route != "q":
+                scratch += [V((h, 128), BF), V((h, 128), BF), V((2, h, 128), BF)]
     return pl.pallas_call(
         functools.partial(kernel, dps, reps, fused),
         out_shape=out_shape,

time: 129 us -> 126 us (0.977)
  Pallas kernels: 128 us -> 125 us
    pallas_call x1, Pallas kernels: 121 us -> 118 us  [run_block(): pl.pallas_call(functools.partial(kernel, dps, reps, fused), out_shape=out...]
where the time goes in v5:
time: 126 us
  Pallas kernels  125 us (99%)
    pallas_call x1, Pallas kernels, run_block(): pl.pallas_call(functools.partial(kernel, dps, reps, fused), out_shape=out...  118 us
    pallas_call x1, Pallas kernels, finish(): pl.pallas_call(functools.partial(finish_kernel, share, fused), out_shape=...  7.44 us

profile of v5, /device:TPU:0, one launch (start us, length us, event | category | flops | bytes accessed | tf_op | source)
XLA Modules:
  0.0 126.1 jit_solution(14030018623389447533)
XLA Ops:
  0.6 117.9 %shard_map.195 = (bf16[64,64,512]{2,1,0:T(8,128)(2,1)}, bf16[64,64,512]{2,1,0:T(8,128)(2,1)}, f32[32,128]{1,0:T(8,128)}, bf16[1376,128]{1,0:T(8,128)(2,1)}) custom-call(bf16[64,64,512]{2,1,0:T(8,128)(2,1)} %bitcast.11, bf16[64,64,512]{2,1,0:T(8,128)(2,1)} %bitcast.12, s32[64,64]{1,0:T(8,128)} %bitcast.19, bf16[16,256,384]{2,1,0:T(8,128)(2,1)} %constant.2.clone.refs_3_, ...), custom_call_target="tpu_custom_call" | custom-call | flops 40000000000 | bytes 30000000 | tf_op jit(solution)/shard_map/pallas_call | solution.py:1399
  118.5 7.4 %shard_map.196 = (bf16[64,64,512]{2,1,0:T(8,128)(2,1)}, bf16[64,64,512]{2,1,0:T(8,128)(2,1)}, f32[1,144,128]{2,1,0:T(8,128)}, f32[1,432,128]{2,1,0:T(8,128)}, f3...) custom-call(bf16[64,64,512]{2,1,0:T(8,128)(2,1)} %get-tuple-element., ...), custom_call_target="tpu_custom_call" | custom-call | tf_op jit(solution)/shard_map/pallas_call | solution.py:1503
